TPU v7x, 1024 devices: a whole 8x8x8 slice. The times are simulated.
1024 devices in a mesh: dp: 8 (over z), seq: 16 (over y, core), tensor: 8 (over x).
Axes of the slice: x: 8, y: 8, z: 8, core: 2. Of those that a mesh axis runs over, the one named last changes fastest.
Arguments:
- inputs: bfloat16 [8, 8192, 4096], P('dp', 'seq', 'tensor'), may hold values from -1.5 to 1.5
- logits: bfloat16 [8, 8192], P('dp', 'seq'), may hold values from -8 to 8
- cotangent: bfloat16 [8, 8192, 4096], P('dp', 'seq', 'tensor'), may hold values from -6 to 6
- attended: bfloat16 [8, 4096, 4096], P('dp', 'seq', 'tensor'), may hold values from -6 to 6
- out_weight: bfloat16 [4096, 4096], P('tensor'), may hold values from -0.09375 to 0.09375
- router_weight: float32 [4096], P('tensor'), may hold values from -6 to 6
- keep_route: int32 [8, 8192], P('dp', 'seq'), may hold values from 0 to 1, as said below
- shard_counts: int32 [8, 16], P('dp'), may hold values from 0 to 512, as said below
Outputs:
- attended_grad: bfloat16 [8, 4096, 4096], P('dp', 'seq', 'tensor')
- inputs_grad: bfloat16 [8, 8192, 4096], P('dp', 'seq', 'tensor')
- router_grad: float32 [4096], P('tensor')
Inputs may be any that keep to these rules, and one draw needn't show every extreme that they name: `keep_route`: sequence b keeps exactly shard_counts[b, s] positions of its s-th block of 512 positions. `shard_counts`: each row sums to 4096; in every sequence some block keeps all its positions.
All inputs are finite; a program needn't handle non-finite values.
Results may differ from a plain program's by a relative error of at most 0.0013.
Values may be sent and summed in bfloat16 or wider, within the bound.
No kernel may reach another device: no remote copies, remote signals or barrier semaphores. Data moves between devices by JAX's collectives and lax.ppermute only.
A program may use at most 32 MiB of HBM per device.

v0:
```python
import math

import jax
import jax.numpy as jnp
from jax import lax
from jax.sharding import PartitionSpec as P


def shards(
    inputs, logits, cotangent, attended, out_weight, router_weight, keep_route, shard_counts
):
    nseq = lax.axis_size("seq")
    here = lax.axis_index("seq")
    batch, tok, width = cotangent.shape
    kept_rows = attended.shape[1]
    heads_width = out_weight.shape[0]
    model = out_weight.shape[1]
    cap = tok // nseq
    scale = 1.0 / math.sqrt(model)
    lanes = jnp.arange(nseq, dtype=jnp.int32)
    offsets = jnp.cumsum(shard_counts, axis=1) - shard_counts
    own_offset = jnp.sum(jnp.where(lanes[None, :] < here, shard_counts, 0), axis=1)
    local = jnp.cumsum(keep_route, axis=1) - 1
    ranks = own_offset[:, None] + local
    slot_ids = jnp.where(keep_route == 1, ranks % nseq * cap + local // nseq, -1)
    send_table = jnp.arange(tok, dtype=jnp.int32)[None, :, None] == slot_ids[:, None, :]
    send_bf = send_table.astype(jnp.bfloat16)

    def pack(values):
        packed = jnp.einsum("bst,btw->bsw", send_bf, values, preferred_element_type=jnp.float32)
        return packed.astype(jnp.bfloat16).reshape(batch, nseq, cap, values.shape[2])

    grad_slots = pack(cotangent)
    logit_slots = jnp.einsum("bst,bt->bs", send_bf, logits, preferred_element_type=jnp.float32)
    logit_slots = logit_slots.astype(jnp.bfloat16).reshape(batch, nseq, cap)
    first = (here - offsets) % nseq
    order_in = first[:, :, None] + nseq * jnp.arange(cap, dtype=jnp.int32)[None, None, :]
    valid = order_in < shard_counts[:, :, None]
    positions = jnp.where(valid, (offsets[:, :, None] + order_in) // nseq, -1).reshape(batch, tok)
    recv_table = jnp.arange(kept_rows, dtype=jnp.int32)[None, :, None] == positions[:, None, :]
    recv_bf = recv_table.astype(jnp.bfloat16)

    def unpack(received):
        flat = received.reshape(batch, tok, received.shape[3])
        placed = jnp.einsum("bks,bsw->bkw", recv_bf, flat, preferred_element_type=jnp.float32)
        return placed.astype(jnp.bfloat16).reshape(batch * kept_rows, received.shape[3])

    grad_in, input_in, logit_in = (
        lax.all_to_all(grad_slots, "seq", split_axis=1, concat_axis=1, tiled=True),
        lax.all_to_all(pack(inputs), "seq", split_axis=1, concat_axis=1, tiled=True),
        lax.all_to_all(logit_slots, "seq", split_axis=1, concat_axis=1, tiled=True),
    )
    grad_kept = unpack(grad_in)
    logit_kept = jnp.einsum(
        "bks,bs->bk", recv_bf, logit_in.reshape(batch, tok), preferred_element_type=jnp.float32
    )
    rate_kept = jax.nn.sigmoid(logit_kept).reshape(batch * kept_rows)
    att_flat = attended.reshape(batch * kept_rows, heads_width)
    piece = lax.all_gather(grad_kept, "tensor", axis=1, tiled=True)
    columns = out_weight
    product = lax.dot_general(
        piece, columns, (((1,), (1,)), ((), ())), preferred_element_type=jnp.float32
    )
    columns, product = (columns, product)
    projected = jnp.dot(att_flat, columns, preferred_element_type=jnp.float32)
    partial_dots = jnp.sum(piece.astype(jnp.float32) * projected, axis=1)
    dots = lax.psum(partial_dots, "tensor")
    att_grad = (
        (rate_kept[:, None] * product).astype(jnp.bfloat16).reshape(batch, kept_rows, heads_width)
    )
    logit_grad = rate_kept * (1.0 - rate_kept) * dots
    back_slots = jnp.einsum(
        "bks,bk->bs",
        recv_table.astype(jnp.float32),
        logit_grad.reshape(batch, kept_rows),
        precision=lax.Precision.HIGHEST,
    )
    returned = lax.all_to_all(
        back_slots.reshape(batch, nseq, cap), "seq", split_axis=1, concat_axis=1, tiled=True
    ).reshape(batch, tok)
    token_grad = jnp.einsum(
        "bst,bs->bt", send_table.astype(jnp.float32), returned, precision=lax.Precision.HIGHEST
    )
    in_grad = (
        cotangent.astype(jnp.float32)
        + scale * token_grad[:, :, None] * router_weight[None, None, :]
    ).astype(jnp.bfloat16)
    inputs_kept = unpack(input_in)
    partial_sum = scale * jnp.sum(inputs_kept.astype(jnp.float32) * logit_grad[:, None], axis=0)
    router_grad = lax.psum(partial_sum, ("dp", "seq"))
    return (att_grad, in_grad, router_grad)


def solution(mesh):
    in_specs = (
        P("dp", "seq", "tensor"),
        P("dp", "seq"),
        P("dp", "seq", "tensor"),
        P("dp", "seq", "tensor"),
        P("tensor", None),
        P("tensor"),
        P("dp", "seq"),
        P("dp", None),
    )
    out_specs = (P("dp", "seq", "tensor"), P("dp", "seq", "tensor"), P("tensor"))
    return jax.shard_map(shards, mesh=mesh, in_specs=in_specs, out_specs=out_specs, check_vma=False)
```

profile of v0, /device:TPU:1, one launch (start us, length us, event | category | flops | bytes accessed | tf_op | source)
XLA Modules:
  0.0 387.4 jit_solution(5709175213970127597)
XLA Ops:
  7.2 1.1 reduce-window.6
  8.3 0.2 slice_reduce_fusion
  8.4 0.2 reduce-window.9
  8.6 0.8 reduce_window_sum.32
  9.5 1.3 fusion.46
  10.8 1.4 compare_select_fusion.2
  12.2 2.3 convolution_convert_fusion.1
  14.5 17.5 %all-to-all-start.1 = ((bf16[1,16,32,512]{3,2,0,1:T(8,128)(2,1)}), bf16[1,16,32,512]{3,2,0,1:T(8,128)(2,1)S(1)}, u32[]{:S(2)}, u32[]{:S(2)}) async-start(bf16[1,16,32,512]{3,2,0,1:T(8,128)(2,1)} %bitcast.14), calls=%async_computation.1 | async-start | bytes 1048576 | tf_op jit(solution)/shard_map/all_to_all | solution.py:49
  32.0 0.8 broadcast_reduce_fusion
  33.0 0.1 broadcast_reduce_fusion.2
  33.2 16.1 %all-to-all-done.1 = bf16[1,16,32,512]{3,2,0,1:T(8,128)(2,1)S(1)} async-done(((bf16[1,16,32,512]{3,2,0,1:T(8,128)(2,1)}), bf16[1,16,32,512]{3,2,0,1:T(8,128)(2,1)S(1)}, u32[]{:S(2)}, u32[]{:S(2)}) %all-to-all-start.1) | async-done | bytes 524320 | tf_op jit(solution)/shard_map/all_to_all | solution.py:49
  49.3 1.0 convolution_convert_fusion.3
  50.4 1.0 fusion.11
  51.4 0.7 reshape.673
  52.0 3.4 all-to-all-start
  55.5 1.2 convolution_convert_fusion
  56.8 5.2 %all-to-all-done = bf16[1,16,32]{2,0,1:T(2,128)(2,1)S(1)} async-done(((bf16[1,16,32]{2,0,1:T(2,128)(2,1)}), bf16[1,16,32]{2,0,1:T(2,128)(2,1)S(1)}, u32[]{:S(2)}, u32[]{:S(2)}) %all-to-all-start) | async-done | bytes 1056 | tf_op jit(solution)/shard_map/all_to_all | solution.py:51
  62.0 4.0 %all-to-all-start.3 = ((bf16[1,16,32,512]{3,2,0,1:T(8,128)(2,1)}), bf16[1,16,32,512]{3,2,0,1:T(8,128)(2,1)S(1)}, u32[]{:S(2)}, u32[]{:S(2)}) async-start(bf16[1,16,32,512]{3,2,0,1:T(8,128)(2,1)} %bitcast.24), calls=%async_computation.3 | async-start | bytes 1048576 | tf_op jit(solution)/shard_map/all_to_all | solution.py:50
  66.0 0.1 reshape.666
  66.1 0.2 fusion.22
  66.3 24.2 %all-gather.2.cloned.1.call-done = bf16[256,4096]{1,0:T(8,128)(2,1)} async-done(((bf16[256,512]{1,0:T(8,128)(2,1)}), bf16[256,4096]{1,0:T(8,128)(2,1)}) %all-gather.2.cloned.1.call-update) | async-done | bytes 2097168 | tf_op jit(solution)/shard_map/all_gather | solution.py:59
  90.5 4.3 %fusion = f32[256]{0:T(256)S(1)} fusion(bf16[512,4096]{1,0:T(8,128)(2,1)} %param.12, bf16[256,4096]{1,0:T(8,128)(2,1)} %all-gather.2.cloned.1.call-done, bf16[1,256,512]{2,1,0:T(8,128)(2,1)S(1)} %copy-done.5), kind=kOutput, calls=%fused_computation.1 | convolution fusion | flops 1076887296 | bytes 6554624 | tf_op jit(solution)/shard_map/dot_general | solution.py:65
  94.9 12.3 %psum.14 = f32[256]{0:T(256)S(1)} all-reduce(f32[256]{0:T(256)S(1)} %fusion), channel_id=1, replica_groups=mesh['dp'=8,'seq'=16,'tensor'=8] {'tensor'}, use_global_device_ids=true, to_apply=%region_5.6 | all-reduce | flops 256 | bytes 2048 | tf_op jit(solution)/shard_map/psum | solution.py:67
  107.2 1.3 fusion.24
  108.5 15.1 %all-to-all-start.2 = ((f32[1,16,32]{2,0,1:T(1,128)}), f32[1,16,32]{2,0,1:T(1,128)S(1)}, u32[]{:S(2)}, u32[]{:S(2)}) async-start(f32[1,16,32]{2,0,1:T(1,128)} %fusion.24), calls=%async_computation.2 | async-start | bytes 16384 | tf_op jit(solution)/shard_map/all_to_all | solution.py:78
  123.6 0.3 fusion.4
  124.0 4.2 %fusion.5 = bf16[1,256,512]{2,1,0:T(8,128)(2,1)} fusion(bf16[256,4096]{1,0:T(8,128)(2,1)S(1)} %copy-done.4, bf16[512,4096]{1,0:T(8,128)(2,1)} %param.12, f32[256]{0:T(256)S(1)} %get-tuple-element.4), kind=kOutput, calls=%fused_computation.11 | convolution fusion | flops 1074003968 | bytes 6554624 | tf_op jit(solution)/shard_map/dot_general | solution.py:61
  128.2 249.7 %psum.15 = f32[512]{0:T(512)} all-reduce(f32[512]{0:T(512)S(1)} %broadcast_multiply_fusion), channel_id=1, replica_groups=mesh['dp'=8,'seq'=16,'tensor'=8] {'dp','seq'}, use_global_device_ids=true, to_apply=%region_7.8 | all-reduce | flops 512 | bytes 4096 | tf_op jit(solution)/shard_map/psum | solution.py:90
  377.9 0.5 broadcast.490
  378.4 0.7 reduce.19
  379.1 0.4 fusion.8
  379.6 1.0 add_convert_fusion
  (32 shorter events, 0.7 us)
Async XLA Ops:
  7.2 48.3 %copy-start = (bf16[1,512,512]{2,1,0:T(8,128)(2,1)S(1)}, bf16[1,512,512]{2,1,0:T(8,128)(2,1)}, u32[]{:S(2)}) copy-start(bf16[1,512,512]{2,1,0:T(8,128)(2,1)} %param.8) | copy-start | bytes 1572868
  7.2 49.5 %copy-start.2 = (s32[1,16]{1,0:T(1,128)S(1)}, s32[1,16]{1,0:T(1,128)}, u32[]{:S(2)}) copy-start(s32[1,16]{1,0:T(1,128)} %param.15) | copy-start | bytes 196
  7.2 83.3 %copy-start.5 = (bf16[1,256,512]{2,1,0:T(8,128)(2,1)S(1)}, bf16[1,256,512]{2,1,0:T(8,128)(2,1)}, u32[]{:S(2)}) copy-start(bf16[1,256,512]{2,1,0:T(8,128)(2,1)} %param.11) | copy-start | bytes 786436
  14.5 34.9 %all-to-all-start.1 = ((bf16[1,16,32,512]{3,2,0,1:T(8,128)(2,1)}), bf16[1,16,32,512]{3,2,0,1:T(8,128)(2,1)S(1)}, u32[]{:S(2)}, u32[]{:S(2)}) async-start(bf16[1,16,32,512]{3,2,0,1:T(8,128)(2,1)} %bitcast.14), calls=%async_computation.1 | async-start | bytes 1048576 | tf_op jit(solution)/shard_map/all_to_all | solution.py:49
  32.0 58.5 %all-gather.2.cloned.1.call-start = ((), (), s32[]{:S(2)}) async-start(), calls=%async_computation.4 | async-start | bytes 2359296 | tf_op jit(solution)/shard_map/all_gather | solution.py:59
  52.0 9.9 %all-to-all-start = ((bf16[1,16,32]{2,0,1:T(2,128)(2,1)}), bf16[1,16,32]{2,0,1:T(2,128)(2,1)S(1)}, u32[]{:S(2)}, u32[]{:S(2)}) async-start(bf16[1,16,32]{2,0,1:T(2,128)(2,1)} %reshape.673), calls=%async_computation | async-start | bytes 16384 | tf_op jit(solution)/shard_map/all_to_all | solution.py:51
  62.0 46.5 %all-to-all-start.3 = ((bf16[1,16,32,512]{3,2,0,1:T(8,128)(2,1)}), bf16[1,16,32,512]{3,2,0,1:T(8,128)(2,1)S(1)}, u32[]{:S(2)}, u32[]{:S(2)}) async-start(bf16[1,16,32,512]{3,2,0,1:T(8,128)(2,1)} %bitcast.24), calls=%async_computation.3 | async-start | bytes 1048576 | tf_op jit(solution)/shard_map/all_to_all | solution.py:50
  90.5 33.4 %copy-start.4 = (bf16[256,4096]{1,0:T(8,128)(2,1)S(1)}, bf16[256,4096]{1,0:T(8,128)(2,1)}, u32[]{:S(2)}) copy-start(bf16[256,4096]{1,0:T(8,128)(2,1)} %all-gather.2.cloned.1.call-done) | copy-start | bytes 6291460
  108.5 269.4 %all-to-all-start.2 = ((f32[1,16,32]{2,0,1:T(1,128)}), f32[1,16,32]{2,0,1:T(1,128)S(1)}, u32[]{:S(2)}, u32[]{:S(2)}) async-start(f32[1,16,32]{2,0,1:T(1,128)} %fusion.24), calls=%async_computation.2 | async-start | bytes 16384 | tf_op jit(solution)/shard_map/all_to_all | solution.py:78
  123.9 255.6 %copy-start.1 = (bf16[1,512,512]{2,1,0:T(8,128)(2,1)S(1)}, bf16[1,512,512]{2,1,0:T(8,128)(2,1)}, u32[]{:S(2)}) copy-start(bf16[1,512,512]{2,1,0:T(8,128)(2,1)} %param.10) | copy-start | bytes 1572868
  123.9 255.6 %copy-start.3 = (f32[512]{0:T(512)S(1)}, f32[512]{0:T(512)}, u32[]{:S(2)}) copy-start(f32[512]{0:T(512)} %param.13) | copy-start | bytes 6148
Sparse Core Ops, SparseCore 0:
  50.5 39.9 all-gather.1
where the time goes:
time: 390 us; the launch traced here: 387 us
  blocking collectives  262 us (67%)
  waiting for transfers between devices  45.5 us (12%)
  starting transfers between devices  40.1 us (10%)
  matrix products  16.3 us (4%)
  between operations  14.2 us (4%)
  other arithmetic  6.53 us (2%)
    psum x1, blocking collectives, shards(): router_grad = lax.psum(partial_sum, ('dp', 'seq'))  250 us
    all_gather x1, waiting for transfers between devices, shards(): piece = lax.all_gather(grad_kept, 'tensor', axis=1, tiled=True)  24.2 us
    all_to_all x1, starting transfers between devices, shards(): lax.all_to_all(grad_slots, 'seq', split_axis=1, concat_axis=1, tiled=True)  17.5 us
    all_to_all x1, waiting for transfers between devices, shards(): lax.all_to_all(grad_slots, 'seq', split_axis=1, concat_axis=1, tiled=True)  16.1 us
    all_to_all x1, starting transfers between devices, shards(): lax.all_to_all(back_slots.reshape(batch, nseq, cap), 'seq', split_axis=1,...  15.1 us
    psum x1, blocking collectives, shards(): dots = lax.psum(partial_dots, 'tensor')  12.3 us
  transfers between devices with their start and end apart: 5, of which 3 were waited for; matrix products, arithmetic and copies ran while one was open for 4% of the time, Pallas kernels for 0%

commit v1 on v0

v1 whole, which is shorter than its diff:
```python
import math

import jax
import jax.numpy as jnp
from jax import lax
from jax.sharding import PartitionSpec as P


def shards(
    inputs, logits, cotangent, attended, out_weight, router_weight, keep_route, shard_counts
):
    nseq = lax.axis_size("seq")
    here = lax.axis_index("seq")
    nten = lax.axis_size("tensor")
    column = lax.axis_index("tensor")
    batch, tok, width = cotangent.shape
    kept_rows = attended.shape[1]
    heads_width, model = out_weight.shape
    cap = tok // nseq
    scale = 1.0 / math.sqrt(model)

    rightward = [(i, (i + 1) % nten) for i in range(nten)]
    leftward = [(i, (i - 1) % nten) for i in range(nten)]

    def times(block, step):
        start = (column + step) % nten * width
        weight = lax.dynamic_slice(out_weight, (0, start), (heads_width, width))
        return lax.dot_general(
            block, weight, (((1,), (1,)), ((), ())), preferred_element_type=jnp.float32
        )

    own = cotangent.reshape(batch * tok, width)
    rows = batch * tok
    product = times(own, 0)
    from_left, from_right = own, own
    for step in range(1, nten // 2):
        from_left = lax.ppermute(from_left, "tensor", rightward)
        from_right = lax.ppermute(from_right, "tensor", leftward)
        product = product + times(from_left, -step) + times(from_right, step)
    upper = lax.ppermute(from_left[: rows // 2], "tensor", rightward)
    lower = lax.ppermute(from_right[rows // 2 :], "tensor", leftward)
    product = product + times(jnp.concatenate([upper, lower], axis=0), nten // 2)

    lanes = jnp.arange(nseq, dtype=jnp.int32)
    offsets = jnp.cumsum(shard_counts, axis=1) - shard_counts
    own_offset = jnp.sum(jnp.where(lanes[None, :] < here, shard_counts, 0), axis=1)
    local = jnp.cumsum(keep_route, axis=1) - 1
    ranks = own_offset[:, None] + local
    slot_ids = jnp.where(keep_route == 1, ranks % nseq * cap + local // nseq, -1)
    slot_table = (
        jnp.arange(tok, dtype=jnp.int32)[None, :, None] == slot_ids[:, None, :]
    ).astype(jnp.bfloat16)
    first = (here - offsets) % nseq
    order_in = first[:, :, None] + nseq * jnp.arange(cap, dtype=jnp.int32)[None, None, :]
    valid = order_in < shard_counts[:, :, None]
    positions = jnp.where(valid, (offsets[:, :, None] + order_in) // nseq, -1).reshape(batch, tok)
    place_table = (
        jnp.arange(kept_rows, dtype=jnp.int32)[None, :, None] == positions[:, None, :]
    ).astype(jnp.bfloat16)

    def exchange(slots):
        parts = slots.astype(jnp.bfloat16).reshape(batch, nseq, cap, slots.shape[2])
        moved = lax.all_to_all(parts, "seq", split_axis=1, concat_axis=1, tiled=True)
        return moved.reshape(batch, tok, slots.shape[2])

    att_slots = jnp.einsum(
        "bks,bkw->bsw", place_table, attended, preferred_element_type=jnp.float32
    )
    att_tok = jnp.einsum(
        "bst,bsw->btw", slot_table, exchange(att_slots), preferred_element_type=jnp.float32
    )

    back = product.reshape(batch, tok, heads_width)
    partial_dots = jnp.sum(att_tok * back, axis=2)
    copies = jnp.broadcast_to(partial_dots[None], (nten, batch, tok))
    dots = jnp.sum(lax.all_to_all(copies, "tensor", 0, 0, tiled=True), axis=0)
    rate = jax.nn.sigmoid(logits.astype(jnp.float32))
    logit_grad = rate * (1.0 - rate) * dots
    partial_sum = scale * jnp.sum(
        inputs.astype(jnp.float32) * logit_grad[:, :, None], axis=(0, 1)
    )
    group = lax.axis_size("dp") * nseq
    sums = jnp.broadcast_to(partial_sum[None], (group, width))
    router_grad = jnp.sum(lax.all_to_all(sums, ("dp", "seq"), 0, 0, tiled=True), axis=0)
    in_grad = (
        cotangent.astype(jnp.float32)
        + scale * logit_grad[:, :, None] * router_weight[None, None, :]
    ).astype(jnp.bfloat16)

    grad_tok = (rate[:, :, None] * back).astype(jnp.bfloat16)
    grad_slots = jnp.einsum(
        "bst,btw->bsw", slot_table, grad_tok, preferred_element_type=jnp.float32
    )
    att_grad = jnp.einsum(
        "bks,bsw->bkw", place_table, exchange(grad_slots), preferred_element_type=jnp.float32
    ).astype(jnp.bfloat16)
    return (att_grad, in_grad, router_grad)


def solution(mesh):
    in_specs = (
        P("dp", "seq", "tensor"),
        P("dp", "seq"),
        P("dp", "seq", "tensor"),
        P("dp", "seq", "tensor"),
        P("tensor", None),
        P("tensor"),
        P("dp", "seq"),
        P("dp", None),
    )
    out_specs = (P("dp", "seq", "tensor"), P("dp", "seq", "tensor"), P("tensor"))
    return jax.shard_map(shards, mesh=mesh, in_specs=in_specs, out_specs=out_specs, check_vma=False)
```

time: 390 us -> 152 us (0.39)
  blocking collectives: 262 us -> 11.2 us
  starting transfers between devices: 40.1 us -> 68.4 us
  between operations: 14.2 us -> 1.02 us
  matrix products: 16.3 us -> 10 us
  waiting for transfers between devices: 45.5 us -> 51.4 us
    psum x2 -> x0, blocking collectives: 262 us -> none  [the longest x1 250 us: shards(): router_grad = lax.psum(partial_sum, ('dp', 'seq'))]
    ppermute x0 -> x8, starting transfers between devices: none -> 25.6 us  [the longest x3 9.8 us: shards(): from_right = lax.ppermute(from_right, 'tensor', leftward)]
    all_gather x1 -> x0, waiting for transfers between devices: 24.2 us -> none  [shards(): piece = lax.all_gather(grad_kept, 'tensor', axis=1, tiled=True)]
    ppermute x0 -> x8, waiting for transfers between devices: none -> 21.8 us  [the longest x3 19 us: shards(): from_left = lax.ppermute(from_left, 'tensor', rightward)]
    all_to_all x0 -> x1, blocking collectives: none -> 11.2 us  [shards(): dots = jnp.sum(lax.all_to_all(copies, 'tensor', 0, 0, tiled=True), axis=0)]
    all_to_all x4 -> x3, waiting for transfers between devices: 21.3 us -> 29.5 us  [the longest x2 15.6 us: exchange(): lax.all_to_all(parts, 'seq', split_axis=1, concat_axis=1, tiled=True)]
    dot_general x10 -> x12, matrix products: 16.3 us -> 10 us  [the longest x8 6.04 us: times(): lax.dot_general(block, weight, (((1,), (1,)), ((), ())), preferred_elemen...]
    all_to_all x4 -> x3, starting transfers between devices: 40 us -> 42.8 us  [the longest x1 21.7 us: shards(): lax.all_to_all(sums, ('dp', 'seq'), 0, 0, tiled=True)]
  transfers between devices with their start and end apart: 5 -> 11, of which waited for: 3 -> 6; matrix products, arithmetic and copies ran while one was open for 4% -> 11% of each run, Pallas kernels for 0% -> 0%
where the time goes in v1:
time: 152 us; the launch traced here: 151 us
  starting transfers between devices  68.4 us (45%)
  waiting for transfers between devices  51.4 us (34%)
  blocking collectives  11.2 us (7%)
  matrix products  10 us (7%)
  other arithmetic  7.02 us (5%)
  local copies, waits for them, and re-layouts  2.37 us (2%)
    all_to_all x1, starting transfers between devices, shards(): lax.all_to_all(sums, ('dp', 'seq'), 0, 0, tiled=True)  21.7 us
    all_to_all x2, starting transfers between devices, exchange(): lax.all_to_all(parts, 'seq', split_axis=1, concat_axis=1, tiled=True)  21 us
    ppermute x3, waiting for transfers between devices, shards(): from_left = lax.ppermute(from_left, 'tensor', rightward)  19 us
    all_to_all x2, waiting for transfers between devices, exchange(): lax.all_to_all(parts, 'seq', split_axis=1, concat_axis=1, tiled=True)  15.6 us
    all_to_all x1, waiting for transfers between devices, shards(): lax.all_to_all(sums, ('dp', 'seq'), 0, 0, tiled=True)  14 us
    all_to_all x1, blocking collectives, shards(): dots = jnp.sum(lax.all_to_all(copies, 'tensor', 0, 0, tiled=True), axis=0)  11.2 us
    ppermute x3, starting transfers between devices, shards(): from_right = lax.ppermute(from_right, 'tensor', leftward)  9.8 us
    ppermute x3, starting transfers between devices, shards(): from_left = lax.ppermute(from_left, 'tensor', rightward)  9.35 us
  transfers between devices with their start and end apart: 11, of which 6 were waited for; matrix products, arithmetic and copies ran while one was open for 11% of the time, Pallas kernels for 0%

profile of v1, /device:TPU:1, one launch (start us, length us, event | category | flops | bytes accessed | tf_op | source)
XLA Modules:
  0.0 151.3 jit_solution(14904296719975762732)
XLA Ops:
  0.6 4.1 %collective-permute-start = (bf16[512,512]{1,0:T(8,128)(2,1)}, bf16[512,512]{1,0:T(8,128)(2,1)S(1)}, u32[]{:S(2)}, u32[]{:S(2)}) collective-permute-start(bf16[512,512]{1,0:T(8,128)(2,1)} %bitcast.50), channel_id=1, source_target_pairs={{0,1},{1,2},{2,3},{3,4},{4,5},{5,6},{6,7},{7,0},{8,9},{9,10},{10,1... | collective-permute-start | bytes 1572872 | tf_op jit(solution)/shard_map/ppermute | solution.py:37
  4.7 3.3 %collective-permute-start.1 = (bf16[512,512]{1,0:T(8,128)(2,1)}, bf16[512,512]{1,0:T(8,128)(2,1)S(1)}, u32[]{:S(2)}, u32[]{:S(2)}) collective-permute-start(bf16[512,512]{1,0:T(8,128)(2,1)} %bitcast.51), channel_id=1, source_target_pairs={{0,7},{1,0},{2,1},{3,2},{4,3},{5,4},{6,5},{7,6},{8,15},{9,8},{10,9... | collective-permute-start | bytes 1572872 | tf_op jit(solution)/shard_map/ppermute | solution.py:38
  8.1 0.8 reduce_window_sum.32
  8.9 1.3 fusion.47
  10.2 0.8 broadcast_reduce_fusion
  11.4 1.2 convolution_convert_fusion.1
  12.6 17.3 %all-to-all-start.1 = ((bf16[1,16,32,512]{3,2,0,1:T(8,128)(2,1)}), bf16[1,16,32,512]{3,2,0,1:T(8,128)(2,1)S(1)}, u32[]{:S(2)}, u32[]{:S(2)}) async-start(bf16[1,16,32,512]{3,2,0,1:T(8,128)(2,1)} %bitcast.19), calls=%async_computation.1 | async-start | bytes 1048576 | tf_op jit(solution)/shard_map/all_to_all | solution.py:63
  29.9 1.0 reduce-window.6
  31.4 1.7 %compare_select_fusion.2 = s32[1,512]{1,0:T(1,128)S(1)} fusion(s32[1,512]{1,0:T(1,128)} %param.14, s32[1,512]{1,0:T(1,128)S(1)} %bitcast.56, s32[1,512]{1,0:T(1,128)S(1)} %bitcast.60, s32[]{:T(128)} %get-tuple-element.7), kind=kLoop, calls=%fused_computation.47 | loop fusion | flops 16896 | bytes 8196 | tf_op jit(solution)/shard_map/jit(_where)/select_n | solution.py:49
  33.1 1.7 %fusion.22 = f32[512,512]{1,0:T(8,128)S(1)} fusion(bf16[512,4096]{1,0:T(8,128)(2,1)} %param.12, s32[]{:T(128)S(6)} %select_n.132, bf16[1,512,512]{2,1,0:T(8,128)(2,1)} %param.10), kind=kOutput, calls=%fused_computation.34 | convolution fusion | flops 268435456 | bytes 2097156 | tf_op jit(solution)/shard_map/dot_general | solution.py:28
  34.8 1.9 %collective-permute-start.3 = (bf16[512,512]{1,0:T(8,128)(2,1)S(1)}, bf16[512,512]{1,0:T(8,128)(2,1)S(1)}, u32[]{:S(2)}, u32[]{:S(2)}) collective-permute-start(bf16[512,512]{1,0:T(8,128)(2,1)S(1)} %collective-permute-done.1), channel_id=1, source_target_pairs={{0,7},{1,0},{2,1},{3,2},{4,3},{5,4},{6,5},{7,6},{8,15},{9,8},{10,9... | collective-permute-start | bytes 1572872 | tf_op jit(solution)/shard_map/ppermute | solution.py:38
  36.7 3.4 %collective-permute-start.2 = (bf16[512,512]{1,0:T(8,128)(2,1)S(1)}, bf16[512,512]{1,0:T(8,128)(2,1)S(1)}, u32[]{:S(2)}, u32[]{:S(2)}) collective-permute-start(bf16[512,512]{1,0:T(8,128)(2,1)S(1)} %collective-permute-done), channel_id=1, source_target_pairs={{0,1},{1,2},{2,3},{3,4},{4,5},{5,6},{6,7},{7,0},{8,9},{9,10},{10,1... | collective-permute-start | bytes 1572872 | tf_op jit(solution)/shard_map/ppermute | solution.py:37
  40.1 1.5 %convolution_add_fusion.3 = f32[512,512]{1,0:T(8,128)S(1)} fusion(f32[512,512]{1,0:T(8,128)S(1)} %fusion.22, bf16[512,512]{1,0:T(8,128)(2,1)S(1)} %collective-permute-done, bf16[512,4096]{1,0:T(8,128)(2,1)} %param.12, s32[]{:T(128)S(6)} %select_n.134), kind=kOutput, calls=%fused_computation.8 | convolution fusion | flops 268697600 | bytes 3145732 | tf_op jit(solution)/shard_map/dot_general | solution.py:28
  42.1 11.0 %collective-permute-done.2 = bf16[512,512]{1,0:T(8,128)(2,1)S(1)} collective-permute-done((bf16[512,512]{1,0:T(8,128)(2,1)S(1)}, bf16[512,512]{1,0:T(8,128)(2,1)S(1)}, u32[]{:S(2)}, u32[]{:S(2)}) %collective-permute-start.2) | collective-permute-done | bytes 524320 | tf_op jit(solution)/shard_map/ppermute | solution.py:37
  53.1 1.9 %collective-permute-start.4 = (bf16[512,512]{1,0:T(8,128)(2,1)S(1)}, bf16[512,512]{1,0:T(8,128)(2,1)S(1)}, u32[]{:S(2)}, u32[]{:S(2)}) collective-permute-start(bf16[512,512]{1,0:T(8,128)(2,1)S(1)} %collective-permute-done.2), channel_id=1, source_target_pairs={{0,1},{1,2},{2,3},{3,4},{4,5},{5,6},{6,7},{7,0},{8,9},{9,10},{10,1... | collective-permute-start | bytes 1572872 | tf_op jit(solution)/shard_map/ppermute | solution.py:37
  55.0 4.6 %collective-permute-start.5 = (bf16[512,512]{1,0:T(8,128)(2,1)S(1)}, bf16[512,512]{1,0:T(8,128)(2,1)S(1)}, u32[]{:S(2)}, u32[]{:S(2)}) collective-permute-start(bf16[512,512]{1,0:T(8,128)(2,1)S(1)} %collective-permute-done.3), channel_id=1, source_target_pairs={{0,7},{1,0},{2,1},{3,2},{4,3},{5,4},{6,5},{7,6},{8,15},{9,8},{10,9... | collective-permute-start | bytes 1572872 | tf_op jit(solution)/shard_map/ppermute | solution.py:38
  60.6 8.0 %collective-permute-done.4 = bf16[512,512]{1,0:T(8,128)(2,1)S(1)} collective-permute-done((bf16[512,512]{1,0:T(8,128)(2,1)S(1)}, bf16[512,512]{1,0:T(8,128)(2,1)S(1)}, u32[]{:S(2)}, u32[]{:S(2)}) %collective-permute-start.4) | collective-permute-done | bytes 524320 | tf_op jit(solution)/shard_map/ppermute | solution.py:37
  68.6 1.9 %collective-permute-start.6 = (bf16[256,512]{1,0:T(8,128)(2,1)S(1)}, bf16[256,512]{1,0:T(8,128)(2,1)S(1)}, u32[]{:S(2)}, u32[]{:S(2)}) collective-permute-start(bf16[256,512]{1,0:T(8,128)(2,1)S(1)} %slice.16), channel_id=1, source_target_pairs={{0,1},{1,2},{2,3},{3,4},{4,5},{5,6},{6,7},{7,0},{8,9},{9,10},{10,1... | collective-permute-start | bytes 786440 | tf_op jit(solution)/shard_map/ppermute | solution.py:40
  70.6 4.6 %collective-permute-start.7 = (bf16[256,512]{1,0:T(8,128)(2,1)S(1)}, bf16[256,512]{1,0:T(8,128)(2,1)S(1)}, u32[]{:S(2)}, u32[]{:S(2)}) collective-permute-start(bf16[256,512]{1,0:T(8,128)(2,1)S(1)} %slice.17), channel_id=1, source_target_pairs={{0,7},{1,0},{2,1},{3,2},{4,3},{5,4},{6,5},{7,6},{8,15},{9,8},{10,9... | collective-permute-start | bytes 786440 | tf_op jit(solution)/shard_map/ppermute | solution.py:41
  75.6 1.9 %collective-permute-done.6 = bf16[256,512]{1,0:T(8,128)(2,1)S(1)} collective-permute-done((bf16[256,512]{1,0:T(8,128)(2,1)S(1)}, bf16[256,512]{1,0:T(8,128)(2,1)S(1)}, u32[]{:S(2)}, u32[]{:S(2)}) %collective-permute-start.6) | collective-permute-done | bytes 262176 | tf_op jit(solution)/shard_map/ppermute | solution.py:40
  77.5 0.9 collective-permute-done.7
  79.4 0.5 fusion.4
  80.0 11.2 %all_to_all.21 = f32[8,1,512]{2,1,0:T(1,128)S(1)} all-to-all(f32[8,1,512]{2,1,0:T(1,128)S(1)} %broadcast_in_dim.11), channel_id=1, replica_groups=mesh['dp'=8,'seq'=16,'tensor'=8] {'tensor'}, dimensions={0} | all-to-all | bytes 32768 | tf_op jit(solution)/shard_map/all_to_all | solution.py:76
  91.4 0.8 broadcast_in_dim.14
  92.2 21.7 %all-to-all-start.3 = ((f32[128,1,512]{2,1,0:T(1,128)}), f32[128,1,512]{2,1,0:T(1,128)S(1)}, u32[]{:S(2)}, u32[]{:S(2)}) async-start(f32[128,1,512]{2,1,0:T(1,128)} %broadcast_in_dim.14), calls=%async_computation.3 | async-start | bytes 524288 | tf_op jit(solution)/shard_map/all_to_all | solution.py:84
  114.0 1.3 convolution_convert_fusion
  115.3 14.0 %all-to-all-done.3 = f32[128,1,512]{2,1,0:T(1,128)S(1)} async-done(((f32[128,1,512]{2,1,0:T(1,128)}), f32[128,1,512]{2,1,0:T(1,128)S(1)}, u32[]{:S(2)}, u32[]{:S(2)}) %all-to-all-start.3) | async-done | bytes 262176 | tf_op jit(solution)/shard_map/all_to_all | solution.py:84
  129.3 3.7 %all-to-all-start = ((bf16[1,16,32,512]{3,2,0,1:T(8,128)(2,1)}), bf16[1,16,32,512]{3,2,0,1:T(8,128)(2,1)S(1)}, u32[]{:S(2)}, u32[]{:S(2)}) async-start(bf16[1,16,32,512]{3,2,0,1:T(8,128)(2,1)} %bitcast.13), calls=%async_computation | async-start | bytes 1048576 | tf_op jit(solution)/shard_map/all_to_all | solution.py:63
  133.0 1.0 add_convert_fusion
  134.0 0.8 reduce_sum.52
  134.8 15.6 %all-to-all-done = bf16[1,16,32,512]{3,2,0,1:T(8,128)(2,1)S(1)} async-done(((bf16[1,16,32,512]{3,2,0,1:T(8,128)(2,1)}), bf16[1,16,32,512]{3,2,0,1:T(8,128)(2,1)S(1)}, u32[]{:S(2)}, u32[]{:S(2)}) %all-to-all-start) | async-done | bytes 524320 | tf_op jit(solution)/shard_map/all_to_all | solution.py:63
  150.3 1.0 fusion.5
  (43 shorter events, 4.1 us)
Async XLA Ops:
  0.6 10.8 %copy-start = (bf16[1,256,512]{2,1,0:T(8,128)(2,1)S(1)}, bf16[1,256,512]{2,1,0:T(8,128)(2,1)}, u32[]{:S(2)}) copy-start(bf16[1,256,512]{2,1,0:T(8,128)(2,1)} %param.11) | copy-start | bytes 786436
  0.6 36.0 %collective-permute-start = (bf16[512,512]{1,0:T(8,128)(2,1)}, bf16[512,512]{1,0:T(8,128)(2,1)S(1)}, u32[]{:S(2)}, u32[]{:S(2)}) collective-permute-start(bf16[512,512]{1,0:T(8,128)(2,1)} %bitcast.50), channel_id=1, source_target_pairs={{0,1},{1,2},{2,3},{3,4},{4,5},{5,6},{6,7},{7,0},{8,9},{9,10},{10,1... | collective-permute-start | bytes 1572872 | tf_op jit(solution)/shard_map/ppermute | solution.py:37
  4.7 30.0 %collective-permute-start.1 = (bf16[512,512]{1,0:T(8,128)(2,1)}, bf16[512,512]{1,0:T(8,128)(2,1)S(1)}, u32[]{:S(2)}, u32[]{:S(2)}) collective-permute-start(bf16[512,512]{1,0:T(8,128)(2,1)} %bitcast.51), channel_id=1, source_target_pairs={{0,7},{1,0},{2,1},{3,2},{4,3},{5,4},{6,5},{7,6},{8,15},{9,8},{10,9... | collective-permute-start | bytes 1572872 | tf_op jit(solution)/shard_map/ppermute | solution.py:38
  12.6 66.9 %all-to-all-start.1 = ((bf16[1,16,32,512]{3,2,0,1:T(8,128)(2,1)}), bf16[1,16,32,512]{3,2,0,1:T(8,128)(2,1)S(1)}, u32[]{:S(2)}, u32[]{:S(2)}) async-start(bf16[1,16,32,512]{3,2,0,1:T(8,128)(2,1)} %bitcast.19), calls=%async_computation.1 | async-start | bytes 1048576 | tf_op jit(solution)/shard_map/all_to_all | solution.py:63
  31.3 10.3 %copy-start.1 = (bf16[512,4096]{1,0:T(8,128)(2,1)S(1)}, bf16[512,4096]{1,0:T(8,128)(2,1)}, u32[]{:S(2)}) copy-start(bf16[512,4096]{1,0:T(8,128)(2,1)} %param.12) | copy-start | bytes 12582916
  34.8 20.3 %collective-permute-start.3 = (bf16[512,512]{1,0:T(8,128)(2,1)S(1)}, bf16[512,512]{1,0:T(8,128)(2,1)S(1)}, u32[]{:S(2)}, u32[]{:S(2)}) collective-permute-start(bf16[512,512]{1,0:T(8,128)(2,1)S(1)} %collective-permute-done.1), channel_id=1, source_target_pairs={{0,7},{1,0},{2,1},{3,2},{4,3},{5,4},{6,5},{7,6},{8,15},{9,8},{10,9... | collective-permute-start | bytes 1572872 | tf_op jit(solution)/shard_map/ppermute | solution.py:38
  36.7 16.4 %collective-permute-start.2 = (bf16[512,512]{1,0:T(8,128)(2,1)S(1)}, bf16[512,512]{1,0:T(8,128)(2,1)S(1)}, u32[]{:S(2)}, u32[]{:S(2)}) collective-permute-start(bf16[512,512]{1,0:T(8,128)(2,1)S(1)} %collective-permute-done), channel_id=1, source_target_pairs={{0,1},{1,2},{2,3},{3,4},{4,5},{5,6},{6,7},{7,0},{8,9},{9,10},{10,1... | collective-permute-start | bytes 1572872 | tf_op jit(solution)/shard_map/ppermute | solution.py:37
  53.1 15.5 %collective-permute-start.4 = (bf16[512,512]{1,0:T(8,128)(2,1)S(1)}, bf16[512,512]{1,0:T(8,128)(2,1)S(1)}, u32[]{:S(2)}, u32[]{:S(2)}) collective-permute-start(bf16[512,512]{1,0:T(8,128)(2,1)S(1)} %collective-permute-done.2), channel_id=1, source_target_pairs={{0,1},{1,2},{2,3},{3,4},{4,5},{5,6},{6,7},{7,0},{8,9},{9,10},{10,1... | collective-permute-start | bytes 1572872 | tf_op jit(solution)/shard_map/ppermute | solution.py:37
  55.0 15.5 %collective-permute-start.5 = (bf16[512,512]{1,0:T(8,128)(2,1)S(1)}, bf16[512,512]{1,0:T(8,128)(2,1)S(1)}, u32[]{:S(2)}, u32[]{:S(2)}) collective-permute-start(bf16[512,512]{1,0:T(8,128)(2,1)S(1)} %collective-permute-done.3), channel_id=1, source_target_pairs={{0,7},{1,0},{2,1},{3,2},{4,3},{5,4},{6,5},{7,6},{8,15},{9,8},{10,9... | collective-permute-start | bytes 1572872 | tf_op jit(solution)/shard_map/ppermute | solution.py:38
  68.6 8.9 %collective-permute-start.6 = (bf16[256,512]{1,0:T(8,128)(2,1)S(1)}, bf16[256,512]{1,0:T(8,128)(2,1)S(1)}, u32[]{:S(2)}, u32[]{:S(2)}) collective-permute-start(bf16[256,512]{1,0:T(8,128)(2,1)S(1)} %slice.16), channel_id=1, source_target_pairs={{0,1},{1,2},{2,3},{3,4},{4,5},{5,6},{6,7},{7,0},{8,9},{9,10},{10,1... | collective-permute-start | bytes 786440 | tf_op jit(solution)/shard_map/ppermute | solution.py:40
  70.6 7.9 %collective-permute-start.7 = (bf16[256,512]{1,0:T(8,128)(2,1)S(1)}, bf16[256,512]{1,0:T(8,128)(2,1)S(1)}, u32[]{:S(2)}, u32[]{:S(2)}) collective-permute-start(bf16[256,512]{1,0:T(8,128)(2,1)S(1)} %slice.17), channel_id=1, source_target_pairs={{0,7},{1,0},{2,1},{3,2},{4,3},{5,4},{6,5},{7,6},{8,15},{9,8},{10,9... | collective-permute-start | bytes 786440 | tf_op jit(solution)/shard_map/ppermute | solution.py:41
  75.6 15.5 %copy-start.5 = (bf16[1,512]{1,0:T(2,128)(2,1)S(1)}, bf16[1,512]{1,0:T(2,128)(2,1)}, u32[]{:S(2)}) copy-start(bf16[1,512]{1,0:T(2,128)(2,1)} %param.9) | copy-start | bytes 3076
  75.6 15.6 %copy-start.3 = (bf16[1,512,512]{2,1,0:T(8,128)(2,1)S(1)}, bf16[1,512,512]{2,1,0:T(8,128)(2,1)}, u32[]{:S(2)}) copy-start(bf16[1,512,512]{2,1,0:T(8,128)(2,1)} %param.8) | copy-start | bytes 1572868
  79.4 53.6 %copy-start.2 = (bf16[1,512,512]{2,1,0:T(8,128)(2,1)S(1)}, bf16[1,512,512]{2,1,0:T(8,128)(2,1)}, u32[]{:S(2)}) copy-start(bf16[1,512,512]{2,1,0:T(8,128)(2,1)} %param.10) | copy-start | bytes 1572868
  79.4 53.6 %copy-start.4 = (f32[512]{0:T(512)S(1)}, f32[512]{0:T(512)}, u32[]{:S(2)}) copy-start(f32[512]{0:T(512)} %param.13) | copy-start | bytes 6148
  92.2 37.0 %all-to-all-start.3 = ((f32[128,1,512]{2,1,0:T(1,128)}), f32[128,1,512]{2,1,0:T(1,128)S(1)}, u32[]{:S(2)}, u32[]{:S(2)}) async-start(f32[128,1,512]{2,1,0:T(1,128)} %broadcast_in_dim.14), calls=%async_computation.3 | async-start | bytes 524288 | tf_op jit(solution)/shard_map/all_to_all | solution.py:84
  129.3 21.1 %all-to-all-start = ((bf16[1,16,32,512]{3,2,0,1:T(8,128)(2,1)}), bf16[1,16,32,512]{3,2,0,1:T(8,128)(2,1)S(1)}, u32[]{:S(2)}, u32[]{:S(2)}) async-start(bf16[1,16,32,512]{3,2,0,1:T(8,128)(2,1)} %bitcast.13), calls=%async_computation | async-start | bytes 1048576 | tf_op jit(solution)/shard_map/all_to_all | solution.py:63

commit v2 on v1

--- a/solution.py
+++ b/solution.py
@@ -30,16 +30,21 @@
         )
 
     own = cotangent.reshape(batch * tok, width)
-    rows = batch * tok
-    product = times(own, 0)
-    from_left, from_right = own, own
+    split = batch * tok // 2
+    gathered = lax.all_gather(own[:split], "tensor", axis=1, tiled=True)
+    from_left = from_right = own[split:]
+    half = from_left.shape[0] // 2
+    ringed = times(from_left, 0)
     for step in range(1, nten // 2):
         from_left = lax.ppermute(from_left, "tensor", rightward)
         from_right = lax.ppermute(from_right, "tensor", leftward)
-        product = product + times(from_left, -step) + times(from_right, step)
-    upper = lax.ppermute(from_left[: rows // 2], "tensor", rightward)
-    lower = lax.ppermute(from_right[rows // 2 :], "tensor", leftward)
-    product = product + times(jnp.concatenate([upper, lower], axis=0), nten // 2)
+        ringed = ringed + times(from_left, -step) + times(from_right, step)
+    upper = lax.ppermute(from_left[:half], "tensor", rightward)
+    lower = lax.ppermute(from_right[half:], "tensor", leftward)
+    ringed = ringed + times(jnp.concatenate([upper, lower], axis=0), nten // 2)
+    straight = lax.dot_general(
+        gathered, out_weight, (((1,), (1,)), ((), ())), preferred_element_type=jnp.float32
+    )
 
     lanes = jnp.arange(nseq, dtype=jnp.int32)
     offsets = jnp.cumsum(shard_counts, axis=1) - shard_counts
@@ -70,15 +75,33 @@
         "bst,bsw->btw", slot_table, exchange(att_slots), preferred_element_type=jnp.float32
     )
 
-    back = product.reshape(batch, tok, heads_width)
-    partial_dots = jnp.sum(att_tok * back, axis=2)
-    copies = jnp.broadcast_to(partial_dots[None], (nten, batch, tok))
-    dots = jnp.sum(lax.all_to_all(copies, "tensor", 0, 0, tiled=True), axis=0)
     rate = jax.nn.sigmoid(logits.astype(jnp.float32))
+    att_flat = att_tok.reshape(batch * tok, heads_width)
+    rate_flat = rate.reshape(batch * tok, 1)
+    partial_dots = jnp.concatenate(
+        [
+            jnp.sum(att_flat[:split] * straight, axis=1),
+            jnp.sum(att_flat[split:] * ringed, axis=1),
+        ]
+    )
+    grad_tok = jnp.concatenate(
+        [
+            (rate_flat[:split] * straight).astype(jnp.bfloat16),
+            (rate_flat[split:] * ringed).astype(jnp.bfloat16),
+        ]
+    ).reshape(batch, tok, heads_width)
+    grad_slots = jnp.einsum(
+        "bst,btw->bsw", slot_table, grad_tok, preferred_element_type=jnp.float32
+    ).astype(jnp.bfloat16)
+    grad_slots, partial_dots = lax.optimization_barrier((grad_slots, partial_dots))
+    grad_in = exchange(grad_slots)
+    dots = lax.psum(partial_dots, "tensor").reshape(batch, tok)
     logit_grad = rate * (1.0 - rate) * dots
     partial_sum = scale * jnp.sum(
         inputs.astype(jnp.float32) * logit_grad[:, :, None], axis=(0, 1)
     )
+    grad_in, partial_sum = lax.optimization_barrier((grad_in, partial_sum))
+
     group = lax.axis_size("dp") * nseq
     sums = jnp.broadcast_to(partial_sum[None], (group, width))
     router_grad = jnp.sum(lax.all_to_all(sums, ("dp", "seq"), 0, 0, tiled=True), axis=0)
@@ -86,13 +109,8 @@
         cotangent.astype(jnp.float32)
         + scale * logit_grad[:, :, None] * router_weight[None, None, :]
     ).astype(jnp.bfloat16)
-
-    grad_tok = (rate[:, :, None] * back).astype(jnp.bfloat16)
-    grad_slots = jnp.einsum(
-        "bst,btw->bsw", slot_table, grad_tok, preferred_element_type=jnp.float32
-    )
     att_grad = jnp.einsum(
-        "bks,bsw->bkw", place_table, exchange(grad_slots), preferred_element_type=jnp.float32
+        "bks,bsw->bkw", place_table, grad_in, preferred_element_type=jnp.float32
     ).astype(jnp.bfloat16)
     return (att_grad, in_grad, router_grad)
 

time: 152 us -> 161 us (1.059)
  waiting for transfers between devices: 51.4 us -> 32.6 us
  between operations: 1.02 us -> 14.5 us
  matrix products: 10 us -> 15.4 us
  blocking collectives: 11.2 us -> 15.3 us
  local copies, waits for them, and re-layouts: 2.37 us -> 4.13 us
    psum x0 -> x1, blocking collectives: none -> 15.3 us  [shards(): dots = lax.psum(partial_dots, 'tensor').reshape(batch, tok)]
    all_to_all x2, waiting for transfers between devices: 15.6 us -> 0.81 us  [exchange(): lax.all_to_all(parts, 'seq', split_axis=1, concat_axis=1, tiled=True)]
    all_to_all x1 -> x0, blocking collectives: 11.2 us -> none  [shards(): dots = jnp.sum(lax.all_to_all(copies, 'tensor', 0, 0, tiled=True), axis=0)]
    all_to_all x2, starting transfers between devices: 21 us -> 26.7 us  [exchange(): lax.all_to_all(parts, 'seq', split_axis=1, concat_axis=1, tiled=True)]
    all_to_all x1, starting transfers between devices: 21.7 us -> 16.4 us  [shards(): lax.all_to_all(sums, ('dp', 'seq'), 0, 0, tiled=True)]
    dot_general x1 -> x2, matrix products: 1.02 us -> 5.17 us  [the longest x1 4.15 us: shards(): lax.dot_general(gathered, out_weight, (((1,), (1,)), ((), ())), preferred...]
    ppermute x3, starting transfers between devices: 9.8 us -> 12.4 us  [shards(): from_right = lax.ppermute(from_right, 'tensor', leftward)]
    ppermute x3, waiting for transfers between devices: 19 us -> 16.9 us  [shards(): from_left = lax.ppermute(from_left, 'tensor', rightward)]
  transfers between devices with their start and end apart: 11 -> 12, of which waited for: 6 -> 5; matrix products, arithmetic and copies ran while one was open for 11% -> 11% of each run, Pallas kernels for 0% -> 0%
where the time goes in v2:
time: 161 us; the launch traced here: 160 us
  starting transfers between devices  69.8 us (43%)
  waiting for transfers between devices  32.6 us (20%)
  matrix products  15.4 us (10%)
  blocking collectives  15.3 us (10%)
  between operations  14.5 us (9%)
  other arithmetic  8.39 us (5%)
  local copies, waits for them, and re-layouts  4.13 us (3%)
    all_to_all x2, starting transfers between devices, exchange(): lax.all_to_all(parts, 'seq', split_axis=1, concat_axis=1, tiled=True)  26.7 us
    ppermute x3, waiting for transfers between devices, shards(): from_left = lax.ppermute(from_left, 'tensor', rightward)  16.9 us
    all_to_all x1, starting transfers between devices, shards(): lax.all_to_all(sums, ('dp', 'seq'), 0, 0, tiled=True)  16.4 us
    psum x1, blocking collectives, shards(): dots = lax.psum(partial_dots, 'tensor').reshape(batch, tok)  15.3 us
    all_to_all x1, waiting for transfers between devices, shards(): lax.all_to_all(sums, ('dp', 'seq'), 0, 0, tiled=True)  13.2 us
    ppermute x3, starting transfers between devices, shards(): from_right = lax.ppermute(from_right, 'tensor', leftward)  12.4 us
    ppermute x3, starting transfers between devices, shards(): from_left = lax.ppermute(from_left, 'tensor', rightward)  7.77 us
    dot_general x8, matrix products, times(): lax.dot_general(block, weight, (((1,), (1,)), ((), ())), preferred_elemen...  7.33 us
  transfers between devices with their start and end apart: 12, of which 5 were waited for; matrix products, arithmetic and copies ran while one was open for 11% of the time, Pallas kernels for 0%

profile of v2, /device:TPU:1, one launch (start us, length us, event | category | flops | bytes accessed | tf_op | source)
XLA Modules:
  0.0 160.1 jit_solution(9275376862698715737)
XLA Ops:
  7.2 1.8 %fusion.60 = (bf16[1,256,512]{2,1,0:T(8,128)(2,1)}, bf16[256,512]{1,0:T(8,128)(2,1)S(1)}) fusion(bf16[1,512,512]{2,1,0:T(8,128)(2,1)} %param.10), kind=kLoop, calls=%fused_computation.103 | loop fusion | bytes 1048576 | tf_op jit(solution)/shard_map/slice | solution.py:34
  9.0 3.9 %collective-permute-start = (bf16[256,512]{1,0:T(8,128)(2,1)S(1)}, bf16[256,512]{1,0:T(8,128)(2,1)S(1)}, u32[]{:S(2)}, u32[]{:S(2)}) collective-permute-start(bf16[256,512]{1,0:T(8,128)(2,1)S(1)} %get-tuple-element.16), channel_id=1, source_target_pairs={{0,1},{1,2},{2,3},{3,4},{4,5},{5,6},{6,7},{7,0},{8,9},{9,10},{10,1... | collective-permute-start | bytes 786440 | tf_op jit(solution)/shard_map/ppermute | solution.py:39
  13.0 3.3 %collective-permute-start.1 = (bf16[256,512]{1,0:T(8,128)(2,1)S(1)}, bf16[256,512]{1,0:T(8,128)(2,1)S(1)}, u32[]{:S(2)}, u32[]{:S(2)}) collective-permute-start(bf16[256,512]{1,0:T(8,128)(2,1)S(1)} %get-tuple-element.16), channel_id=1, source_target_pairs={{0,7},{1,0},{2,1},{3,2},{4,3},{5,4},{6,5},{7,6},{8,15},{9,8},{10,9... | collective-permute-start | bytes 786440 | tf_op jit(solution)/shard_map/ppermute | solution.py:40
  16.3 0.8 reduce_window_sum.32
  17.2 1.3 fusion.55
  19.7 1.2 convolution_convert_fusion.1
  20.8 17.3 %all-to-all-start = ((bf16[1,16,32,512]{3,2,0,1:T(8,128)(2,1)}), bf16[1,16,32,512]{3,2,0,1:T(8,128)(2,1)S(1)}, u32[]{:S(2)}, u32[]{:S(2)}) async-start(bf16[1,16,32,512]{3,2,0,1:T(8,128)(2,1)} %bitcast.18), calls=%async_computation | async-start | bytes 1048576 | tf_op jit(solution)/shard_map/all_to_all | solution.py:68
  38.1 1.0 reduce-window.6
  40.3 1.4 compare_select_fusion.2
  41.8 1.6 fusion.28
  43.4 1.9 %collective-permute-start.2 = (bf16[256,512]{1,0:T(8,128)(2,1)S(1)}, bf16[256,512]{1,0:T(8,128)(2,1)S(1)}, u32[]{:S(2)}, u32[]{:S(2)}) collective-permute-start(bf16[256,512]{1,0:T(8,128)(2,1)S(1)} %collective-permute-done), channel_id=1, source_target_pairs={{0,1},{1,2},{2,3},{3,4},{4,5},{5,6},{6,7},{7,0},{8,9},{9,10},{10,1... | collective-permute-start | bytes 786440 | tf_op jit(solution)/shard_map/ppermute | solution.py:39
  45.3 4.6 %collective-permute-start.3 = (bf16[256,512]{1,0:T(8,128)(2,1)S(1)}, bf16[256,512]{1,0:T(8,128)(2,1)S(1)}, u32[]{:S(2)}, u32[]{:S(2)}) collective-permute-start(bf16[256,512]{1,0:T(8,128)(2,1)S(1)} %collective-permute-done.1), channel_id=1, source_target_pairs={{0,7},{1,0},{2,1},{3,2},{4,3},{5,4},{6,5},{7,6},{8,15},{9,8},{10,9... | collective-permute-start | bytes 786440 | tf_op jit(solution)/shard_map/ppermute | solution.py:40
  49.9 1.4 convolution_add_fusion.3
  51.3 1.4 convolution_add_fusion.2
  52.7 7.2 %collective-permute-done.2 = bf16[256,512]{1,0:T(8,128)(2,1)S(1)} collective-permute-done((bf16[256,512]{1,0:T(8,128)(2,1)S(1)}, bf16[256,512]{1,0:T(8,128)(2,1)S(1)}, u32[]{:S(2)}, u32[]{:S(2)}) %collective-permute-start.2) | collective-permute-done | bytes 262176 | tf_op jit(solution)/shard_map/ppermute | solution.py:39
  59.9 1.9 %collective-permute-start.4 = (bf16[256,512]{1,0:T(8,128)(2,1)S(1)}, bf16[256,512]{1,0:T(8,128)(2,1)S(1)}, u32[]{:S(2)}, u32[]{:S(2)}) collective-permute-start(bf16[256,512]{1,0:T(8,128)(2,1)S(1)} %collective-permute-done.2), channel_id=1, source_target_pairs={{0,1},{1,2},{2,3},{3,4},{4,5},{5,6},{6,7},{7,0},{8,9},{9,10},{10,1... | collective-permute-start | bytes 786440 | tf_op jit(solution)/shard_map/ppermute | solution.py:39
  61.8 4.6 %collective-permute-start.5 = (bf16[256,512]{1,0:T(8,128)(2,1)S(1)}, bf16[256,512]{1,0:T(8,128)(2,1)S(1)}, u32[]{:S(2)}, u32[]{:S(2)}) collective-permute-start(bf16[256,512]{1,0:T(8,128)(2,1)S(1)} %collective-permute-done.3), channel_id=1, source_target_pairs={{0,7},{1,0},{2,1},{3,2},{4,3},{5,4},{6,5},{7,6},{8,15},{9,8},{10,9... | collective-permute-start | bytes 786440 | tf_op jit(solution)/shard_map/ppermute | solution.py:40
  67.1 9.7 %collective-permute-done.4 = bf16[256,512]{1,0:T(8,128)(2,1)S(1)} collective-permute-done((bf16[256,512]{1,0:T(8,128)(2,1)S(1)}, bf16[256,512]{1,0:T(8,128)(2,1)S(1)}, u32[]{:S(2)}, u32[]{:S(2)}) %collective-permute-start.4) | collective-permute-done | bytes 262176 | tf_op jit(solution)/shard_map/ppermute | solution.py:39
  76.9 1.9 %collective-permute-start.6 = (bf16[128,512]{1,0:T(8,128)(2,1)S(1)}, bf16[128,512]{1,0:T(8,128)(2,1)S(1)}, u32[]{:S(2)}, u32[]{:S(2)}) collective-permute-start(bf16[128,512]{1,0:T(8,128)(2,1)S(1)} %slice.53), channel_id=1, source_target_pairs={{0,1},{1,2},{2,3},{3,4},{4,5},{5,6},{6,7},{7,0},{8,9},{9,10},{10,1... | collective-permute-start | bytes 393224 | tf_op jit(solution)/shard_map/ppermute | solution.py:42
  78.8 4.6 %collective-permute-start.7 = (bf16[128,512]{1,0:T(8,128)(2,1)S(1)}, bf16[128,512]{1,0:T(8,128)(2,1)S(1)}, u32[]{:S(2)}, u32[]{:S(2)}) collective-permute-start(bf16[128,512]{1,0:T(8,128)(2,1)S(1)} %slice.54), channel_id=1, source_target_pairs={{0,7},{1,0},{2,1},{3,2},{4,3},{5,4},{6,5},{7,6},{8,15},{9,8},{10,9... | collective-permute-start | bytes 393224 | tf_op jit(solution)/shard_map/ppermute | solution.py:43
  83.8 1.5 collective-permute-done.7
  86.2 4.1 %fusion = f32[256,512]{1,0:T(8,128)S(1)} fusion(bf16[512,4096]{1,0:T(8,128)(2,1)} %param.12, bf16[1,256,4096]{2,1,0:T(8,128)(2,1)} %all-gather.3.cloned.1.call-done), kind=kOutput, calls=%fused_computation | convolution fusion | flops 1073741824 | bytes 6815744 | tf_op jit(solution)/shard_map/dot_general | solution.py:45
  90.4 1.6 fusion.12
  92.0 1.2 fusion.2
  93.3 9.3 %all-to-all-start.1 = ((bf16[1,16,32,512]{3,2,0,1:T(8,128)(2,1)}), bf16[1,16,32,512]{3,2,0,1:T(8,128)(2,1)S(1)}, u32[]{:S(2)}, u32[]{:S(2)}) async-start(bf16[1,16,32,512]{3,2,0,1:T(8,128)(2,1)} %bitcast.21), calls=%async_computation.1 | async-start | bytes 1048576 | tf_op jit(solution)/shard_map/all_to_all | solution.py:68
  102.6 15.3 %psum.7 = f32[1,512]{1,0:T(1,128)S(1)} all-reduce(f32[1,512]{1,0:T(1,128)S(1)} %bitcast.68), channel_id=1, replica_groups=mesh['dp'=8,'seq'=16,'tensor'=8] {'tensor'}, use_global_device_ids=true, to_apply=%region_6.7 | all-reduce | flops 512 | bytes 4096 | tf_op jit(solution)/shard_map/psum | solution.py:98
  117.9 1.2 multiply_reduce_fusion
  119.9 0.8 broadcast_in_dim.7
  120.7 16.4 %all-to-all-start.2 = ((f32[128,1,512]{2,1,0:T(1,128)}), f32[128,1,512]{2,1,0:T(1,128)S(1)}, u32[]{:S(2)}, u32[]{:S(2)}) async-start(f32[128,1,512]{2,1,0:T(1,128)} %broadcast_in_dim.7), calls=%async_computation.2 | async-start | bytes 524288 | tf_op jit(solution)/shard_map/all_to_all | solution.py:107
  137.2 1.0 add_convert_fusion
  138.2 1.0 fusion.7
  139.2 13.2 %all-to-all-done.2 = f32[128,1,512]{2,1,0:T(1,128)S(1)} async-done(((f32[128,1,512]{2,1,0:T(1,128)}), f32[128,1,512]{2,1,0:T(1,128)S(1)}, u32[]{:S(2)}, u32[]{:S(2)}) %all-to-all-start.2) | async-done | bytes 262176 | tf_op jit(solution)/shard_map/all_to_all | solution.py:107
  (51 shorter events, 6.0 us)
Async XLA Ops:
  7.2 12.5 %copy-start = (bf16[1,256,512]{2,1,0:T(8,128)(2,1)S(1)}, bf16[1,256,512]{2,1,0:T(8,128)(2,1)}, u32[]{:S(2)}) copy-start(bf16[1,256,512]{2,1,0:T(8,128)(2,1)} %param.11) | copy-start | bytes 786436
  7.2 79.0 %all-gather.3.cloned.1.call-start = ((), (), s32[]{:S(2)}) async-start(), calls=%async_computation.3 | async-start | bytes 2359296 | tf_op jit(solution)/shard_map/all_gather | solution.py:34
  9.0 34.4 %collective-permute-start = (bf16[256,512]{1,0:T(8,128)(2,1)S(1)}, bf16[256,512]{1,0:T(8,128)(2,1)S(1)}, u32[]{:S(2)}, u32[]{:S(2)}) collective-permute-start(bf16[256,512]{1,0:T(8,128)(2,1)S(1)} %get-tuple-element.16), channel_id=1, source_target_pairs={{0,1},{1,2},{2,3},{3,4},{4,5},{5,6},{6,7},{7,0},{8,9},{9,10},{10,1... | collective-permute-start | bytes 786440 | tf_op jit(solution)/shard_map/ppermute | solution.py:39
  13.0 32.3 %collective-permute-start.1 = (bf16[256,512]{1,0:T(8,128)(2,1)S(1)}, bf16[256,512]{1,0:T(8,128)(2,1)S(1)}, u32[]{:S(2)}, u32[]{:S(2)}) collective-permute-start(bf16[256,512]{1,0:T(8,128)(2,1)S(1)} %get-tuple-element.16), channel_id=1, source_target_pairs={{0,7},{1,0},{2,1},{3,2},{4,3},{5,4},{6,5},{7,6},{8,15},{9,8},{10,9... | collective-permute-start | bytes 786440 | tf_op jit(solution)/shard_map/ppermute | solution.py:40
  20.8 64.8 %all-to-all-start = ((bf16[1,16,32,512]{3,2,0,1:T(8,128)(2,1)}), bf16[1,16,32,512]{3,2,0,1:T(8,128)(2,1)S(1)}, u32[]{:S(2)}, u32[]{:S(2)}) async-start(bf16[1,16,32,512]{3,2,0,1:T(8,128)(2,1)} %bitcast.18), calls=%async_computation | async-start | bytes 1048576 | tf_op jit(solution)/shard_map/all_to_all | solution.py:68
  41.8 24.7 %copy-start.1 = (bf16[512,4096]{1,0:T(8,128)(2,1)S(1)}, bf16[512,4096]{1,0:T(8,128)(2,1)}, u32[]{:S(2)}) copy-start(bf16[512,4096]{1,0:T(8,128)(2,1)} %param.12) | copy-start | bytes 12582916
  43.4 16.5 %collective-permute-start.2 = (bf16[256,512]{1,0:T(8,128)(2,1)S(1)}, bf16[256,512]{1,0:T(8,128)(2,1)S(1)}, u32[]{:S(2)}, u32[]{:S(2)}) collective-permute-start(bf16[256,512]{1,0:T(8,128)(2,1)S(1)} %collective-permute-done), channel_id=1, source_target_pairs={{0,1},{1,2},{2,3},{3,4},{4,5},{5,6},{6,7},{7,0},{8,9},{9,10},{10,1... | collective-permute-start | bytes 786440 | tf_op jit(solution)/shard_map/ppermute | solution.py:39
  45.3 16.5 %collective-permute-start.3 = (bf16[256,512]{1,0:T(8,128)(2,1)S(1)}, bf16[256,512]{1,0:T(8,128)(2,1)S(1)}, u32[]{:S(2)}, u32[]{:S(2)}) collective-permute-start(bf16[256,512]{1,0:T(8,128)(2,1)S(1)} %collective-permute-done.1), channel_id=1, source_target_pairs={{0,7},{1,0},{2,1},{3,2},{4,3},{5,4},{6,5},{7,6},{8,15},{9,8},{10,9... | collective-permute-start | bytes 786440 | tf_op jit(solution)/shard_map/ppermute | solution.py:40
  59.9 16.9 %collective-permute-start.4 = (bf16[256,512]{1,0:T(8,128)(2,1)S(1)}, bf16[256,512]{1,0:T(8,128)(2,1)S(1)}, u32[]{:S(2)}, u32[]{:S(2)}) collective-permute-start(bf16[256,512]{1,0:T(8,128)(2,1)S(1)} %collective-permute-done.2), channel_id=1, source_target_pairs={{0,1},{1,2},{2,3},{3,4},{4,5},{5,6},{6,7},{7,0},{8,9},{9,10},{10,1... | collective-permute-start | bytes 786440 | tf_op jit(solution)/shard_map/ppermute | solution.py:39
  61.8 16.9 %collective-permute-start.5 = (bf16[256,512]{1,0:T(8,128)(2,1)S(1)}, bf16[256,512]{1,0:T(8,128)(2,1)S(1)}, u32[]{:S(2)}, u32[]{:S(2)}) collective-permute-start(bf16[256,512]{1,0:T(8,128)(2,1)S(1)} %collective-permute-done.3), channel_id=1, source_target_pairs={{0,7},{1,0},{2,1},{3,2},{4,3},{5,4},{6,5},{7,6},{8,15},{9,8},{10,9... | collective-permute-start | bytes 786440 | tf_op jit(solution)/shard_map/ppermute | solution.py:40
  76.8 8.8 %copy-start.3 = (bf16[256,512]{1,0:T(8,128)(2,1)}, bf16[256,512]{1,0:T(8,128)(2,1)S(1)}, u32[]{:S(2)}) copy-start(bf16[256,512]{1,0:T(8,128)(2,1)S(1)} %collective-permute-done.4) | copy-start | bytes 786436
  76.9 6.9 %collective-permute-start.6 = (bf16[128,512]{1,0:T(8,128)(2,1)S(1)}, bf16[128,512]{1,0:T(8,128)(2,1)S(1)}, u32[]{:S(2)}, u32[]{:S(2)}) collective-permute-start(bf16[128,512]{1,0:T(8,128)(2,1)S(1)} %slice.53), channel_id=1, source_target_pairs={{0,1},{1,2},{2,3},{3,4},{4,5},{5,6},{6,7},{7,0},{8,9},{9,10},{10,1... | collective-permute-start | bytes 393224 | tf_op jit(solution)/shard_map/ppermute | solution.py:42
  78.8 6.5 %collective-permute-start.7 = (bf16[128,512]{1,0:T(8,128)(2,1)S(1)}, bf16[128,512]{1,0:T(8,128)(2,1)S(1)}, u32[]{:S(2)}, u32[]{:S(2)}) collective-permute-start(bf16[128,512]{1,0:T(8,128)(2,1)S(1)} %slice.54), channel_id=1, source_target_pairs={{0,7},{1,0},{2,1},{3,2},{4,3},{5,4},{6,5},{7,6},{8,15},{9,8},{10,9... | collective-permute-start | bytes 393224 | tf_op jit(solution)/shard_map/ppermute | solution.py:43
  86.2 4.2 %copy-start.4 = (bf16[256,512]{1,0:T(8,128)(2,1)S(1)}, bf16[256,512]{1,0:T(8,128)(2,1)}, u32[]{:S(2)}) copy-start(bf16[256,512]{1,0:T(8,128)(2,1)} %copy-done.3) | copy-start | bytes 786436
  90.4 27.5 %copy-start.5 = (bf16[1,512]{1,0:T(2,128)(2,1)S(1)}, bf16[1,512]{1,0:T(2,128)(2,1)}, u32[]{:S(2)}) copy-start(bf16[1,512]{1,0:T(2,128)(2,1)} %param.9) | copy-start | bytes 3076
  90.4 46.8 %copy-start.2 = (bf16[1,512,512]{2,1,0:T(8,128)(2,1)S(1)}, bf16[1,512,512]{2,1,0:T(8,128)(2,1)}, u32[]{:S(2)}) copy-start(bf16[1,512,512]{2,1,0:T(8,128)(2,1)} %param.10) | copy-start | bytes 1572868
  90.4 46.8 %copy-start.6 = (f32[512]{0:T(512)S(1)}, f32[512]{0:T(512)}, u32[]{:S(2)}) copy-start(f32[512]{0:T(512)} %param.13) | copy-start | bytes 6148
  93.3 26.7 %all-to-all-start.1 = ((bf16[1,16,32,512]{3,2,0,1:T(8,128)(2,1)}), bf16[1,16,32,512]{3,2,0,1:T(8,128)(2,1)S(1)}, u32[]{:S(2)}, u32[]{:S(2)}) async-start(bf16[1,16,32,512]{3,2,0,1:T(8,128)(2,1)} %bitcast.21), calls=%async_computation.1 | async-start | bytes 1048576 | tf_op jit(solution)/shard_map/all_to_all | solution.py:68
  120.7 31.7 %all-to-all-start.2 = ((f32[128,1,512]{2,1,0:T(1,128)}), f32[128,1,512]{2,1,0:T(1,128)S(1)}, u32[]{:S(2)}, u32[]{:S(2)}) async-start(f32[128,1,512]{2,1,0:T(1,128)} %broadcast_in_dim.7), calls=%async_computation.2 | async-start | bytes 524288 | tf_op jit(solution)/shard_map/all_to_all | solution.py:107
Sparse Core Ops, SparseCore 0:
  16.4 63.7 all-gather.2

commit v3 on v1

--- a/solution.py
+++ b/solution.py
@@ -29,18 +29,6 @@
             block, weight, (((1,), (1,)), ((), ())), preferred_element_type=jnp.float32
         )
 
-    own = cotangent.reshape(batch * tok, width)
-    rows = batch * tok
-    product = times(own, 0)
-    from_left, from_right = own, own
-    for step in range(1, nten // 2):
-        from_left = lax.ppermute(from_left, "tensor", rightward)
-        from_right = lax.ppermute(from_right, "tensor", leftward)
-        product = product + times(from_left, -step) + times(from_right, step)
-    upper = lax.ppermute(from_left[: rows // 2], "tensor", rightward)
-    lower = lax.ppermute(from_right[rows // 2 :], "tensor", leftward)
-    product = product + times(jnp.concatenate([upper, lower], axis=0), nten // 2)
-
     lanes = jnp.arange(nseq, dtype=jnp.int32)
     offsets = jnp.cumsum(shard_counts, axis=1) - shard_counts
     own_offset = jnp.sum(jnp.where(lanes[None, :] < here, shard_counts, 0), axis=1)
@@ -59,26 +47,47 @@
     ).astype(jnp.bfloat16)
 
     def exchange(slots):
-        parts = slots.astype(jnp.bfloat16).reshape(batch, nseq, cap, slots.shape[2])
+        parts = slots.reshape(batch, nseq, cap, slots.shape[2])
         moved = lax.all_to_all(parts, "seq", split_axis=1, concat_axis=1, tiled=True)
         return moved.reshape(batch, tok, slots.shape[2])
 
-    att_slots = jnp.einsum(
-        "bks,bkw->bsw", place_table, attended, preferred_element_type=jnp.float32
-    )
-    att_tok = jnp.einsum(
-        "bst,bsw->btw", slot_table, exchange(att_slots), preferred_element_type=jnp.float32
-    )
+    own = cotangent.reshape(batch * tok, width)
+    rows = batch * tok
+    from_left, from_right = own, own
+    product = times(own, 0)
+    for step in range(1, nten // 2):
+        from_left = lax.ppermute(from_left, "tensor", rightward)
+        from_right = lax.ppermute(from_right, "tensor", leftward)
+        if step == 1:
+            attended, place_table, from_left, from_right, product = lax.optimization_barrier(
+                (attended, place_table, from_left, from_right, product)
+            )
+            att_slots = jnp.einsum(
+                "bks,bkw->bsw", place_table, attended, preferred_element_type=jnp.float32
+            ).astype(jnp.bfloat16)
+            att_in = exchange(att_slots)
+        product = product + times(from_left, -step) + times(from_right, step)
+    upper = lax.ppermute(from_left[: rows // 2], "tensor", rightward)
+    lower = lax.ppermute(from_right[rows // 2 :], "tensor", leftward)
+    product = product + times(jnp.concatenate([upper, lower], axis=0), nten // 2)
+    att_tok = jnp.einsum("bst,bsw->btw", slot_table, att_in, preferred_element_type=jnp.float32)
 
+    rate = jax.nn.sigmoid(logits.astype(jnp.float32))
     back = product.reshape(batch, tok, heads_width)
     partial_dots = jnp.sum(att_tok * back, axis=2)
-    copies = jnp.broadcast_to(partial_dots[None], (nten, batch, tok))
-    dots = jnp.sum(lax.all_to_all(copies, "tensor", 0, 0, tiled=True), axis=0)
-    rate = jax.nn.sigmoid(logits.astype(jnp.float32))
+    grad_tok = (rate[:, :, None] * back).astype(jnp.bfloat16)
+    grad_slots = jnp.einsum(
+        "bst,btw->bsw", slot_table, grad_tok, preferred_element_type=jnp.float32
+    ).astype(jnp.bfloat16)
+    grad_slots, partial_dots = lax.optimization_barrier((grad_slots, partial_dots))
+    grad_in = exchange(grad_slots)
+    dots = lax.psum(partial_dots, "tensor")
     logit_grad = rate * (1.0 - rate) * dots
     partial_sum = scale * jnp.sum(
         inputs.astype(jnp.float32) * logit_grad[:, :, None], axis=(0, 1)
     )
+    grad_in, partial_sum = lax.optimization_barrier((grad_in, partial_sum))
+
     group = lax.axis_size("dp") * nseq
     sums = jnp.broadcast_to(partial_sum[None], (group, width))
     router_grad = jnp.sum(lax.all_to_all(sums, ("dp", "seq"), 0, 0, tiled=True), axis=0)
@@ -86,13 +95,8 @@
         cotangent.astype(jnp.float32)
         + scale * logit_grad[:, :, None] * router_weight[None, None, :]
     ).astype(jnp.bfloat16)
-
-    grad_tok = (rate[:, :, None] * back).astype(jnp.bfloat16)
-    grad_slots = jnp.einsum(
-        "bst,btw->bsw", slot_table, grad_tok, preferred_element_type=jnp.float32
-    )
     att_grad = jnp.einsum(
-        "bks,bsw->bkw", place_table, exchange(grad_slots), preferred_element_type=jnp.float32
+        "bks,bsw->bkw", place_table, grad_in, preferred_element_type=jnp.float32
     ).astype(jnp.bfloat16)
     return (att_grad, in_grad, router_grad)
 

time: 152 us -> 140 us (0.921)
  waiting for transfers between devices: 51.4 us -> 26.8 us
  starting transfers between devices: 68.4 us -> 73 us
  blocking collectives: 11.2 us -> 15.3 us
  matrix products: 10 us -> 13.5 us
    psum x0 -> x1, blocking collectives: none -> 15.3 us  [shards(): dots = lax.psum(partial_dots, 'tensor')]
    all_to_all x2, waiting for transfers between devices: 15.6 us -> 1.82 us  [exchange(): lax.all_to_all(parts, 'seq', split_axis=1, concat_axis=1, tiled=True)]
    all_to_all x1 -> x0, blocking collectives: 11.2 us -> none  [shards(): dots = jnp.sum(lax.all_to_all(copies, 'tensor', 0, 0, tiled=True), axis=0)]
    ppermute x3, waiting for transfers between devices: 19 us -> 8.02 us  [shards(): from_left = lax.ppermute(from_left, 'tensor', rightward)]
    all_to_all x2, starting transfers between devices: 21 us -> 28.7 us  [exchange(): lax.all_to_all(parts, 'seq', split_axis=1, concat_axis=1, tiled=True)]
    all_to_all x1, starting transfers between devices: 21.7 us -> 16.4 us  [shards(): lax.all_to_all(sums, ('dp', 'seq'), 0, 0, tiled=True)]
    dot_general x8, matrix products: 6.04 us -> 8.5 us  [times(): lax.dot_general(block, weight, (((1,), (1,)), ((), ())), preferred_elemen...]
    ppermute x3, starting transfers between devices: 9.35 us -> 11.6 us  [shards(): from_left = lax.ppermute(from_left, 'tensor', rightward)]
  transfers between devices with their start and end apart: 11 -> 11, of which waited for: 6 -> 5; matrix products, arithmetic and copies ran while one was open for 11% -> 13% of each run, Pallas kernels for 0% -> 0%
where the time goes in v3:
time: 140 us
  starting transfers between devices  73 us (52%)
  waiting for transfers between devices  26.8 us (19%)
  blocking collectives  15.3 us (11%)
  matrix products  13.5 us (10%)
  other arithmetic  7.39 us (5%)
  local copies, waits for them, and re-layouts  2.34 us (2%)
    all_to_all x2, starting transfers between devices, exchange(): lax.all_to_all(parts, 'seq', split_axis=1, concat_axis=1, tiled=True)  28.7 us
    all_to_all x1, starting transfers between devices, shards(): lax.all_to_all(sums, ('dp', 'seq'), 0, 0, tiled=True)  16.4 us
    psum x1, blocking collectives, shards(): dots = lax.psum(partial_dots, 'tensor')  15.3 us
    all_to_all x1, waiting for transfers between devices, shards(): lax.all_to_all(sums, ('dp', 'seq'), 0, 0, tiled=True)  13.2 us
    ppermute x3, starting transfers between devices, shards(): from_left = lax.ppermute(from_left, 'tensor', rightward)  11.6 us
    ppermute x3, starting transfers between devices, shards(): from_right = lax.ppermute(from_right, 'tensor', leftward)  9.8 us
    dot_general x8, matrix products, times(): lax.dot_general(block, weight, (((1,), (1,)), ((), ())), preferred_elemen...  8.5 us
    ppermute x3, waiting for transfers between devices, shards(): from_left = lax.ppermute(from_left, 'tensor', rightward)  8.02 us
  transfers between devices with their start and end apart: 11, of which 5 were waited for; matrix products, arithmetic and copies ran while one was open for 13% of the time, Pallas kernels for 0%

profile of v3, /device:TPU:1, one launch (start us, length us, event | category | flops | bytes accessed | tf_op | source)
XLA Modules:
  0.0 139.5 jit_solution(3958402168480506688)
XLA Ops:
  0.6 4.1 %collective-permute-start = (bf16[512,512]{1,0:T(8,128)(2,1)}, bf16[512,512]{1,0:T(8,128)(2,1)S(1)}, u32[]{:S(2)}, u32[]{:S(2)}) collective-permute-start(bf16[512,512]{1,0:T(8,128)(2,1)} %bitcast.53), channel_id=1, source_target_pairs={{0,1},{1,2},{2,3},{3,4},{4,5},{5,6},{6,7},{7,0},{8,9},{9,10},{10,1... | collective-permute-start | bytes 1572872 | tf_op jit(solution)/shard_map/ppermute | solution.py:59
  4.7 3.3 %collective-permute-start.1 = (bf16[512,512]{1,0:T(8,128)(2,1)}, bf16[512,512]{1,0:T(8,128)(2,1)S(1)}, u32[]{:S(2)}, u32[]{:S(2)}) collective-permute-start(bf16[512,512]{1,0:T(8,128)(2,1)} %bitcast.54), channel_id=1, source_target_pairs={{0,7},{1,0},{2,1},{3,2},{4,3},{5,4},{6,5},{7,6},{8,15},{9,8},{10,9... | collective-permute-start | bytes 1572872 | tf_op jit(solution)/shard_map/ppermute | solution.py:60
  8.1 0.8 reduce_window_sum.32
  8.9 1.3 fusion.47
  11.4 1.0 reduce-window.6
  12.8 1.4 compare_select_fusion.2
  15.1 1.7 %convolution_bitcast_fusion = f32[512,512]{0,1:T(8,128)S(1)} fusion(bf16[512,4096]{1,0:T(8,128)(2,1)} %param.12, s32[]{:T(128)S(6)} %select_n.128, bf16[1,512,512]{2,1,0:T(8,128)(2,1)} %param.10), kind=kOutput, calls=%fused_computation.4 | convolution fusion | flops 268435456 | bytes 2097156 | tf_op jit(solution)/shard_map/dot_general | solution.py:28
  16.8 5.6 %collective-permute-start.2 = (bf16[512,512]{1,0:T(8,128)(2,1)S(1)}, bf16[512,512]{1,0:T(8,128)(2,1)}, u32[]{:S(2)}, u32[]{:S(2)}) collective-permute-start(bf16[512,512]{1,0:T(8,128)(2,1)S(1)} %collective-permute-done), channel_id=1, source_target_pairs={{0,1},{1,2},{2,3},{3,4},{4,5},{5,6},{6,7},{7,0},{8,9},{9,10},{10,1... | collective-permute-start | bytes 1572872 | tf_op jit(solution)/shard_map/ppermute | solution.py:59
  22.4 1.9 %collective-permute-start.3 = (bf16[512,512]{1,0:T(8,128)(2,1)S(1)}, bf16[512,512]{1,0:T(8,128)(2,1)S(1)}, u32[]{:S(2)}, u32[]{:S(2)}) collective-permute-start(bf16[512,512]{1,0:T(8,128)(2,1)S(1)} %collective-permute-done.1), channel_id=1, source_target_pairs={{0,7},{1,0},{2,1},{3,2},{4,3},{5,4},{6,5},{7,6},{8,15},{9,8},{10,9... | collective-permute-start | bytes 1572872 | tf_op jit(solution)/shard_map/ppermute | solution.py:60
  24.4 1.1 convolution_convert_fusion.1
  25.5 19.6 %all-to-all-start = ((bf16[1,16,32,512]{3,2,0,1:T(8,128)(2,1)}), bf16[1,16,32,512]{3,2,0,1:T(8,128)(2,1)}, u32[]{:S(2)}, u32[]{:S(2)}) async-start(bf16[1,16,32,512]{3,2,0,1:T(8,128)(2,1)} %bitcast.16), calls=%async_computation | async-start | bytes 1048576 | tf_op jit(solution)/shard_map/all_to_all | solution.py:51
  45.1 1.7 %fusion.21 = f32[512,512]{0,1:T(8,128)S(1)} fusion(bf16[512,512]{1,0:T(8,128)(2,1)S(1)} %collective-permute-done.1, bf16[512,4096]{1,0:T(8,128)(2,1)} %param.12, s32[]{:T(128)S(6)} %select_n.136), kind=kOutput, calls=%fused_computation.31 | convolution fusion | flops 268435456 | bytes 2097156 | tf_op jit(solution)/shard_map/dot_general | solution.py:28
  46.8 1.5 %fusion.23 = f32[512,512]{0,1:T(8,128)S(1)} fusion(bf16[512,512]{1,0:T(8,128)(2,1)S(1)} %collective-permute-done, bf16[512,4096]{1,0:T(8,128)(2,1)} %param.12, s32[]{:T(128)S(6)} %select_n.134), kind=kOutput, calls=%fused_computation.33 | convolution fusion | flops 268435456 | bytes 2097156 | tf_op jit(solution)/shard_map/dot_general | solution.py:28
  48.3 1.9 %collective-permute-start.4 = (bf16[512,512]{1,0:T(8,128)(2,1)}, bf16[512,512]{1,0:T(8,128)(2,1)S(1)}, u32[]{:S(2)}, u32[]{:S(2)}) collective-permute-start(bf16[512,512]{1,0:T(8,128)(2,1)} %collective-permute-done.2), channel_id=1, source_target_pairs={{0,1},{1,2},{2,3},{3,4},{4,5},{5,6},{6,7},{7,0},{8,9},{9,10},{10,1... | collective-permute-start | bytes 1572872 | tf_op jit(solution)/shard_map/ppermute | solution.py:59
  50.2 4.6 %collective-permute-start.5 = (bf16[512,512]{1,0:T(8,128)(2,1)S(1)}, bf16[512,512]{1,0:T(8,128)(2,1)S(1)}, u32[]{:S(2)}, u32[]{:S(2)}) collective-permute-start(bf16[512,512]{1,0:T(8,128)(2,1)S(1)} %collective-permute-done.3), channel_id=1, source_target_pairs={{0,7},{1,0},{2,1},{3,2},{4,3},{5,4},{6,5},{7,6},{8,15},{9,8},{10,9... | collective-permute-start | bytes 1572872 | tf_op jit(solution)/shard_map/ppermute | solution.py:60
  55.3 1.5 %fusion.19 = f32[512,512]{0,1:T(8,128)S(1)} fusion(bf16[512,512]{1,0:T(8,128)(2,1)} %collective-permute-done.2, bf16[512,4096]{1,0:T(8,128)(2,1)S(1)} %copy-done.1, s32[]{:T(128)S(6)} %select_n.138), kind=kOutput, calls=%fused_computation.29 | convolution fusion | flops 268435456 | bytes 2097156 | tf_op jit(solution)/shard_map/dot_general | solution.py:28
  56.8 8.0 %collective-permute-done.4 = bf16[512,512]{1,0:T(8,128)(2,1)S(1)} collective-permute-done((bf16[512,512]{1,0:T(8,128)(2,1)}, bf16[512,512]{1,0:T(8,128)(2,1)S(1)}, u32[]{:S(2)}, u32[]{:S(2)}) %collective-permute-start.4) | collective-permute-done | bytes 524320 | tf_op jit(solution)/shard_map/ppermute | solution.py:59
  64.9 1.9 %collective-permute-start.6 = (bf16[256,512]{1,0:T(8,128)(2,1)S(1)}, bf16[256,512]{1,0:T(8,128)(2,1)S(1)}, u32[]{:S(2)}, u32[]{:S(2)}) collective-permute-start(bf16[256,512]{1,0:T(8,128)(2,1)S(1)} %slice.16), channel_id=1, source_target_pairs={{0,1},{1,2},{2,3},{3,4},{4,5},{5,6},{6,7},{7,0},{8,9},{9,10},{10,1... | collective-permute-start | bytes 786440 | tf_op jit(solution)/shard_map/ppermute | solution.py:70
  66.8 4.6 %collective-permute-start.7 = (bf16[256,512]{1,0:T(8,128)(2,1)S(1)}, bf16[256,512]{1,0:T(8,128)(2,1)S(1)}, u32[]{:S(2)}, u32[]{:S(2)}) collective-permute-start(bf16[256,512]{1,0:T(8,128)(2,1)S(1)} %slice.17), channel_id=1, source_target_pairs={{0,7},{1,0},{2,1},{3,2},{4,3},{5,4},{6,5},{7,6},{8,15},{9,8},{10,9... | collective-permute-start | bytes 786440 | tf_op jit(solution)/shard_map/ppermute | solution.py:71
  71.9 2.8 %collective-permute-done.6 = bf16[256,512]{1,0:T(8,128)(2,1)S(1)} collective-permute-done((bf16[256,512]{1,0:T(8,128)(2,1)S(1)}, bf16[256,512]{1,0:T(8,128)(2,1)S(1)}, u32[]{:S(2)}, u32[]{:S(2)}) %collective-permute-start.6) | collective-permute-done | bytes 262176 | tf_op jit(solution)/shard_map/ppermute | solution.py:70
  74.7 0.9 collective-permute-done.7
  76.9 1.6 %fusion.2 = f32[512]{0:T(512)S(1)} fusion(f32[512,512]{0,1:T(8,128)S(1)} %fusion.1, bf16[512,512]{1,0:T(8,128)(2,1)} %bitcast.17, s32[512]{0:T(512)S(1)} %bitcast.59), kind=kOutput, calls=%fused_computation.7 | convolution fusion | flops 269221376 | bytes 1576960 | tf_op jit(solution)/shard_map/bst,bsw->btw/dot_general | solution.py:73
  78.5 1.3 fusion.3
  79.8 9.1 %all-to-all-start.1 = ((bf16[1,16,32,512]{3,2,0,1:T(8,128)(2,1)}), bf16[1,16,32,512]{3,2,0,1:T(8,128)(2,1)S(1)}, u32[]{:S(2)}, u32[]{:S(2)}) async-start(bf16[1,16,32,512]{3,2,0,1:T(8,128)(2,1)} %bitcast.20), calls=%async_computation.1 | async-start | bytes 1048576 | tf_op jit(solution)/shard_map/all_to_all | solution.py:51
  88.9 15.3 %psum.7 = f32[1,512]{1,0:T(1,128)S(1)} all-reduce(f32[1,512]{1,0:T(1,128)S(1)} %bitcast.64), channel_id=1, replica_groups=mesh['dp'=8,'seq'=16,'tensor'=8] {'tensor'}, use_global_device_ids=true, to_apply=%region_5.6 | all-reduce | flops 512 | bytes 4096 | tf_op jit(solution)/shard_map/psum | solution.py:84
  104.4 1.8 %all-to-all-done.1 = bf16[1,16,32,512]{3,2,0,1:T(8,128)(2,1)S(1)} async-done(((bf16[1,16,32,512]{3,2,0,1:T(8,128)(2,1)}), bf16[1,16,32,512]{3,2,0,1:T(8,128)(2,1)S(1)}, u32[]{:S(2)}, u32[]{:S(2)}) %all-to-all-start.1) | async-done | bytes 524320 | tf_op jit(solution)/shard_map/all_to_all | solution.py:51
  106.2 0.8 broadcast_in_dim.7
  107.1 16.4 %all-to-all-start.2 = ((f32[128,1,512]{2,1,0:T(1,128)}), f32[128,1,512]{2,1,0:T(1,128)S(1)}, u32[]{:S(2)}, u32[]{:S(2)}) async-start(f32[128,1,512]{2,1,0:T(1,128)} %broadcast_in_dim.7), calls=%async_computation.2 | async-start | bytes 524288 | tf_op jit(solution)/shard_map/all_to_all | solution.py:93
  123.5 1.0 add_convert_fusion
  124.5 1.0 fusion.4
  125.5 13.2 %all-to-all-done.2 = f32[128,1,512]{2,1,0:T(1,128)S(1)} async-done(((f32[128,1,512]{2,1,0:T(1,128)}), f32[128,1,512]{2,1,0:T(1,128)S(1)}, u32[]{:S(2)}, u32[]{:S(2)}) %all-to-all-start.2) | async-done | bytes 262176 | tf_op jit(solution)/shard_map/all_to_all | solution.py:93
  138.7 0.8 reduce_sum.42
  (43 shorter events, 4.8 us)
Async XLA Ops:
  0.6 23.7 %copy-start = (bf16[1,256,512]{2,1,0:T(8,128)(2,1)S(1)}, bf16[1,256,512]{2,1,0:T(8,128)(2,1)}, u32[]{:S(2)}) copy-start(bf16[1,256,512]{2,1,0:T(8,128)(2,1)} %param.11) | copy-start | bytes 786436
  0.6 16.1 %collective-permute-start = (bf16[512,512]{1,0:T(8,128)(2,1)}, bf16[512,512]{1,0:T(8,128)(2,1)S(1)}, u32[]{:S(2)}, u32[]{:S(2)}) collective-permute-start(bf16[512,512]{1,0:T(8,128)(2,1)} %bitcast.53), channel_id=1, source_target_pairs={{0,1},{1,2},{2,3},{3,4},{4,5},{5,6},{6,7},{7,0},{8,9},{9,10},{10,1... | collective-permute-start | bytes 1572872 | tf_op jit(solution)/shard_map/ppermute | solution.py:59
  4.7 12.0 %collective-permute-start.1 = (bf16[512,512]{1,0:T(8,128)(2,1)}, bf16[512,512]{1,0:T(8,128)(2,1)S(1)}, u32[]{:S(2)}, u32[]{:S(2)}) collective-permute-start(bf16[512,512]{1,0:T(8,128)(2,1)} %bitcast.54), channel_id=1, source_target_pairs={{0,7},{1,0},{2,1},{3,2},{4,3},{5,4},{6,5},{7,6},{8,15},{9,8},{10,9... | collective-permute-start | bytes 1572872 | tf_op jit(solution)/shard_map/ppermute | solution.py:60
  16.8 31.5 %collective-permute-start.2 = (bf16[512,512]{1,0:T(8,128)(2,1)S(1)}, bf16[512,512]{1,0:T(8,128)(2,1)}, u32[]{:S(2)}, u32[]{:S(2)}) collective-permute-start(bf16[512,512]{1,0:T(8,128)(2,1)S(1)} %collective-permute-done), channel_id=1, source_target_pairs={{0,1},{1,2},{2,3},{3,4},{4,5},{5,6},{6,7},{7,0},{8,9},{9,10},{10,1... | collective-permute-start | bytes 1572872 | tf_op jit(solution)/shard_map/ppermute | solution.py:59
  22.4 27.8 %collective-permute-start.3 = (bf16[512,512]{1,0:T(8,128)(2,1)S(1)}, bf16[512,512]{1,0:T(8,128)(2,1)S(1)}, u32[]{:S(2)}, u32[]{:S(2)}) collective-permute-start(bf16[512,512]{1,0:T(8,128)(2,1)S(1)} %collective-permute-done.1), channel_id=1, source_target_pairs={{0,7},{1,0},{2,1},{3,2},{4,3},{5,4},{6,5},{7,6},{8,15},{9,8},{10,9... | collective-permute-start | bytes 1572872 | tf_op jit(solution)/shard_map/ppermute | solution.py:60
  25.5 51.4 %all-to-all-start = ((bf16[1,16,32,512]{3,2,0,1:T(8,128)(2,1)}), bf16[1,16,32,512]{3,2,0,1:T(8,128)(2,1)}, u32[]{:S(2)}, u32[]{:S(2)}) async-start(bf16[1,16,32,512]{3,2,0,1:T(8,128)(2,1)} %bitcast.16), calls=%async_computation | async-start | bytes 1048576 | tf_op jit(solution)/shard_map/all_to_all | solution.py:51
  45.1 9.7 %copy-start.1 = (bf16[512,4096]{1,0:T(8,128)(2,1)S(1)}, bf16[512,4096]{1,0:T(8,128)(2,1)}, u32[]{:S(2)}) copy-start(bf16[512,4096]{1,0:T(8,128)(2,1)} %param.12) | copy-start | bytes 12582916
  48.3 16.5 %collective-permute-start.4 = (bf16[512,512]{1,0:T(8,128)(2,1)}, bf16[512,512]{1,0:T(8,128)(2,1)S(1)}, u32[]{:S(2)}, u32[]{:S(2)}) collective-permute-start(bf16[512,512]{1,0:T(8,128)(2,1)} %collective-permute-done.2), channel_id=1, source_target_pairs={{0,1},{1,2},{2,3},{3,4},{4,5},{5,6},{6,7},{7,0},{8,9},{9,10},{10,1... | collective-permute-start | bytes 1572872 | tf_op jit(solution)/shard_map/ppermute | solution.py:59
  50.2 16.6 %collective-permute-start.5 = (bf16[512,512]{1,0:T(8,128)(2,1)S(1)}, bf16[512,512]{1,0:T(8,128)(2,1)S(1)}, u32[]{:S(2)}, u32[]{:S(2)}) collective-permute-start(bf16[512,512]{1,0:T(8,128)(2,1)S(1)} %collective-permute-done.3), channel_id=1, source_target_pairs={{0,7},{1,0},{2,1},{3,2},{4,3},{5,4},{6,5},{7,6},{8,15},{9,8},{10,9... | collective-permute-start | bytes 1572872 | tf_op jit(solution)/shard_map/ppermute | solution.py:60
  64.9 9.8 %collective-permute-start.6 = (bf16[256,512]{1,0:T(8,128)(2,1)S(1)}, bf16[256,512]{1,0:T(8,128)(2,1)S(1)}, u32[]{:S(2)}, u32[]{:S(2)}) collective-permute-start(bf16[256,512]{1,0:T(8,128)(2,1)S(1)} %slice.16), channel_id=1, source_target_pairs={{0,1},{1,2},{2,3},{3,4},{4,5},{5,6},{6,7},{7,0},{8,9},{9,10},{10,1... | collective-permute-start | bytes 786440 | tf_op jit(solution)/shard_map/ppermute | solution.py:70
  66.8 8.8 %collective-permute-start.7 = (bf16[256,512]{1,0:T(8,128)(2,1)S(1)}, bf16[256,512]{1,0:T(8,128)(2,1)S(1)}, u32[]{:S(2)}, u32[]{:S(2)}) collective-permute-start(bf16[256,512]{1,0:T(8,128)(2,1)S(1)} %slice.17), channel_id=1, source_target_pairs={{0,7},{1,0},{2,1},{3,2},{4,3},{5,4},{6,5},{7,6},{8,15},{9,8},{10,9... | collective-permute-start | bytes 786440 | tf_op jit(solution)/shard_map/ppermute | solution.py:71
  76.8 27.4 %copy-start.4 = (bf16[1,512]{1,0:T(2,128)(2,1)S(1)}, bf16[1,512]{1,0:T(2,128)(2,1)}, u32[]{:S(2)}) copy-start(bf16[1,512]{1,0:T(2,128)(2,1)} %param.9) | copy-start | bytes 3076
  76.8 27.4 %copy-start.3 = (bf16[1,512,512]{2,1,0:T(8,128)(2,1)S(1)}, bf16[1,512,512]{2,1,0:T(8,128)(2,1)}, u32[]{:S(2)}) copy-start(bf16[1,512,512]{2,1,0:T(8,128)(2,1)} %param.8) | copy-start | bytes 1572868
  76.8 46.7 %copy-start.2 = (bf16[1,512,512]{2,1,0:T(8,128)(2,1)S(1)}, bf16[1,512,512]{2,1,0:T(8,128)(2,1)}, u32[]{:S(2)}) copy-start(bf16[1,512,512]{2,1,0:T(8,128)(2,1)} %param.10) | copy-start | bytes 1572868
  76.8 46.6 %copy-start.5 = (f32[512]{0:T(512)S(1)}, f32[512]{0:T(512)}, u32[]{:S(2)}) copy-start(f32[512]{0:T(512)} %param.13) | copy-start | bytes 6148
  79.8 26.5 %all-to-all-start.1 = ((bf16[1,16,32,512]{3,2,0,1:T(8,128)(2,1)}), bf16[1,16,32,512]{3,2,0,1:T(8,128)(2,1)S(1)}, u32[]{:S(2)}, u32[]{:S(2)}) async-start(bf16[1,16,32,512]{3,2,0,1:T(8,128)(2,1)} %bitcast.20), calls=%async_computation.1 | async-start | bytes 1048576 | tf_op jit(solution)/shard_map/all_to_all | solution.py:51
  107.1 31.6 %all-to-all-start.2 = ((f32[128,1,512]{2,1,0:T(1,128)}), f32[128,1,512]{2,1,0:T(1,128)S(1)}, u32[]{:S(2)}, u32[]{:S(2)}) async-start(f32[128,1,512]{2,1,0:T(1,128)} %broadcast_in_dim.7), calls=%async_computation.2 | async-start | bytes 524288 | tf_op jit(solution)/shard_map/all_to_all | solution.py:93

commit v4 on v3

--- a/solution.py
+++ b/solution.py
@@ -19,11 +19,18 @@
     cap = tok // nseq
     scale = 1.0 / math.sqrt(model)
 
-    rightward = [(i, (i + 1) % nten) for i in range(nten)]
-    leftward = [(i, (i - 1) % nten) for i in range(nten)]
+    flip = 1 - 2 * (here % 2)
+
+    def turn(block, way):
+        pairs = [
+            (s * nten + i, s * nten + (i + (way if s % 2 == 0 else -way)) % nten)
+            for s in range(nseq)
+            for i in range(nten)
+        ]
+        return lax.ppermute(block, ("seq", "tensor"), pairs)
 
     def times(block, step):
-        start = (column + step) % nten * width
+        start = (column + step * flip) % nten * width
         weight = lax.dynamic_slice(out_weight, (0, start), (heads_width, width))
         return lax.dot_general(
             block, weight, (((1,), (1,)), ((), ())), preferred_element_type=jnp.float32
@@ -38,8 +45,8 @@
     slot_table = (
         jnp.arange(tok, dtype=jnp.int32)[None, :, None] == slot_ids[:, None, :]
     ).astype(jnp.bfloat16)
-    first = (here - offsets) % nseq
-    order_in = first[:, :, None] + nseq * jnp.arange(cap, dtype=jnp.int32)[None, None, :]
+    start = (here - offsets) % nseq
+    order_in = start[:, :, None] + nseq * jnp.arange(cap, dtype=jnp.int32)[None, None, :]
     valid = order_in < shard_counts[:, :, None]
     positions = jnp.where(valid, (offsets[:, :, None] + order_in) // nseq, -1).reshape(batch, tok)
     place_table = (
@@ -53,22 +60,22 @@
 
     own = cotangent.reshape(batch * tok, width)
     rows = batch * tok
-    from_left, from_right = own, own
+    first_in, second_in = own, own
     product = times(own, 0)
     for step in range(1, nten // 2):
-        from_left = lax.ppermute(from_left, "tensor", rightward)
-        from_right = lax.ppermute(from_right, "tensor", leftward)
+        first_in = turn(first_in, 1)
+        second_in = turn(second_in, -1)
         if step == 1:
-            attended, place_table, from_left, from_right, product = lax.optimization_barrier(
-                (attended, place_table, from_left, from_right, product)
+            attended, place_table, first_in = lax.optimization_barrier(
+                (attended, place_table, first_in)
             )
             att_slots = jnp.einsum(
                 "bks,bkw->bsw", place_table, attended, preferred_element_type=jnp.float32
             ).astype(jnp.bfloat16)
             att_in = exchange(att_slots)
-        product = product + times(from_left, -step) + times(from_right, step)
-    upper = lax.ppermute(from_left[: rows // 2], "tensor", rightward)
-    lower = lax.ppermute(from_right[rows // 2 :], "tensor", leftward)
+        product = product + times(first_in, -step) + times(second_in, step)
+    upper = turn(first_in[: rows // 2], 1)
+    lower = turn(second_in[rows // 2 :], -1)
     product = product + times(jnp.concatenate([upper, lower], axis=0), nten // 2)
     att_tok = jnp.einsum("bst,bsw->btw", slot_table, att_in, preferred_element_type=jnp.float32)
 

time: 140 us -> 136 us (0.971)
  starting transfers between devices: 73 us -> 68.2 us
  waiting for transfers between devices: 26.8 us -> 28.8 us
  matrix products: 13.5 us -> 12 us
    all_to_all x2, starting transfers between devices: 28.7 us -> 20.9 us  [exchange(): lax.all_to_all(parts, 'seq', split_axis=1, concat_axis=1, tiled=True)]
    ppermute x8, waiting for transfers between devices: 11.7 us -> 13.7 us  [turn(): return lax.ppermute(block, ('seq', 'tensor'), pairs)]
    all_to_all x1, starting transfers between devices: 16.4 us -> 18.2 us  [shards(): lax.all_to_all(sums, ('dp', 'seq'), 0, 0, tiled=True)]
  transfers between devices with their start and end apart: 11 -> 11, of which waited for: 5 -> 6; matrix products, arithmetic and copies ran while one was open for 13% -> 14% of each run, Pallas kernels for 0% -> 0%
where the time goes in v4:
time: 136 us; the launch traced here: 135 us
  starting transfers between devices  68.2 us (50%)
  waiting for transfers between devices  28.8 us (21%)
  blocking collectives  15.3 us (11%)
  matrix products  12 us (9%)
  other arithmetic  7.4 us (5%)
  local copies, waits for them, and re-layouts  2.34 us (2%)
    ppermute x8, starting transfers between devices, turn(): return lax.ppermute(block, ('seq', 'tensor'), pairs)  29.1 us
    all_to_all x2, starting transfers between devices, exchange(): lax.all_to_all(parts, 'seq', split_axis=1, concat_axis=1, tiled=True)  20.9 us
    all_to_all x1, starting transfers between devices, shards(): lax.all_to_all(sums, ('dp', 'seq'), 0, 0, tiled=True)  18.2 us
    psum x1, blocking collectives, shards(): dots = lax.psum(partial_dots, 'tensor')  15.3 us
    ppermute x8, waiting for transfers between devices, turn(): return lax.ppermute(block, ('seq', 'tensor'), pairs)  13.7 us
    all_to_all x1, waiting for transfers between devices, shards(): lax.all_to_all(sums, ('dp', 'seq'), 0, 0, tiled=True)  13.2 us
    dot_general x8, matrix products, times(): lax.dot_general(block, weight, (((1,), (1,)), ((), ())), preferred_elemen...  8.11 us
  transfers between devices with their start and end apart: 11, of which 6 were waited for; matrix products, arithmetic and copies ran while one was open for 14% of the time, Pallas kernels for 0%

profile of v4, /device:TPU:1, one launch (start us, length us, event | category | flops | bytes accessed | tf_op | source)
XLA Modules:
  0.0 135.2 jit_solution(15586676752956770901)
XLA Ops:
  0.6 4.1 %collective-permute-start.1 = (bf16[512,512]{1,0:T(8,128)(2,1)}, bf16[512,512]{1,0:T(8,128)(2,1)S(1)}, u32[]{:S(2)}, u32[]{:S(2)}) collective-permute-start(bf16[512,512]{1,0:T(8,128)(2,1)} %bitcast.65), channel_id=1, source_target_pairs={{0,7},{1,0},{2,1},{3,2},{4,3},{5,4},{6,5},{7,6},{8,9},{9,10},{10,1... | collective-permute-start | bytes 1572872 | tf_op jit(solution)/shard_map/ppermute | solution.py:30
  4.7 3.3 %collective-permute-start = (bf16[512,512]{1,0:T(8,128)(2,1)}, bf16[512,512]{1,0:T(8,128)(2,1)S(1)}, u32[]{:S(2)}, u32[]{:S(2)}) collective-permute-start(bf16[512,512]{1,0:T(8,128)(2,1)} %bitcast.66), channel_id=1, source_target_pairs={{0,1},{1,2},{2,3},{3,4},{4,5},{5,6},{6,7},{7,0},{8,15},{9,8},{10,9... | collective-permute-start | bytes 1572872 | tf_op jit(solution)/shard_map/ppermute | solution.py:30
  8.1 0.8 reduce_window_sum.32
  8.9 1.3 fusion.44
  11.5 1.0 reduce-window.6
  12.9 1.4 %compare_select_fusion.2 = s32[1,512]{1,0:T(1,128)S(1)} fusion(s32[1,512]{1,0:T(1,128)} %param.14, s32[1,512]{1,0:T(1,128)S(1)} %bitcast.71, s32[1,512]{1,0:T(1,128)S(1)} %bitcast.75, s32[]{:T(128)} %get-tuple-element.19), kind=kLoop, calls=%fused_computation.49 | loop fusion | flops 16896 | bytes 8196 | tf_op jit(solution)/shard_map/jit(_where)/select_n | solution.py:44
  15.1 1.7 %convolution_bitcast_fusion.3 = f32[512,512]{0,1:T(8,128)S(1)} fusion(bf16[512,4096]{1,0:T(8,128)(2,1)} %param.12, s32[]{:T(128)S(6)} %select_n.136, bf16[1,512,512]{2,1,0:T(8,128)(2,1)} %param.10), kind=kOutput, calls=%fused_computation.11 | convolution fusion | flops 268435456 | bytes 2097156 | tf_op jit(solution)/shard_map/dot_general | solution.py:35
  16.8 6.2 %collective-permute-start.2 = (bf16[512,512]{1,0:T(8,128)(2,1)S(1)}, bf16[512,512]{1,0:T(8,128)(2,1)}, u32[]{:S(2)}, u32[]{:S(2)}) collective-permute-start(bf16[512,512]{1,0:T(8,128)(2,1)S(1)} %collective-permute-done), channel_id=1, source_target_pairs={{0,1},{1,2},{2,3},{3,4},{4,5},{5,6},{6,7},{7,0},{8,15},{9,8},{10,9... | collective-permute-start | bytes 1572872 | tf_op jit(solution)/shard_map/ppermute | solution.py:30
  23.0 1.1 convolution_convert_fusion.1
  24.1 12.4 %all-to-all-start = ((bf16[1,16,32,512]{3,2,0,1:T(8,128)(2,1)}), bf16[1,16,32,512]{3,2,0,1:T(8,128)(2,1)S(1)}, u32[]{:S(2)}, u32[]{:S(2)}) async-start(bf16[1,16,32,512]{3,2,0,1:T(8,128)(2,1)} %bitcast.19), calls=%async_computation | async-start | bytes 1048576 | tf_op jit(solution)/shard_map/all_to_all | solution.py:58
  36.6 2.2 %collective-permute-start.3 = (bf16[512,512]{1,0:T(8,128)(2,1)S(1)}, bf16[512,512]{1,0:T(8,128)(2,1)S(1)}, u32[]{:S(2)}, u32[]{:S(2)}) collective-permute-start(bf16[512,512]{1,0:T(8,128)(2,1)S(1)} %collective-permute-done.1), channel_id=1, source_target_pairs={{0,7},{1,0},{2,1},{3,2},{4,3},{5,4},{6,5},{7,6},{8,9},{9,10},{10,1... | collective-permute-start | bytes 1572872 | tf_op jit(solution)/shard_map/ppermute | solution.py:30
  38.8 1.5 %convolution_bitcast_fusion.2 = f32[512,512]{0,1:T(8,128)S(1)} fusion(bf16[512,512]{1,0:T(8,128)(2,1)S(1)} %collective-permute-done.1, bf16[512,4096]{1,0:T(8,128)(2,1)} %param.12, s32[]{:T(128)S(6)} %select_n.141), kind=kOutput, calls=%fused_computation.8 | convolution fusion | flops 268435456 | bytes 2097156 | tf_op jit(solution)/shard_map/dot_general | solution.py:35
  40.3 1.5 %fusion.3 = f32[512,512]{0,1:T(8,128)S(1)} fusion(f32[512,512]{0,1:T(8,128)S(1)} %convolution_bitcast_fusion.2, f32[512,512]{0,1:T(8,128)S(1)} %convolution_bitcast_fusion.3, bf16[512,512]{1,0:T(8,128)(2,1)S(1)} %collective-permute-done, bf16[512,4096]{1,0:T(8,128)(2,1)} %param.12, s32[]{:T(128)S(6)} %select_n.139), kind=kOutput, calls=%fused_computation.10 | convolution fusion | flops 268959744 | bytes 4194308 | tf_op jit(solution)/shard_map/dot_general | solution.py:35
  41.8 4.6 %collective-permute-start.4 = (bf16[512,512]{1,0:T(8,128)(2,1)}, bf16[512,512]{1,0:T(8,128)(2,1)S(1)}, u32[]{:S(2)}, u32[]{:S(2)}) collective-permute-start(bf16[512,512]{1,0:T(8,128)(2,1)} %collective-permute-done.2), channel_id=1, source_target_pairs={{0,1},{1,2},{2,3},{3,4},{4,5},{5,6},{6,7},{7,0},{8,15},{9,8},{10,9... | collective-permute-start | bytes 1572872 | tf_op jit(solution)/shard_map/ppermute | solution.py:30
  46.4 1.9 %collective-permute-done.3 = bf16[512,512]{1,0:T(8,128)(2,1)S(1)} collective-permute-done((bf16[512,512]{1,0:T(8,128)(2,1)S(1)}, bf16[512,512]{1,0:T(8,128)(2,1)S(1)}, u32[]{:S(2)}, u32[]{:S(2)}) %collective-permute-start.3) | collective-permute-done | bytes 524320 | tf_op jit(solution)/shard_map/ppermute | solution.py:30
  48.3 1.9 %collective-permute-start.5 = (bf16[512,512]{1,0:T(8,128)(2,1)S(1)}, bf16[512,512]{1,0:T(8,128)(2,1)S(1)}, u32[]{:S(2)}, u32[]{:S(2)}) collective-permute-start(bf16[512,512]{1,0:T(8,128)(2,1)S(1)} %collective-permute-done.3), channel_id=1, source_target_pairs={{0,7},{1,0},{2,1},{3,2},{4,3},{5,4},{6,5},{7,6},{8,9},{9,10},{10,1... | collective-permute-start | bytes 1572872 | tf_op jit(solution)/shard_map/ppermute | solution.py:30
  50.2 1.5 %convolution_add_fusion.1 = f32[512,512]{0,1:T(8,128)S(1)} fusion(f32[512,512]{0,1:T(8,128)S(1)} %fusion.3, bf16[512,512]{1,0:T(8,128)(2,1)} %collective-permute-done.2, bf16[512,4096]{1,0:T(8,128)(2,1)S(1)} %copy-done.1, s32[]{:T(128)S(6)} %select_n.143), kind=kOutput, calls=%fused_computation.7 | convolution fusion | flops 268697600 | bytes 3145732 | tf_op jit(solution)/shard_map/dot_general | solution.py:35
  52.2 1.4 %collective-permute-done.4 = bf16[512,512]{1,0:T(8,128)(2,1)S(1)} collective-permute-done((bf16[512,512]{1,0:T(8,128)(2,1)}, bf16[512,512]{1,0:T(8,128)(2,1)S(1)}, u32[]{:S(2)}, u32[]{:S(2)}) %collective-permute-start.4) | collective-permute-done | bytes 524320 | tf_op jit(solution)/shard_map/ppermute | solution.py:30
  53.7 4.9 %collective-permute-start.6 = (bf16[256,512]{1,0:T(8,128)(2,1)S(1)}, bf16[256,512]{1,0:T(8,128)(2,1)S(1)}, u32[]{:S(2)}, u32[]{:S(2)}) collective-permute-start(bf16[256,512]{1,0:T(8,128)(2,1)S(1)} %slice.16), channel_id=1, source_target_pairs={{0,1},{1,2},{2,3},{3,4},{4,5},{5,6},{6,7},{7,0},{8,15},{9,8},{10,9... | collective-permute-start | bytes 786440 | tf_op jit(solution)/shard_map/ppermute | solution.py:30
  58.6 3.5 %collective-permute-done.5 = bf16[512,512]{1,0:T(8,128)(2,1)S(1)} collective-permute-done((bf16[512,512]{1,0:T(8,128)(2,1)S(1)}, bf16[512,512]{1,0:T(8,128)(2,1)S(1)}, u32[]{:S(2)}, u32[]{:S(2)}) %collective-permute-start.5) | collective-permute-done | bytes 524320 | tf_op jit(solution)/shard_map/ppermute | solution.py:30
  62.1 1.9 %collective-permute-start.7 = (bf16[256,512]{1,0:T(8,128)(2,1)S(1)}, bf16[256,512]{1,0:T(8,128)(2,1)S(1)}, u32[]{:S(2)}, u32[]{:S(2)}) collective-permute-start(bf16[256,512]{1,0:T(8,128)(2,1)S(1)} %slice.17), channel_id=1, source_target_pairs={{0,7},{1,0},{2,1},{3,2},{4,3},{5,4},{6,5},{7,6},{8,9},{9,10},{10,1... | collective-permute-start | bytes 786440 | tf_op jit(solution)/shard_map/ppermute | solution.py:30
  64.5 6.9 %collective-permute-done.7 = bf16[256,512]{1,0:T(8,128)(2,1)S(1)} collective-permute-done((bf16[256,512]{1,0:T(8,128)(2,1)S(1)}, bf16[256,512]{1,0:T(8,128)(2,1)S(1)}, u32[]{:S(2)}, u32[]{:S(2)}) %collective-permute-start.7) | collective-permute-done | bytes 262176 | tf_op jit(solution)/shard_map/ppermute | solution.py:30
  73.0 1.3 fusion.5
  74.3 8.5 %all-to-all-start.1 = ((bf16[1,16,32,512]{3,2,0,1:T(8,128)(2,1)}), bf16[1,16,32,512]{3,2,0,1:T(8,128)(2,1)S(1)}, u32[]{:S(2)}, u32[]{:S(2)}) async-start(bf16[1,16,32,512]{3,2,0,1:T(8,128)(2,1)} %bitcast.23), calls=%async_computation.1 | async-start | bytes 1048576 | tf_op jit(solution)/shard_map/all_to_all | solution.py:58
  82.8 15.3 %psum.7 = f32[1,512]{1,0:T(1,128)S(1)} all-reduce(f32[1,512]{1,0:T(1,128)S(1)} %bitcast.77), channel_id=1, replica_groups=mesh['dp'=8,'seq'=16,'tensor'=8] {'tensor'}, use_global_device_ids=true, to_apply=%region_5.6 | all-reduce | flops 512 | bytes 4096 | tf_op jit(solution)/shard_map/psum | solution.py:91
  98.3 1.8 %all-to-all-done.1 = bf16[1,16,32,512]{3,2,0,1:T(8,128)(2,1)S(1)} async-done(((bf16[1,16,32,512]{3,2,0,1:T(8,128)(2,1)}), bf16[1,16,32,512]{3,2,0,1:T(8,128)(2,1)S(1)}, u32[]{:S(2)}, u32[]{:S(2)}) %all-to-all-start.1) | async-done | bytes 524320 | tf_op jit(solution)/shard_map/all_to_all | solution.py:58
  100.1 0.8 broadcast_in_dim.7
  100.9 18.2 %all-to-all-start.2 = ((f32[128,1,512]{2,1,0:T(1,128)}), f32[128,1,512]{2,1,0:T(1,128)S(1)}, u32[]{:S(2)}, u32[]{:S(2)}) async-start(f32[128,1,512]{2,1,0:T(1,128)} %broadcast_in_dim.7), calls=%async_computation.2 | async-start | bytes 524288 | tf_op jit(solution)/shard_map/all_to_all | solution.py:100
  119.2 1.0 add_convert_fusion
  120.2 1.0 fusion.6
  121.2 13.2 %all-to-all-done.2 = f32[128,1,512]{2,1,0:T(1,128)S(1)} async-done(((f32[128,1,512]{2,1,0:T(1,128)}), f32[128,1,512]{2,1,0:T(1,128)S(1)}, u32[]{:S(2)}, u32[]{:S(2)}) %all-to-all-start.2) | async-done | bytes 262176 | tf_op jit(solution)/shard_map/all_to_all | solution.py:100
  134.4 0.8 reduce_sum.42
  (43 shorter events, 5.1 us)
Async XLA Ops:
  0.6 22.4 %copy-start = (bf16[1,256,512]{2,1,0:T(8,128)(2,1)S(1)}, bf16[1,256,512]{2,1,0:T(8,128)(2,1)}, u32[]{:S(2)}) copy-start(bf16[1,256,512]{2,1,0:T(8,128)(2,1)} %param.11) | copy-start | bytes 786436
  0.6 35.9 %collective-permute-start.1 = (bf16[512,512]{1,0:T(8,128)(2,1)}, bf16[512,512]{1,0:T(8,128)(2,1)S(1)}, u32[]{:S(2)}, u32[]{:S(2)}) collective-permute-start(bf16[512,512]{1,0:T(8,128)(2,1)} %bitcast.65), channel_id=1, source_target_pairs={{0,7},{1,0},{2,1},{3,2},{4,3},{5,4},{6,5},{7,6},{8,9},{9,10},{10,1... | collective-permute-start | bytes 1572872 | tf_op jit(solution)/shard_map/ppermute | solution.py:30
  4.7 12.1 %collective-permute-start = (bf16[512,512]{1,0:T(8,128)(2,1)}, bf16[512,512]{1,0:T(8,128)(2,1)S(1)}, u32[]{:S(2)}, u32[]{:S(2)}) collective-permute-start(bf16[512,512]{1,0:T(8,128)(2,1)} %bitcast.66), channel_id=1, source_target_pairs={{0,1},{1,2},{2,3},{3,4},{4,5},{5,6},{6,7},{7,0},{8,15},{9,8},{10,9... | collective-permute-start | bytes 1572872 | tf_op jit(solution)/shard_map/ppermute | solution.py:30
  16.8 25.0 %collective-permute-start.2 = (bf16[512,512]{1,0:T(8,128)(2,1)S(1)}, bf16[512,512]{1,0:T(8,128)(2,1)}, u32[]{:S(2)}, u32[]{:S(2)}) collective-permute-start(bf16[512,512]{1,0:T(8,128)(2,1)S(1)} %collective-permute-done), channel_id=1, source_target_pairs={{0,1},{1,2},{2,3},{3,4},{4,5},{5,6},{6,7},{7,0},{8,15},{9,8},{10,9... | collective-permute-start | bytes 1572872 | tf_op jit(solution)/shard_map/ppermute | solution.py:30
  24.1 48.3 %all-to-all-start = ((bf16[1,16,32,512]{3,2,0,1:T(8,128)(2,1)}), bf16[1,16,32,512]{3,2,0,1:T(8,128)(2,1)S(1)}, u32[]{:S(2)}, u32[]{:S(2)}) async-start(bf16[1,16,32,512]{3,2,0,1:T(8,128)(2,1)} %bitcast.19), calls=%async_computation | async-start | bytes 1048576 | tf_op jit(solution)/shard_map/all_to_all | solution.py:58
  36.6 13.6 %copy-start.1 = (bf16[512,4096]{1,0:T(8,128)(2,1)S(1)}, bf16[512,4096]{1,0:T(8,128)(2,1)}, u32[]{:S(2)}) copy-start(bf16[512,4096]{1,0:T(8,128)(2,1)} %param.12) | copy-start | bytes 12582916
  36.6 11.7 %collective-permute-start.3 = (bf16[512,512]{1,0:T(8,128)(2,1)S(1)}, bf16[512,512]{1,0:T(8,128)(2,1)S(1)}, u32[]{:S(2)}, u32[]{:S(2)}) collective-permute-start(bf16[512,512]{1,0:T(8,128)(2,1)S(1)} %collective-permute-done.1), channel_id=1, source_target_pairs={{0,7},{1,0},{2,1},{3,2},{4,3},{5,4},{6,5},{7,6},{8,9},{9,10},{10,1... | collective-permute-start | bytes 1572872 | tf_op jit(solution)/shard_map/ppermute | solution.py:30
  41.8 11.8 %collective-permute-start.4 = (bf16[512,512]{1,0:T(8,128)(2,1)}, bf16[512,512]{1,0:T(8,128)(2,1)S(1)}, u32[]{:S(2)}, u32[]{:S(2)}) collective-permute-start(bf16[512,512]{1,0:T(8,128)(2,1)} %collective-permute-done.2), channel_id=1, source_target_pairs={{0,1},{1,2},{2,3},{3,4},{4,5},{5,6},{6,7},{7,0},{8,15},{9,8},{10,9... | collective-permute-start | bytes 1572872 | tf_op jit(solution)/shard_map/ppermute | solution.py:30
  48.3 13.8 %collective-permute-start.5 = (bf16[512,512]{1,0:T(8,128)(2,1)S(1)}, bf16[512,512]{1,0:T(8,128)(2,1)S(1)}, u32[]{:S(2)}, u32[]{:S(2)}) collective-permute-start(bf16[512,512]{1,0:T(8,128)(2,1)S(1)} %collective-permute-done.3), channel_id=1, source_target_pairs={{0,7},{1,0},{2,1},{3,2},{4,3},{5,4},{6,5},{7,6},{8,9},{9,10},{10,1... | collective-permute-start | bytes 1572872 | tf_op jit(solution)/shard_map/ppermute | solution.py:30
  53.7 10.9 %collective-permute-start.6 = (bf16[256,512]{1,0:T(8,128)(2,1)S(1)}, bf16[256,512]{1,0:T(8,128)(2,1)S(1)}, u32[]{:S(2)}, u32[]{:S(2)}) collective-permute-start(bf16[256,512]{1,0:T(8,128)(2,1)S(1)} %slice.16), channel_id=1, source_target_pairs={{0,1},{1,2},{2,3},{3,4},{4,5},{5,6},{6,7},{7,0},{8,15},{9,8},{10,9... | collective-permute-start | bytes 786440 | tf_op jit(solution)/shard_map/ppermute | solution.py:30
  62.1 9.3 %collective-permute-start.7 = (bf16[256,512]{1,0:T(8,128)(2,1)S(1)}, bf16[256,512]{1,0:T(8,128)(2,1)S(1)}, u32[]{:S(2)}, u32[]{:S(2)}) collective-permute-start(bf16[256,512]{1,0:T(8,128)(2,1)S(1)} %slice.17), channel_id=1, source_target_pairs={{0,7},{1,0},{2,1},{3,2},{4,3},{5,4},{6,5},{7,6},{8,9},{9,10},{10,1... | collective-permute-start | bytes 786440 | tf_op jit(solution)/shard_map/ppermute | solution.py:30
  71.9 26.1 %copy-start.4 = (bf16[1,512]{1,0:T(2,128)(2,1)S(1)}, bf16[1,512]{1,0:T(2,128)(2,1)}, u32[]{:S(2)}) copy-start(bf16[1,512]{1,0:T(2,128)(2,1)} %param.9) | copy-start | bytes 3076
  71.9 26.1 %copy-start.3 = (bf16[1,512,512]{2,1,0:T(8,128)(2,1)S(1)}, bf16[1,512,512]{2,1,0:T(8,128)(2,1)}, u32[]{:S(2)}) copy-start(bf16[1,512,512]{2,1,0:T(8,128)(2,1)} %param.8) | copy-start | bytes 1572868
  71.9 47.2 %copy-start.2 = (bf16[1,512,512]{2,1,0:T(8,128)(2,1)S(1)}, bf16[1,512,512]{2,1,0:T(8,128)(2,1)}, u32[]{:S(2)}) copy-start(bf16[1,512,512]{2,1,0:T(8,128)(2,1)} %param.10) | copy-start | bytes 1572868
  71.9 47.2 %copy-start.5 = (f32[512]{0:T(512)S(1)}, f32[512]{0:T(512)}, u32[]{:S(2)}) copy-start(f32[512]{0:T(512)} %param.13) | copy-start | bytes 6148
  74.3 25.8 %all-to-all-start.1 = ((bf16[1,16,32,512]{3,2,0,1:T(8,128)(2,1)}), bf16[1,16,32,512]{3,2,0,1:T(8,128)(2,1)S(1)}, u32[]{:S(2)}, u32[]{:S(2)}) async-start(bf16[1,16,32,512]{3,2,0,1:T(8,128)(2,1)} %bitcast.23), calls=%async_computation.1 | async-start | bytes 1048576 | tf_op jit(solution)/shard_map/all_to_all | solution.py:58
  100.9 33.5 %all-to-all-start.2 = ((f32[128,1,512]{2,1,0:T(1,128)}), f32[128,1,512]{2,1,0:T(1,128)S(1)}, u32[]{:S(2)}, u32[]{:S(2)}) async-start(f32[128,1,512]{2,1,0:T(1,128)} %broadcast_in_dim.7), calls=%async_computation.2 | async-start | bytes 524288 | tf_op jit(solution)/shard_map/all_to_all | solution.py:100

commit v5 on v4

v5 whole, which is shorter than its diff:
```python
import functools
import math

import jax
import jax.numpy as jnp
from jax import lax
from jax.experimental import pallas as pl
from jax.experimental.pallas import tpu as pltpu
from jax.sharding import PartitionSpec as P


VMEM = pl.BlockSpec(memory_space=pltpu.VMEM)
SMEM = pl.BlockSpec(memory_space=pltpu.SMEM)
PARAMS = pltpu.CompilerParams(vmem_limit_bytes=32 * 1024 * 1024)


def pack_kernel(here_ref, counts_ref, keep_ref, att_ref, slots_ref, ids_ref, places_ref):
    nseq = counts_ref.shape[1]
    tok = keep_ref.shape[1]
    kept_rows = att_ref.shape[0]
    cap = tok // nseq
    seq_bits, cap_bits = nseq.bit_length() - 1, cap.bit_length() - 1
    here = here_ref[0]
    lane = lax.broadcasted_iota(jnp.int32, (1, tok), 1)
    block = lane >> cap_bits
    offset, own_offset = jnp.int32(0), jnp.int32(0)
    offsets = jnp.zeros((1, tok), jnp.int32)
    counts = jnp.zeros((1, tok), jnp.int32)
    for j in range(nseq):
        count = counts_ref[0, j]
        offsets = jnp.where(block == j, offset, offsets)
        counts = jnp.where(block == j, count, counts)
        own_offset = own_offset + jnp.where(j < here, count, 0)
        offset = offset + count
    order_in = ((here - offsets) & (nseq - 1)) + nseq * (lane & (cap - 1))
    places = jnp.where(order_in < counts, (offsets + order_in) >> seq_bits, -1)
    places_ref[...] = places

    keep = keep_ref[...]
    flags = jnp.broadcast_to(keep.astype(jnp.float32), (16, tok)).astype(jnp.bfloat16)
    upto = lax.broadcasted_iota(jnp.int32, (tok, tok), 0) <= lax.broadcasted_iota(
        jnp.int32, (tok, tok), 1
    )
    upto = jnp.where(upto, 1.0, 0.0).astype(jnp.bfloat16)
    sums = jnp.dot(flags, upto, preferred_element_type=jnp.float32)
    local = sums[0:1].astype(jnp.int32) - 1
    ranks = own_offset + local
    slot = (ranks & (nseq - 1)) * cap + (local >> seq_bits)
    ids_ref[...] = jnp.where(keep == 1, slot, -1)

    table = lax.broadcasted_iota(jnp.int32, (kept_rows, tok), 0) == places
    table = jnp.where(table, 1.0, 0.0).astype(jnp.bfloat16)
    slots_ref[...] = lax.dot_general(
        table, att_ref[...], (((0,), (0,)), ((), ())), preferred_element_type=jnp.float32
    ).astype(jnp.bfloat16)


def finish_kernel(att_ref, ids_ref, rate_ref, back_ref, slots_ref, dots_ref):
    tok = ids_ref.shape[1]
    table = lax.broadcasted_iota(jnp.int32, (tok, tok), 0) == ids_ref[...]
    table = jnp.where(table, 1.0, 0.0).astype(jnp.bfloat16)
    att_tok = lax.dot_general(
        table, att_ref[...], (((0,), (0,)), ((), ())), preferred_element_type=jnp.float32
    )
    back = back_ref[...]
    column = jnp.sum(att_tok * back, axis=1, keepdims=True)
    dots_ref[...] = jnp.broadcast_to(column, (tok, 128)).T[0:1]
    rate = jnp.broadcast_to(rate_ref[...], (128, tok)).T[:, 0:1]
    grad = (rate * back).astype(jnp.bfloat16)
    slots_ref[...] = jnp.dot(table, grad, preferred_element_type=jnp.float32).astype(jnp.bfloat16)


def router_kernel(scale, dots_ref, rate_ref, inputs_ref, copies_ref, grad_ref):
    rate = rate_ref[...]
    grad = rate * (1.0 - rate) * dots_ref[...]
    grad_ref[...] = grad
    high = grad.astype(jnp.bfloat16).astype(jnp.float32)
    middle = (grad - high).astype(jnp.bfloat16).astype(jnp.float32)
    low = grad - high - middle
    row = lax.broadcasted_iota(jnp.int32, (16, grad.shape[1]), 0)
    parts = jnp.where(row == 0, high, jnp.where(row == 1, middle, jnp.where(row == 2, low, 0.0)))
    sums = jnp.dot(
        parts.astype(jnp.bfloat16), inputs_ref[...], preferred_element_type=jnp.float32
    )
    total = scale * jnp.sum(sums, axis=0, keepdims=True)
    copies_ref[...] = jnp.broadcast_to(total[None], copies_ref.shape)


def shards(
    inputs, logits, cotangent, attended, out_weight, router_weight, keep_route, shard_counts
):
    nseq = lax.axis_size("seq")
    here = lax.axis_index("seq")
    nten = lax.axis_size("tensor")
    column = lax.axis_index("tensor")
    batch, tok, width = cotangent.shape
    kept_rows = attended.shape[1]
    heads_width, model = out_weight.shape
    cap = tok // nseq
    scale = 1.0 / math.sqrt(model)

    flip = 1 - 2 * (here % 2)

    def turn(block, way):
        pairs = [
            (s * nten + i, s * nten + (i + (way if s % 2 == 0 else -way)) % nten)
            for s in range(nseq)
            for i in range(nten)
        ]
        return lax.ppermute(block, ("seq", "tensor"), pairs)

    def times(block, step):
        start = (column + step * flip) % nten * width
        weight = lax.dynamic_slice(out_weight, (0, start), (heads_width, width))
        return lax.dot_general(
            block, weight, (((1,), (1,)), ((), ())), preferred_element_type=jnp.float32
        )

    slots_shape = jax.ShapeDtypeStruct((tok, heads_width), jnp.bfloat16)
    row_shape = jax.ShapeDtypeStruct((1, tok), jnp.int32)
    att_slots, slot_ids, places = pl.pallas_call(
        pack_kernel,
        out_shape=(slots_shape, row_shape, row_shape),
        in_specs=[SMEM, SMEM, VMEM, VMEM],
        out_specs=(VMEM, VMEM, VMEM),
        compiler_params=PARAMS,
        cost_estimate=pl.CostEstimate(
            flops=2 * tok * kept_rows * heads_width, bytes_accessed=2**20, transcendentals=0
        ),
    )(here.reshape(1), shard_counts, keep_route, attended[0])

    def exchange(slots):
        parts = slots.reshape(nseq, cap, slots.shape[1])
        moved = lax.all_to_all(parts, "seq", split_axis=0, concat_axis=0, tiled=True)
        return moved.reshape(tok, slots.shape[1])

    att_in = exchange(att_slots)

    own = cotangent[0]
    first_in, second_in = own, own
    product = None
    for step in range(1, nten // 2):
        first_in = turn(first_in, 1)
        second_in = turn(second_in, -1)
        if step == 1:
            own, first_in = lax.optimization_barrier((own, first_in))
            product = times(own, 0)
        product = product + times(first_in, -step) + times(second_in, step)
    upper = turn(first_in[: tok // 2], 1)
    lower = turn(second_in[tok // 2 :], -1)
    product = product + times(jnp.concatenate([upper, lower], axis=0), nten // 2)

    rate = jax.nn.sigmoid(logits.astype(jnp.float32))
    grad_slots, partial_dots = pl.pallas_call(
        finish_kernel,
        out_shape=(slots_shape, jax.ShapeDtypeStruct((1, tok), jnp.float32)),
        in_specs=[VMEM] * 4,
        out_specs=(VMEM, VMEM),
        compiler_params=PARAMS,
        cost_estimate=pl.CostEstimate(
            flops=4 * tok * tok * heads_width, bytes_accessed=2**21, transcendentals=0
        ),
    )(att_in, slot_ids, rate, product)
    grad_in = exchange(grad_slots)
    dots = lax.psum(partial_dots, "tensor")
    group = lax.axis_size("dp") * nseq
    copies, logit_grad = pl.pallas_call(
        functools.partial(router_kernel, scale),
        out_shape=(
            jax.ShapeDtypeStruct((group, 1, width), jnp.float32),
            jax.ShapeDtypeStruct((1, tok), jnp.float32),
        ),
        in_specs=[VMEM] * 3,
        out_specs=(VMEM, VMEM),
        compiler_params=PARAMS,
        cost_estimate=pl.CostEstimate(
            flops=32 * tok * width, bytes_accessed=2**20, transcendentals=0
        ),
    )(dots, rate, inputs[0])
    grad_in, copies = lax.optimization_barrier((grad_in, copies))

    router_grad = jnp.sum(lax.all_to_all(copies, ("dp", "seq"), 0, 0, tiled=True), axis=(0, 1))
    in_grad = (
        cotangent.astype(jnp.float32)
        + scale * logit_grad[:, :, None] * router_weight[None, None, :]
    ).astype(jnp.bfloat16)
    place_table = (
        jnp.arange(kept_rows, dtype=jnp.int32)[:, None] == places
    ).astype(jnp.bfloat16)
    att_grad = jnp.dot(place_table, grad_in, preferred_element_type=jnp.float32)
    att_grad = att_grad.astype(jnp.bfloat16)[None]
    return (att_grad, in_grad, router_grad)


def solution(mesh):
    in_specs = (
        P("dp", "seq", "tensor"),
        P("dp", "seq"),
        P("dp", "seq", "tensor"),
        P("dp", "seq", "tensor"),
        P("tensor", None),
        P("tensor"),
        P("dp", "seq"),
        P("dp", None),
    )
    out_specs = (P("dp", "seq", "tensor"), P("dp", "seq", "tensor"), P("tensor"))
    return jax.shard_map(shards, mesh=mesh, in_specs=in_specs, out_specs=out_specs, check_vma=False)
```

time: 136 us -> 134 us (0.985)
  waiting for transfers between devices: 28.8 us -> 38.1 us
  matrix products: 12 us -> 6.92 us
  other arithmetic: 7.4 us -> 2.62 us
  starting transfers between devices: 68.2 us -> 63.6 us
  Pallas kernels: 0 us -> 4.19 us
    ppermute x8, waiting for transfers between devices: 13.7 us -> 22.8 us  [turn(): return lax.ppermute(block, ('seq', 'tensor'), pairs)]
    ppermute x8, starting transfers between devices: 29.1 us -> 23 us  [turn(): return lax.ppermute(block, ('seq', 'tensor'), pairs)]
    pallas_call x0 -> x3, Pallas kernels: none -> 4.19 us  [the longest x1 1.68 us: shards(): pl.pallas_call(pack_kernel, out_shape=(slots_shape, row_shape, row_shape)...]
    dot_general x4 -> x1, matrix products: 3.93 us -> 1.02 us  [shards(): att_grad = jnp.dot(place_table, grad_in, preferred_element_type=jnp.float32)]
    select_n x3 -> x0, other arithmetic: 2.66 us -> none  [the longest x1 1.35 us: shards(): jnp.where(keep_route == 1, ranks % nseq * cap + local // nseq, -1)]
    unnamed x12 -> x14, local copies, waits for them, and re-layouts: 0.04 us -> 2.3 us
    dot_general x8, matrix products: 8.11 us -> 5.9 us  [times(): lax.dot_general(block, weight, (((1,), (1,)), ((), ())), preferred_elemen...]
    another operation x3 -> x0, other arithmetic: 2 us -> none
  transfers between devices with their start and end apart: 11 -> 11, of which waited for: 6 -> 7; matrix products, arithmetic and copies ran while one was open for 14% -> 7% of each run, Pallas kernels for 0% -> 2%
where the time goes in v5:
time: 134 us; the launch traced here: 133 us
  starting transfers between devices  63.6 us (47%)
  waiting for transfers between devices  38.1 us (28%)
  blocking collectives  14.4 us (11%)
  matrix products  6.92 us (5%)
  Pallas kernels  4.19 us (3%)
  other arithmetic  2.62 us (2%)
  local copies, waits for them, and re-layouts  2.33 us (2%)
    all_to_all x2, starting transfers between devices, exchange(): lax.all_to_all(parts, 'seq', split_axis=0, concat_axis=0, tiled=True)  24.4 us
    ppermute x8, starting transfers between devices, turn(): return lax.ppermute(block, ('seq', 'tensor'), pairs)  23 us
    ppermute x8, waiting for transfers between devices, turn(): return lax.ppermute(block, ('seq', 'tensor'), pairs)  22.8 us
    all_to_all x1, starting transfers between devices, shards(): lax.all_to_all(copies, ('dp', 'seq'), 0, 0, tiled=True)  16.2 us
    psum x1, blocking collectives, shards(): dots = lax.psum(partial_dots, 'tensor')  14.4 us
    all_to_all x1, waiting for transfers between devices, shards(): lax.all_to_all(copies, ('dp', 'seq'), 0, 0, tiled=True)  13.2 us
    dot_general x8, matrix products, times(): lax.dot_general(block, weight, (((1,), (1,)), ((), ())), preferred_elemen...  5.9 us
  transfers between devices with their start and end apart: 11, of which 7 were waited for; matrix products, arithmetic and copies ran while one was open for 7% of the time, Pallas kernels for 2%

profile of v5, /device:TPU:1, one launch (start us, length us, event | category | flops | bytes accessed | tf_op | source)
XLA Modules:
  0.0 133.0 jit_solution(7594756315544791090)
XLA Ops:
  0.6 5.3 %collective-permute-start = (bf16[512,512]{1,0:T(8,128)(2,1)}, bf16[512,512]{1,0:T(8,128)(2,1)S(1)}, u32[]{:S(2)}, u32[]{:S(2)}) collective-permute-start(bf16[512,512]{1,0:T(8,128)(2,1)} %bitcast.36), channel_id=1, source_target_pairs={{0,1},{1,2},{2,3},{3,4},{4,5},{5,6},{6,7},{7,0},{8,15},{9,8},{10,9... | collective-permute-start | bytes 1572872 | tf_op jit(solution)/shard_map/ppermute | solution.py:110
  6.0 1.9 %collective-permute-start.1 = (bf16[512,512]{1,0:T(8,128)(2,1)}, bf16[512,512]{1,0:T(8,128)(2,1)S(1)}, u32[]{:S(2)}, u32[]{:S(2)}) collective-permute-start(bf16[512,512]{1,0:T(8,128)(2,1)} %bitcast.37), channel_id=1, source_target_pairs={{0,7},{1,0},{2,1},{3,2},{4,3},{5,4},{6,5},{7,6},{8,9},{9,10},{10,1... | collective-permute-start | bytes 1572872 | tf_op jit(solution)/shard_map/ppermute | solution.py:110
  7.9 0.9 copy-done.1
  8.9 0.7 copy-done.2
  9.5 0.7 copy-done.3
  10.2 1.7 %shard_map.103 = (bf16[512,512]{1,0:T(8,128)(2,1)}, s32[1,512]{1,0:T(1,128)S(1)}, s32[1,512]{1,0:T(1,128)S(1)}) custom-call(s32[1]{0:T(128)} %bitcast.here_ref, s32[1,16]{1,0:T(1,128)S(1)} %copy-done.3, s32[1,512]{1,0:T(1,128)S(1)} %copy-done.2, bf16[256,512]{1,0:T(8,128)(2,1)S(1)} %bitcast.35), custom_call_target="tpu_custom_call" | custom-call | flops 134217728 | bytes 1048576 | tf_op jit(solution)/shard_map/pallas_call | solution.py:121
  11.9 17.3 %all-to-all-start = ((bf16[16,32,512]{2,1,0:T(8,128)(2,1)}), bf16[16,32,512]{2,1,0:T(8,128)(2,1)S(1)}, u32[]{:S(2)}, u32[]{:S(2)}) async-start(bf16[16,32,512]{2,1,0:T(8,128)(2,1)} %bitcast.3), calls=%async_computation | async-start | bytes 1048576 | tf_op jit(solution)/shard_map/all_to_all | solution.py:134
  29.2 0.8 add_divide_fusion.rate_ref
  30.1 2.1 %collective-permute-start.2 = (bf16[512,512]{1,0:T(8,128)(2,1)S(1)}, bf16[512,512]{1,0:T(8,128)(2,1)S(1)}, u32[]{:S(2)}, u32[]{:S(2)}) collective-permute-start(bf16[512,512]{1,0:T(8,128)(2,1)S(1)} %collective-permute-done), channel_id=1, source_target_pairs={{0,1},{1,2},{2,3},{3,4},{4,5},{5,6},{6,7},{7,0},{8,15},{9,8},{10,9... | collective-permute-start | bytes 1572872 | tf_op jit(solution)/shard_map/ppermute | solution.py:110
  32.1 1.5 %fusion.15 = f32[512,512]{1,0:T(8,128)S(1)} fusion(bf16[512,512]{1,0:T(8,128)(2,1)S(1)} %collective-permute-done, bf16[512,4096]{1,0:T(8,128)(2,1)} %param.12, s32[]{:T(128)S(6)} %select_n.67), kind=kOutput, calls=%fused_computation.23 | convolution fusion | flops 268435456 | bytes 2097156 | tf_op jit(solution)/shard_map/dot_general | solution.py:115
  33.6 3.4 %collective-permute-start.3 = (bf16[512,512]{1,0:T(8,128)(2,1)S(1)}, bf16[512,512]{1,0:T(8,128)(2,1)S(1)}, u32[]{:S(2)}, u32[]{:S(2)}) collective-permute-start(bf16[512,512]{1,0:T(8,128)(2,1)S(1)} %collective-permute-done.1), channel_id=1, source_target_pairs={{0,7},{1,0},{2,1},{3,2},{4,3},{5,4},{6,5},{7,6},{8,9},{9,10},{10,1... | collective-permute-start | bytes 1572872 | tf_op jit(solution)/shard_map/ppermute | solution.py:110
  37.0 1.5 %convolution_bitcast_fusion.2 = f32[512,512]{1,0:T(8,128)S(1)} fusion(bf16[512,512]{1,0:T(8,128)(2,1)S(1)} %collective-permute-done.1, bf16[512,4096]{1,0:T(8,128)(2,1)} %param.12, s32[]{:T(128)S(6)} %select_n.69), kind=kOutput, calls=%fused_computation.7 | convolution fusion | flops 268435456 | bytes 2097156 | tf_op jit(solution)/shard_map/dot_general | solution.py:115
  39.0 2.6 %collective-permute-done.2 = bf16[512,512]{1,0:T(8,128)(2,1)S(1)} collective-permute-done((bf16[512,512]{1,0:T(8,128)(2,1)S(1)}, bf16[512,512]{1,0:T(8,128)(2,1)S(1)}, u32[]{:S(2)}, u32[]{:S(2)}) %collective-permute-start.2) | collective-permute-done | bytes 524320 | tf_op jit(solution)/shard_map/ppermute | solution.py:110
  41.6 1.9 %collective-permute-start.4 = (bf16[512,512]{1,0:T(8,128)(2,1)S(1)}, bf16[512,512]{1,0:T(8,128)(2,1)S(1)}, u32[]{:S(2)}, u32[]{:S(2)}) collective-permute-start(bf16[512,512]{1,0:T(8,128)(2,1)S(1)} %collective-permute-done.2), channel_id=1, source_target_pairs={{0,1},{1,2},{2,3},{3,4},{4,5},{5,6},{6,7},{7,0},{8,15},{9,8},{10,9... | collective-permute-start | bytes 1572872 | tf_op jit(solution)/shard_map/ppermute | solution.py:110
  43.6 4.2 %collective-permute-done.3 = bf16[512,512]{1,0:T(8,128)(2,1)S(1)} collective-permute-done((bf16[512,512]{1,0:T(8,128)(2,1)S(1)}, bf16[512,512]{1,0:T(8,128)(2,1)S(1)}, u32[]{:S(2)}, u32[]{:S(2)}) %collective-permute-start.3) | collective-permute-done | bytes 524320 | tf_op jit(solution)/shard_map/ppermute | solution.py:110
  47.8 1.9 %collective-permute-start.5 = (bf16[512,512]{1,0:T(8,128)(2,1)S(1)}, bf16[512,512]{1,0:T(8,128)(2,1)S(1)}, u32[]{:S(2)}, u32[]{:S(2)}) collective-permute-start(bf16[512,512]{1,0:T(8,128)(2,1)S(1)} %collective-permute-done.3), channel_id=1, source_target_pairs={{0,7},{1,0},{2,1},{3,2},{4,3},{5,4},{6,5},{7,6},{8,9},{9,10},{10,1... | collective-permute-start | bytes 1572872 | tf_op jit(solution)/shard_map/ppermute | solution.py:110
  49.7 0.5 convolution_add_fusion.1
  50.7 0.8 collective-permute-done.4
  51.6 4.6 %collective-permute-start.6 = (bf16[256,512]{1,0:T(8,128)(2,1)S(1)}, bf16[256,512]{1,0:T(8,128)(2,1)S(1)}, u32[]{:S(2)}, u32[]{:S(2)}) collective-permute-start(bf16[256,512]{1,0:T(8,128)(2,1)S(1)} %slice.8), channel_id=1, source_target_pairs={{0,1},{1,2},{2,3},{3,4},{4,5},{5,6},{6,7},{7,0},{8,15},{9,8},{10,9... | collective-permute-start | bytes 786440 | tf_op jit(solution)/shard_map/ppermute | solution.py:110
  56.1 6.9 %collective-permute-done.5 = bf16[512,512]{1,0:T(8,128)(2,1)S(1)} collective-permute-done((bf16[512,512]{1,0:T(8,128)(2,1)S(1)}, bf16[512,512]{1,0:T(8,128)(2,1)S(1)}, u32[]{:S(2)}, u32[]{:S(2)}) %collective-permute-start.5) | collective-permute-done | bytes 524320 | tf_op jit(solution)/shard_map/ppermute | solution.py:110
  63.1 1.9 %collective-permute-start.7 = (bf16[256,512]{1,0:T(8,128)(2,1)S(1)}, bf16[256,512]{1,0:T(8,128)(2,1)S(1)}, u32[]{:S(2)}, u32[]{:S(2)}) collective-permute-start(bf16[256,512]{1,0:T(8,128)(2,1)S(1)} %slice.9), channel_id=1, source_target_pairs={{0,7},{1,0},{2,1},{3,2},{4,3},{5,4},{6,5},{7,6},{8,9},{9,10},{10,1... | collective-permute-start | bytes 786440 | tf_op jit(solution)/shard_map/ppermute | solution.py:110
  65.5 8.3 %collective-permute-done.7 = bf16[256,512]{1,0:T(8,128)(2,1)S(1)} collective-permute-done((bf16[256,512]{1,0:T(8,128)(2,1)S(1)}, bf16[256,512]{1,0:T(8,128)(2,1)S(1)}, u32[]{:S(2)}, u32[]{:S(2)}) %collective-permute-start.7) | collective-permute-done | bytes 262176 | tf_op jit(solution)/shard_map/ppermute | solution.py:110
  74.7 1.6 %shard_map.104 = (bf16[512,512]{1,0:T(8,128)(2,1)}, f32[1,512]{1,0:T(1,128)S(1)}) custom-call(bf16[512,512]{1,0:T(8,128)(2,1)S(1)} %bitcast.33, s32[1,512]{1,0:T(1,128)S(1)} %get-tuple-element.16.ids_ref, f32[1,512]{1,0:T(1,128)S(1)} %add_divide_fusion.rate_ref, f32[512,512]{1,0:T(8,128)S(1)} %fusion.1.back_ref), custom_call_target="tpu_custom_call" | custom-call | flops 536870912 | bytes 2097152 | tf_op jit(solution)/shard_map/pallas_call | solution.py:154
  76.3 7.1 %all-to-all-start.1 = ((bf16[16,32,512]{2,1,0:T(8,128)(2,1)}), bf16[16,32,512]{2,1,0:T(8,128)(2,1)S(1)}, u32[]{:S(2)}, u32[]{:S(2)}) async-start(bf16[16,32,512]{2,1,0:T(8,128)(2,1)} %bitcast.9), calls=%async_computation.1 | async-start | bytes 1048576 | tf_op jit(solution)/shard_map/all_to_all | solution.py:134
  83.4 14.4 %psum.7.dots_ref = f32[1,512]{1,0:T(1,128)S(1)} all-reduce(f32[1,512]{1,0:T(1,128)S(1)} %get-tuple-element.20), channel_id=1, replica_groups=mesh['dp'=8,'seq'=16,'tensor'=8] {'tensor'}, use_global_device_ids=true, to_apply=%region_0.1 | all-reduce | flops 512 | bytes 4096 | tf_op jit(solution)/shard_map/psum | solution.py:165
  97.8 0.9 shard_map.105
  98.7 2.0 %all-to-all-done.1 = bf16[16,32,512]{2,1,0:T(8,128)(2,1)S(1)} async-done(((bf16[16,32,512]{2,1,0:T(8,128)(2,1)}), bf16[16,32,512]{2,1,0:T(8,128)(2,1)S(1)}, u32[]{:S(2)}, u32[]{:S(2)}) %all-to-all-start.1) | async-done | bytes 524320 | tf_op jit(solution)/shard_map/all_to_all | solution.py:134
  100.7 16.2 %all-to-all-start.2 = ((f32[128,1,512]{2,1,0:T(1,128)}), f32[128,1,512]{2,1,0:T(1,128)S(1)}, u32[]{:S(2)}, u32[]{:S(2)}) async-start(f32[128,1,512]{2,1,0:T(1,128)} %get-tuple-element.24), calls=%async_computation.2 | async-start | bytes 524288 | tf_op jit(solution)/shard_map/all_to_all | solution.py:182
  117.0 1.0 add_convert_fusion
  117.9 1.0 fusion.4
  119.0 13.2 %all-to-all-done.2 = f32[128,1,512]{2,1,0:T(1,128)S(1)} async-done(((f32[128,1,512]{2,1,0:T(1,128)}), f32[128,1,512]{2,1,0:T(1,128)S(1)}, u32[]{:S(2)}, u32[]{:S(2)}) %all-to-all-start.2) | async-done | bytes 262176 | tf_op jit(solution)/shard_map/all_to_all | solution.py:182
  132.2 0.8 reduce_sum.9
  (23 shorter events, 2.5 us)
Async XLA Ops:
  0.6 29.4 %collective-permute-start = (bf16[512,512]{1,0:T(8,128)(2,1)}, bf16[512,512]{1,0:T(8,128)(2,1)S(1)}, u32[]{:S(2)}, u32[]{:S(2)}) collective-permute-start(bf16[512,512]{1,0:T(8,128)(2,1)} %bitcast.36), channel_id=1, source_target_pairs={{0,1},{1,2},{2,3},{3,4},{4,5},{5,6},{6,7},{7,0},{8,15},{9,8},{10,9... | collective-permute-start | bytes 1572872 | tf_op jit(solution)/shard_map/ppermute | solution.py:110
  6.0 27.7 %collective-permute-start.1 = (bf16[512,512]{1,0:T(8,128)(2,1)}, bf16[512,512]{1,0:T(8,128)(2,1)S(1)}, u32[]{:S(2)}, u32[]{:S(2)}) collective-permute-start(bf16[512,512]{1,0:T(8,128)(2,1)} %bitcast.37), channel_id=1, source_target_pairs={{0,7},{1,0},{2,1},{3,2},{4,3},{5,4},{6,5},{7,6},{8,9},{9,10},{10,1... | collective-permute-start | bytes 1572872 | tf_op jit(solution)/shard_map/ppermute | solution.py:110
  7.9 1.0 copy-start.1
  8.9 0.7 copy-start.2
  9.5 0.7 copy-start.3
  10.2 28.3 %copy-start.5 = (bf16[1,512,512]{2,1,0:T(8,128)(2,1)S(1)}, bf16[1,512,512]{2,1,0:T(8,128)(2,1)}, u32[]{:S(2)}) copy-start(bf16[1,512,512]{2,1,0:T(8,128)(2,1)} %param.10) | copy-start | bytes 1572868
  11.9 62.9 %all-to-all-start = ((bf16[16,32,512]{2,1,0:T(8,128)(2,1)}), bf16[16,32,512]{2,1,0:T(8,128)(2,1)S(1)}, u32[]{:S(2)}, u32[]{:S(2)}) async-start(bf16[16,32,512]{2,1,0:T(8,128)(2,1)} %bitcast.3), calls=%async_computation | async-start | bytes 1048576 | tf_op jit(solution)/shard_map/all_to_all | solution.py:134
  29.2 9.4 %copy-start.4 = (bf16[512,4096]{1,0:T(8,128)(2,1)S(1)}, bf16[512,4096]{1,0:T(8,128)(2,1)}, u32[]{:S(2)}) copy-start(bf16[512,4096]{1,0:T(8,128)(2,1)} %param.12) | copy-start | bytes 12582916
  30.1 11.6 %collective-permute-start.2 = (bf16[512,512]{1,0:T(8,128)(2,1)S(1)}, bf16[512,512]{1,0:T(8,128)(2,1)S(1)}, u32[]{:S(2)}, u32[]{:S(2)}) collective-permute-start(bf16[512,512]{1,0:T(8,128)(2,1)S(1)} %collective-permute-done), channel_id=1, source_target_pairs={{0,1},{1,2},{2,3},{3,4},{4,5},{5,6},{6,7},{7,0},{8,15},{9,8},{10,9... | collective-permute-start | bytes 1572872 | tf_op jit(solution)/shard_map/ppermute | solution.py:110
  33.6 14.2 %collective-permute-start.3 = (bf16[512,512]{1,0:T(8,128)(2,1)S(1)}, bf16[512,512]{1,0:T(8,128)(2,1)S(1)}, u32[]{:S(2)}, u32[]{:S(2)}) collective-permute-start(bf16[512,512]{1,0:T(8,128)(2,1)S(1)} %collective-permute-done.1), channel_id=1, source_target_pairs={{0,7},{1,0},{2,1},{3,2},{4,3},{5,4},{6,5},{7,6},{8,9},{9,10},{10,1... | collective-permute-start | bytes 1572872 | tf_op jit(solution)/shard_map/ppermute | solution.py:110
  41.6 9.9 %collective-permute-start.4 = (bf16[512,512]{1,0:T(8,128)(2,1)S(1)}, bf16[512,512]{1,0:T(8,128)(2,1)S(1)}, u32[]{:S(2)}, u32[]{:S(2)}) collective-permute-start(bf16[512,512]{1,0:T(8,128)(2,1)S(1)} %collective-permute-done.2), channel_id=1, source_target_pairs={{0,1},{1,2},{2,3},{3,4},{4,5},{5,6},{6,7},{7,0},{8,15},{9,8},{10,9... | collective-permute-start | bytes 1572872 | tf_op jit(solution)/shard_map/ppermute | solution.py:110
  47.8 15.2 %collective-permute-start.5 = (bf16[512,512]{1,0:T(8,128)(2,1)S(1)}, bf16[512,512]{1,0:T(8,128)(2,1)S(1)}, u32[]{:S(2)}, u32[]{:S(2)}) collective-permute-start(bf16[512,512]{1,0:T(8,128)(2,1)S(1)} %collective-permute-done.3), channel_id=1, source_target_pairs={{0,7},{1,0},{2,1},{3,2},{4,3},{5,4},{6,5},{7,6},{8,9},{9,10},{10,1... | collective-permute-start | bytes 1572872 | tf_op jit(solution)/shard_map/ppermute | solution.py:110
  51.6 13.9 %collective-permute-start.6 = (bf16[256,512]{1,0:T(8,128)(2,1)S(1)}, bf16[256,512]{1,0:T(8,128)(2,1)S(1)}, u32[]{:S(2)}, u32[]{:S(2)}) collective-permute-start(bf16[256,512]{1,0:T(8,128)(2,1)S(1)} %slice.8), channel_id=1, source_target_pairs={{0,1},{1,2},{2,3},{3,4},{4,5},{5,6},{6,7},{7,0},{8,15},{9,8},{10,9... | collective-permute-start | bytes 786440 | tf_op jit(solution)/shard_map/ppermute | solution.py:110
  63.1 10.7 %collective-permute-start.7 = (bf16[256,512]{1,0:T(8,128)(2,1)S(1)}, bf16[256,512]{1,0:T(8,128)(2,1)S(1)}, u32[]{:S(2)}, u32[]{:S(2)}) collective-permute-start(bf16[256,512]{1,0:T(8,128)(2,1)S(1)} %slice.9), channel_id=1, source_target_pairs={{0,7},{1,0},{2,1},{3,2},{4,3},{5,4},{6,5},{7,6},{8,9},{9,10},{10,1... | collective-permute-start | bytes 786440 | tf_op jit(solution)/shard_map/ppermute | solution.py:110
  65.5 32.3 %copy-start = (bf16[1,512,512]{2,1,0:T(8,128)(2,1)S(1)}, bf16[1,512,512]{2,1,0:T(8,128)(2,1)}, u32[]{:S(2)}) copy-start(bf16[1,512,512]{2,1,0:T(8,128)(2,1)} %param.8) | copy-start | bytes 1572868
  74.2 42.7 %copy-start.6 = (f32[512]{0:T(512)S(1)}, f32[512]{0:T(512)}, u32[]{:S(2)}) copy-start(f32[512]{0:T(512)} %param.13) | copy-start | bytes 6148
  76.3 24.4 %all-to-all-start.1 = ((bf16[16,32,512]{2,1,0:T(8,128)(2,1)}), bf16[16,32,512]{2,1,0:T(8,128)(2,1)S(1)}, u32[]{:S(2)}, u32[]{:S(2)}) async-start(bf16[16,32,512]{2,1,0:T(8,128)(2,1)} %bitcast.9), calls=%async_computation.1 | async-start | bytes 1048576 | tf_op jit(solution)/shard_map/all_to_all | solution.py:134
  100.7 31.5 %all-to-all-start.2 = ((f32[128,1,512]{2,1,0:T(1,128)}), f32[128,1,512]{2,1,0:T(1,128)S(1)}, u32[]{:S(2)}, u32[]{:S(2)}) async-start(f32[128,1,512]{2,1,0:T(1,128)} %get-tuple-element.24), calls=%async_computation.2 | async-start | bytes 524288 | tf_op jit(solution)/shard_map/all_to_all | solution.py:182

commit v6 on v5

--- a/solution.py
+++ b/solution.py
@@ -14,7 +14,11 @@
 PARAMS = pltpu.CompilerParams(vmem_limit_bytes=32 * 1024 * 1024)
 
 
-def pack_kernel(here_ref, counts_ref, keep_ref, att_ref, slots_ref, ids_ref, places_ref):
+def pack_kernel(
+    here_ref, counts_ref, keep_ref, att_any, slots_ref, ids_ref, places_ref, att_ref, att_sem
+):
+    fetch = pltpu.make_async_copy(att_any, att_ref, att_sem)
+    fetch.start()
     nseq = counts_ref.shape[1]
     tok = keep_ref.shape[1]
     kept_rows = att_ref.shape[0]
@@ -50,12 +54,17 @@
 
     table = lax.broadcasted_iota(jnp.int32, (kept_rows, tok), 0) == places
     table = jnp.where(table, 1.0, 0.0).astype(jnp.bfloat16)
+    fetch.wait()
     slots_ref[...] = lax.dot_general(
         table, att_ref[...], (((0,), (0,)), ((), ())), preferred_element_type=jnp.float32
     ).astype(jnp.bfloat16)
 
 
-def finish_kernel(att_ref, ids_ref, rate_ref, back_ref, slots_ref, dots_ref):
+def rate_of(logits_ref):
+    return jax.nn.sigmoid(logits_ref[...].astype(jnp.float32))
+
+
+def finish_kernel(att_ref, ids_ref, logits_ref, back_ref, slots_ref, dots_ref):
     tok = ids_ref.shape[1]
     table = lax.broadcasted_iota(jnp.int32, (tok, tok), 0) == ids_ref[...]
     table = jnp.where(table, 1.0, 0.0).astype(jnp.bfloat16)
@@ -65,13 +74,13 @@
     back = back_ref[...]
     column = jnp.sum(att_tok * back, axis=1, keepdims=True)
     dots_ref[...] = jnp.broadcast_to(column, (tok, 128)).T[0:1]
-    rate = jnp.broadcast_to(rate_ref[...], (128, tok)).T[:, 0:1]
+    rate = jnp.broadcast_to(rate_of(logits_ref), (128, tok)).T[:, 0:1]
     grad = (rate * back).astype(jnp.bfloat16)
     slots_ref[...] = jnp.dot(table, grad, preferred_element_type=jnp.float32).astype(jnp.bfloat16)
 
 
-def router_kernel(scale, dots_ref, rate_ref, inputs_ref, copies_ref, grad_ref):
-    rate = rate_ref[...]
+def router_kernel(scale, dots_ref, logits_ref, inputs_ref, copies_ref, grad_ref):
+    rate = rate_of(logits_ref)
     grad = rate * (1.0 - rate) * dots_ref[...]
     grad_ref[...] = grad
     high = grad.astype(jnp.bfloat16).astype(jnp.float32)
@@ -121,8 +130,12 @@
     att_slots, slot_ids, places = pl.pallas_call(
         pack_kernel,
         out_shape=(slots_shape, row_shape, row_shape),
-        in_specs=[SMEM, SMEM, VMEM, VMEM],
+        in_specs=[SMEM, SMEM, VMEM, pl.BlockSpec(memory_space=pl.ANY)],
         out_specs=(VMEM, VMEM, VMEM),
+        scratch_shapes=[
+            pltpu.VMEM((kept_rows, heads_width), jnp.bfloat16),
+            pltpu.SemaphoreType.DMA,
+        ],
         compiler_params=PARAMS,
         cost_estimate=pl.CostEstimate(
             flops=2 * tok * kept_rows * heads_width, bytes_accessed=2**20, transcendentals=0
@@ -138,19 +151,19 @@
 
     own = cotangent[0]
     first_in, second_in = own, own
-    product = None
+    blocks = [(own, 0)]
     for step in range(1, nten // 2):
         first_in = turn(first_in, 1)
         second_in = turn(second_in, -1)
-        if step == 1:
-            own, first_in = lax.optimization_barrier((own, first_in))
-            product = times(own, 0)
-        product = product + times(first_in, -step) + times(second_in, step)
-    upper = turn(first_in[: tok // 2], 1)
-    lower = turn(second_in[tok // 2 :], -1)
-    product = product + times(jnp.concatenate([upper, lower], axis=0), nten // 2)
-
-    rate = jax.nn.sigmoid(logits.astype(jnp.float32))
+        if step == 2:
+            waiting = tuple(block for block, _ in blocks)
+            waiting, second_in = lax.optimization_barrier((waiting, second_in))
+            blocks = [(block, way) for block, (_, way) in zip(waiting, blocks)]
+        blocks += [(first_in, -step), (second_in, step)]
+    product = sum(times(block, way) for block, way in blocks)
+    last_in = turn(first_in, 1)
+    product = product + times(last_in, nten // 2)
+
     grad_slots, partial_dots = pl.pallas_call(
         finish_kernel,
         out_shape=(slots_shape, jax.ShapeDtypeStruct((1, tok), jnp.float32)),
@@ -160,7 +173,7 @@
         cost_estimate=pl.CostEstimate(
             flops=4 * tok * tok * heads_width, bytes_accessed=2**21, transcendentals=0
         ),
-    )(att_in, slot_ids, rate, product)
+    )(att_in, slot_ids, logits, product)
     grad_in = exchange(grad_slots)
     dots = lax.psum(partial_dots, "tensor")
     group = lax.axis_size("dp") * nseq
@@ -176,7 +189,7 @@
         cost_estimate=pl.CostEstimate(
             flops=32 * tok * width, bytes_accessed=2**20, transcendentals=0
         ),
-    )(dots, rate, inputs[0])
+    )(dots, logits, inputs[0])
     grad_in, copies = lax.optimization_barrier((grad_in, copies))
 
     router_grad = jnp.sum(lax.all_to_all(copies, ("dp", "seq"), 0, 0, tiled=True), axis=(0, 1))

time: 134 us -> 142 us (1.060)
  starting transfers between devices: 63.6 us -> 74.5 us
  blocking collectives: 14.4 us -> 11.8 us
    all_to_all x2, starting transfers between devices: 24.4 us -> 32.7 us  [exchange(): lax.all_to_all(parts, 'seq', split_axis=0, concat_axis=0, tiled=True)]
    all_to_all x1, starting transfers between devices: 16.2 us -> 20.4 us  [shards(): lax.all_to_all(copies, ('dp', 'seq'), 0, 0, tiled=True)]
    psum x1, blocking collectives: 14.4 us -> 11.8 us  [shards(): dots = lax.psum(partial_dots, 'tensor')]
    all_to_all x2, waiting for transfers between devices: 2.02 us -> 4.53 us  [exchange(): lax.all_to_all(parts, 'seq', split_axis=0, concat_axis=0, tiled=True)]
    ppermute x8 -> x7, waiting for transfers between devices: 22.8 us -> 21.1 us  [turn(): return lax.ppermute(block, ('seq', 'tensor'), pairs)]
    ppermute x8 -> x7, starting transfers between devices: 23 us -> 21.4 us  [turn(): return lax.ppermute(block, ('seq', 'tensor'), pairs)]
  transfers between devices with their start and end apart: 11 -> 10, of which waited for: 7 -> 6; matrix products, arithmetic and copies ran while one was open for 7% -> 6% of each run, Pallas kernels for 2% -> 2%
where the time goes in v6:
time: 142 us
  starting transfers between devices  74.5 us (52%)
  waiting for transfers between devices  38.8 us (27%)
  blocking collectives  11.8 us (8%)
  matrix products  6.95 us (5%)
  Pallas kernels  4.41 us (3%)
  local copies, waits for them, and re-layouts  2.31 us (2%)
  other arithmetic  1.78 us (1%)
    all_to_all x2, starting transfers between devices, exchange(): lax.all_to_all(parts, 'seq', split_axis=0, concat_axis=0, tiled=True)  32.7 us
    ppermute x7, starting transfers between devices, turn(): return lax.ppermute(block, ('seq', 'tensor'), pairs)  21.4 us
    ppermute x7, waiting for transfers between devices, turn(): return lax.ppermute(block, ('seq', 'tensor'), pairs)  21.1 us
    all_to_all x1, starting transfers between devices, shards(): lax.all_to_all(copies, ('dp', 'seq'), 0, 0, tiled=True)  20.4 us
    all_to_all x1, waiting for transfers between devices, shards(): lax.all_to_all(copies, ('dp', 'seq'), 0, 0, tiled=True)  13.2 us
    psum x1, blocking collectives, shards(): dots = lax.psum(partial_dots, 'tensor')  11.8 us
    dot_general x8, matrix products, times(): lax.dot_general(block, weight, (((1,), (1,)), ((), ())), preferred_elemen...  5.94 us
    all_to_all x2, waiting for transfers between devices, exchange(): lax.all_to_all(parts, 'seq', split_axis=0, concat_axis=0, tiled=True)  4.53 us
  transfers between devices with their start and end apart: 10, of which 6 were waited for; matrix products, arithmetic and copies ran while one was open for 6% of the time, Pallas kernels for 2%

profile of v6, /device:TPU:1, one launch (start us, length us, event | category | flops | bytes accessed | tf_op | source)
XLA Modules:
  0.0 141.5 jit_solution(4632706467623814995)
XLA Ops:
  0.6 3.9 %collective-permute-start.1 = (bf16[512,512]{1,0:T(8,128)(2,1)}, bf16[512,512]{1,0:T(8,128)(2,1)S(1)}, u32[]{:S(2)}, u32[]{:S(2)}) collective-permute-start(bf16[512,512]{1,0:T(8,128)(2,1)} %bitcast.36), channel_id=1, source_target_pairs={{0,7},{1,0},{2,1},{3,2},{4,3},{5,4},{6,5},{7,6},{8,9},{9,10},{10,1... | collective-permute-start | bytes 1572872 | tf_op jit(solution)/shard_map/ppermute | solution.py:119
  4.6 3.3 %collective-permute-start = (bf16[512,512]{1,0:T(8,128)(2,1)}, bf16[512,512]{1,0:T(8,128)(2,1)S(1)}, u32[]{:S(2)}, u32[]{:S(2)}) collective-permute-start(bf16[512,512]{1,0:T(8,128)(2,1)} %bitcast.37), channel_id=1, source_target_pairs={{0,1},{1,2},{2,3},{3,4},{4,5},{5,6},{6,7},{7,0},{8,15},{9,8},{10,9... | collective-permute-start | bytes 1572872 | tf_op jit(solution)/shard_map/ppermute | solution.py:119
  7.9 4.8 %collective-permute-done.1 = bf16[512,512]{1,0:T(8,128)(2,1)S(1)} collective-permute-done((bf16[512,512]{1,0:T(8,128)(2,1)}, bf16[512,512]{1,0:T(8,128)(2,1)S(1)}, u32[]{:S(2)}, u32[]{:S(2)}) %collective-permute-start.1) | collective-permute-done | bytes 524320 | tf_op jit(solution)/shard_map/ppermute | solution.py:119
  12.7 3.6 %collective-permute-start.2 = (bf16[512,512]{1,0:T(8,128)(2,1)S(1)}, bf16[512,512]{1,0:T(8,128)(2,1)S(1)}, u32[]{:S(2)}, u32[]{:S(2)}) collective-permute-start(bf16[512,512]{1,0:T(8,128)(2,1)S(1)} %collective-permute-done.1), channel_id=1, source_target_pairs={{0,7},{1,0},{2,1},{3,2},{4,3},{5,4},{6,5},{7,6},{8,9},{9,10},{10,1... | collective-permute-start | bytes 1572872 | tf_op jit(solution)/shard_map/ppermute | solution.py:119
  16.3 0.9 copy-done.2
  17.3 0.7 copy-done.3
  18.0 0.7 copy-done.4
  18.6 1.9 %shard_map.103 = (bf16[512,512]{1,0:T(8,128)(2,1)}, s32[1,512]{1,0:T(1,128)S(1)}, s32[1,512]{1,0:T(1,128)S(1)}) custom-call(s32[1]{0:T(128)} %bitcast.here_ref, s32[1,16]{1,0:T(1,128)S(1)} %copy-done.4, s32[1,512]{1,0:T(1,128)S(1)} %copy-done.3, bf16[256,512]{1,0:T(8,128)(2,1)S(1)} %bitcast.34), custom_call_target="tpu_custom_call" | custom-call | flops 134217728 | bytes 1048576 | tf_op jit(solution)/shard_map/pallas_call | solution.py:130
  20.5 16.2 %all-to-all-start = ((bf16[16,32,512]{2,1,0:T(8,128)(2,1)}), bf16[16,32,512]{2,1,0:T(8,128)(2,1)S(1)}, u32[]{:S(2)}, u32[]{:S(2)}) async-start(bf16[16,32,512]{2,1,0:T(8,128)(2,1)} %bitcast.3), calls=%async_computation | async-start | bytes 1048576 | tf_op jit(solution)/shard_map/all_to_all | solution.py:147
  36.8 2.2 %collective-permute-start.3 = (bf16[512,512]{1,0:T(8,128)(2,1)S(1)}, bf16[512,512]{1,0:T(8,128)(2,1)S(1)}, u32[]{:S(2)}, u32[]{:S(2)}) collective-permute-start(bf16[512,512]{1,0:T(8,128)(2,1)S(1)} %collective-permute-done), channel_id=1, source_target_pairs={{0,1},{1,2},{2,3},{3,4},{4,5},{5,6},{6,7},{7,0},{8,15},{9,8},{10,9... | collective-permute-start | bytes 1572872 | tf_op jit(solution)/shard_map/ppermute | solution.py:119
  39.0 3.4 %collective-permute-start.5 = (bf16[512,512]{1,0:T(8,128)(2,1)S(1)}, bf16[512,512]{1,0:T(8,128)(2,1)S(1)}, u32[]{:S(2)}, u32[]{:S(2)}) collective-permute-start(bf16[512,512]{1,0:T(8,128)(2,1)S(1)} %collective-permute-done.2), channel_id=1, source_target_pairs={{0,7},{1,0},{2,1},{3,2},{4,3},{5,4},{6,5},{7,6},{8,9},{9,10},{10,1... | collective-permute-start | bytes 1572872 | tf_op jit(solution)/shard_map/ppermute | solution.py:119
  42.4 1.5 %fusion.12 = f32[512,512]{1,0:T(8,128)S(1)} fusion(bf16[512,512]{1,0:T(8,128)(2,1)S(1)} %collective-permute-done, bf16[512,4096]{1,0:T(8,128)(2,1)} %param.12, s32[]{:T(128)S(6)} %select_n.67), kind=kOutput, calls=%fused_computation.20 | convolution fusion | flops 268435456 | bytes 2097156 | tf_op jit(solution)/shard_map/dot_general | solution.py:124
  43.9 1.5 %fusion.10 = f32[512,512]{1,0:T(8,128)S(1)} fusion(bf16[512,512]{1,0:T(8,128)(2,1)S(1)} %collective-permute-done.1, bf16[512,4096]{1,0:T(8,128)(2,1)} %param.12, s32[]{:T(128)S(6)} %select_n.69), kind=kOutput, calls=%fused_computation.18 | convolution fusion | flops 268435456 | bytes 2097156 | tf_op jit(solution)/shard_map/dot_general | solution.py:124
  45.4 3.8 %collective-permute-done.3 = bf16[512,512]{1,0:T(8,128)(2,1)S(1)} collective-permute-done((bf16[512,512]{1,0:T(8,128)(2,1)S(1)}, bf16[512,512]{1,0:T(8,128)(2,1)S(1)}, u32[]{:S(2)}, u32[]{:S(2)}) %collective-permute-start.3) | collective-permute-done | bytes 524320 | tf_op jit(solution)/shard_map/ppermute | solution.py:119
  49.2 1.9 %collective-permute-start.4 = (bf16[512,512]{1,0:T(8,128)(2,1)S(1)}, bf16[512,512]{1,0:T(8,128)(2,1)S(1)}, u32[]{:S(2)}, u32[]{:S(2)}) collective-permute-start(bf16[512,512]{1,0:T(8,128)(2,1)S(1)} %collective-permute-done.3), channel_id=1, source_target_pairs={{0,1},{1,2},{2,3},{3,4},{4,5},{5,6},{6,7},{7,0},{8,15},{9,8},{10,9... | collective-permute-start | bytes 1572872 | tf_op jit(solution)/shard_map/ppermute | solution.py:119
  51.2 0.5 convolution_bitcast_fusion.2
  51.7 0.5 fusion.3
  52.2 0.5 convolution_add_fusion.1
  52.7 6.5 %collective-permute-done.4 = bf16[512,512]{1,0:T(8,128)(2,1)S(1)} collective-permute-done((bf16[512,512]{1,0:T(8,128)(2,1)S(1)}, bf16[512,512]{1,0:T(8,128)(2,1)S(1)}, u32[]{:S(2)}, u32[]{:S(2)}) %collective-permute-start.4) | collective-permute-done | bytes 524320 | tf_op jit(solution)/shard_map/ppermute | solution.py:119
  59.1 3.1 %collective-permute-start.6 = (bf16[512,512]{1,0:T(8,128)(2,1)S(1)}, bf16[512,512]{1,0:T(8,128)(2,1)S(1)}, u32[]{:S(2)}, u32[]{:S(2)}) collective-permute-start(bf16[512,512]{1,0:T(8,128)(2,1)S(1)} %collective-permute-done.4), channel_id=1, source_target_pairs={{0,1},{1,2},{2,3},{3,4},{4,5},{5,6},{6,7},{7,0},{8,15},{9,8},{10,9... | collective-permute-start | bytes 1572872 | tf_op jit(solution)/shard_map/ppermute | solution.py:119
  62.8 0.5 convolution_add_fusion
  63.3 5.9 %collective-permute-done.6 = bf16[512,512]{1,0:T(8,128)(2,1)S(1)} collective-permute-done((bf16[512,512]{1,0:T(8,128)(2,1)S(1)}, bf16[512,512]{1,0:T(8,128)(2,1)S(1)}, u32[]{:S(2)}, u32[]{:S(2)}) %collective-permute-start.6) | collective-permute-done | bytes 524320 | tf_op jit(solution)/shard_map/ppermute | solution.py:119
  69.7 1.6 %shard_map.104 = (bf16[512,512]{1,0:T(8,128)(2,1)}, f32[1,512]{1,0:T(1,128)S(1)}) custom-call(bf16[512,512]{1,0:T(8,128)(2,1)S(1)} %bitcast.32, s32[1,512]{1,0:T(1,128)S(1)} %get-tuple-element.18.ids_ref, bf16[1,512]{1,0:T(2,128)(2,1)S(1)} %copy-done.1, f32[512,512]{1,0:T(8,128)S(1)} %fusion.back_ref), custom_call_target="tpu_custom_call" | custom-call | flops 536870912 | bytes 2097152 | tf_op jit(solution)/shard_map/pallas_call | solution.py:167
  71.3 16.4 %all-to-all-start.1 = ((bf16[16,32,512]{2,1,0:T(8,128)(2,1)}), bf16[16,32,512]{2,1,0:T(8,128)(2,1)S(1)}, u32[]{:S(2)}, u32[]{:S(2)}) async-start(bf16[16,32,512]{2,1,0:T(8,128)(2,1)} %bitcast.9), calls=%async_computation.1 | async-start | bytes 1048576 | tf_op jit(solution)/shard_map/all_to_all | solution.py:147
  87.7 11.8 %psum.7.dots_ref = f32[1,512]{1,0:T(1,128)S(1)} all-reduce(f32[1,512]{1,0:T(1,128)S(1)} %get-tuple-element.24), channel_id=1, replica_groups=mesh['dp'=8,'seq'=16,'tensor'=8] {'tensor'}, use_global_device_ids=true, to_apply=%region_0.1 | all-reduce | flops 512 | bytes 4096 | tf_op jit(solution)/shard_map/psum | solution.py:178
  99.6 0.9 shard_map.105
  100.5 4.5 %all-to-all-done.1 = bf16[16,32,512]{2,1,0:T(8,128)(2,1)S(1)} async-done(((bf16[16,32,512]{2,1,0:T(8,128)(2,1)}), bf16[16,32,512]{2,1,0:T(8,128)(2,1)S(1)}, u32[]{:S(2)}, u32[]{:S(2)}) %all-to-all-start.1) | async-done | bytes 524320 | tf_op jit(solution)/shard_map/all_to_all | solution.py:147
  105.0 20.4 %all-to-all-start.2 = ((f32[128,1,512]{2,1,0:T(1,128)}), f32[128,1,512]{2,1,0:T(1,128)S(1)}, u32[]{:S(2)}, u32[]{:S(2)}) async-start(f32[128,1,512]{2,1,0:T(1,128)} %get-tuple-element.28), calls=%async_computation.2 | async-start | bytes 524288 | tf_op jit(solution)/shard_map/all_to_all | solution.py:195
  125.5 1.0 add_convert_fusion
  126.5 1.0 fusion.4
  127.5 13.2 %all-to-all-done.2 = f32[128,1,512]{2,1,0:T(1,128)S(1)} async-done(((f32[128,1,512]{2,1,0:T(1,128)}), f32[128,1,512]{2,1,0:T(1,128)S(1)}, u32[]{:S(2)}, u32[]{:S(2)}) %all-to-all-start.2) | async-done | bytes 262176 | tf_op jit(solution)/shard_map/all_to_all | solution.py:195
  140.7 0.8 reduce_sum.9
  (20 shorter events, 1.0 us)
Async XLA Ops:
  0.6 12.1 %collective-permute-start.1 = (bf16[512,512]{1,0:T(8,128)(2,1)}, bf16[512,512]{1,0:T(8,128)(2,1)S(1)}, u32[]{:S(2)}, u32[]{:S(2)}) collective-permute-start(bf16[512,512]{1,0:T(8,128)(2,1)} %bitcast.36), channel_id=1, source_target_pairs={{0,7},{1,0},{2,1},{3,2},{4,3},{5,4},{6,5},{7,6},{8,9},{9,10},{10,1... | collective-permute-start | bytes 1572872 | tf_op jit(solution)/shard_map/ppermute | solution.py:119
  4.6 32.2 %collective-permute-start = (bf16[512,512]{1,0:T(8,128)(2,1)}, bf16[512,512]{1,0:T(8,128)(2,1)S(1)}, u32[]{:S(2)}, u32[]{:S(2)}) collective-permute-start(bf16[512,512]{1,0:T(8,128)(2,1)} %bitcast.37), channel_id=1, source_target_pairs={{0,1},{1,2},{2,3},{3,4},{4,5},{5,6},{6,7},{7,0},{8,15},{9,8},{10,9... | collective-permute-start | bytes 1572872 | tf_op jit(solution)/shard_map/ppermute | solution.py:119
  12.7 26.3 %collective-permute-start.2 = (bf16[512,512]{1,0:T(8,128)(2,1)S(1)}, bf16[512,512]{1,0:T(8,128)(2,1)S(1)}, u32[]{:S(2)}, u32[]{:S(2)}) collective-permute-start(bf16[512,512]{1,0:T(8,128)(2,1)S(1)} %collective-permute-done.1), channel_id=1, source_target_pairs={{0,7},{1,0},{2,1},{3,2},{4,3},{5,4},{6,5},{7,6},{8,9},{9,10},{10,1... | collective-permute-start | bytes 1572872 | tf_op jit(solution)/shard_map/ppermute | solution.py:119
  16.3 1.0 copy-start.2
  17.3 0.7 copy-start.3
  18.0 0.7 copy-start.4
  18.6 33.0 %copy-start.6 = (bf16[1,512,512]{2,1,0:T(8,128)(2,1)S(1)}, bf16[1,512,512]{2,1,0:T(8,128)(2,1)}, u32[]{:S(2)}) copy-start(bf16[1,512,512]{2,1,0:T(8,128)(2,1)} %param.10) | copy-start | bytes 1572868
  20.5 49.2 %all-to-all-start = ((bf16[16,32,512]{2,1,0:T(8,128)(2,1)}), bf16[16,32,512]{2,1,0:T(8,128)(2,1)S(1)}, u32[]{:S(2)}, u32[]{:S(2)}) async-start(bf16[16,32,512]{2,1,0:T(8,128)(2,1)} %bitcast.3), calls=%async_computation | async-start | bytes 1048576 | tf_op jit(solution)/shard_map/all_to_all | solution.py:147
  36.8 14.4 %copy-start.5 = (bf16[512,4096]{1,0:T(8,128)(2,1)S(1)}, bf16[512,4096]{1,0:T(8,128)(2,1)}, u32[]{:S(2)}) copy-start(bf16[512,4096]{1,0:T(8,128)(2,1)} %param.12) | copy-start | bytes 12582916
  36.8 12.4 %collective-permute-start.3 = (bf16[512,512]{1,0:T(8,128)(2,1)S(1)}, bf16[512,512]{1,0:T(8,128)(2,1)S(1)}, u32[]{:S(2)}, u32[]{:S(2)}) collective-permute-start(bf16[512,512]{1,0:T(8,128)(2,1)S(1)} %collective-permute-done), channel_id=1, source_target_pairs={{0,1},{1,2},{2,3},{3,4},{4,5},{5,6},{6,7},{7,0},{8,15},{9,8},{10,9... | collective-permute-start | bytes 1572872 | tf_op jit(solution)/shard_map/ppermute | solution.py:119
  39.0 23.8 %collective-permute-start.5 = (bf16[512,512]{1,0:T(8,128)(2,1)S(1)}, bf16[512,512]{1,0:T(8,128)(2,1)S(1)}, u32[]{:S(2)}, u32[]{:S(2)}) collective-permute-start(bf16[512,512]{1,0:T(8,128)(2,1)S(1)} %collective-permute-done.2), channel_id=1, source_target_pairs={{0,7},{1,0},{2,1},{3,2},{4,3},{5,4},{6,5},{7,6},{8,9},{9,10},{10,1... | collective-permute-start | bytes 1572872 | tf_op jit(solution)/shard_map/ppermute | solution.py:119
  49.2 9.9 %collective-permute-start.4 = (bf16[512,512]{1,0:T(8,128)(2,1)S(1)}, bf16[512,512]{1,0:T(8,128)(2,1)S(1)}, u32[]{:S(2)}, u32[]{:S(2)}) collective-permute-start(bf16[512,512]{1,0:T(8,128)(2,1)S(1)} %collective-permute-done.3), channel_id=1, source_target_pairs={{0,1},{1,2},{2,3},{3,4},{4,5},{5,6},{6,7},{7,0},{8,15},{9,8},{10,9... | collective-permute-start | bytes 1572872 | tf_op jit(solution)/shard_map/ppermute | solution.py:119
  52.7 17.0 %copy-start.1 = (bf16[1,512]{1,0:T(2,128)(2,1)S(1)}, bf16[1,512]{1,0:T(2,128)(2,1)}, u32[]{:S(2)}) copy-start(bf16[1,512]{1,0:T(2,128)(2,1)} %logits_ref.3) | copy-start | bytes 3076
  59.1 10.1 %collective-permute-start.6 = (bf16[512,512]{1,0:T(8,128)(2,1)S(1)}, bf16[512,512]{1,0:T(8,128)(2,1)S(1)}, u32[]{:S(2)}, u32[]{:S(2)}) collective-permute-start(bf16[512,512]{1,0:T(8,128)(2,1)S(1)} %collective-permute-done.4), channel_id=1, source_target_pairs={{0,1},{1,2},{2,3},{3,4},{4,5},{5,6},{6,7},{7,0},{8,15},{9,8},{10,9... | collective-permute-start | bytes 1572872 | tf_op jit(solution)/shard_map/ppermute | solution.py:119
  62.8 36.8 %copy-start = (bf16[1,512,512]{2,1,0:T(8,128)(2,1)S(1)}, bf16[1,512,512]{2,1,0:T(8,128)(2,1)}, u32[]{:S(2)}) copy-start(bf16[1,512,512]{2,1,0:T(8,128)(2,1)} %param.8) | copy-start | bytes 1572868
  63.3 62.2 %copy-start.7 = (f32[512]{0:T(512)S(1)}, f32[512]{0:T(512)}, u32[]{:S(2)}) copy-start(f32[512]{0:T(512)} %param.13) | copy-start | bytes 6148
  71.3 33.7 %all-to-all-start.1 = ((bf16[16,32,512]{2,1,0:T(8,128)(2,1)}), bf16[16,32,512]{2,1,0:T(8,128)(2,1)S(1)}, u32[]{:S(2)}, u32[]{:S(2)}) async-start(bf16[16,32,512]{2,1,0:T(8,128)(2,1)} %bitcast.9), calls=%async_computation.1 | async-start | bytes 1048576 | tf_op jit(solution)/shard_map/all_to_all | solution.py:147
  105.0 35.7 %all-to-all-start.2 = ((f32[128,1,512]{2,1,0:T(1,128)}), f32[128,1,512]{2,1,0:T(1,128)S(1)}, u32[]{:S(2)}, u32[]{:S(2)}) async-start(f32[128,1,512]{2,1,0:T(1,128)} %get-tuple-element.28), calls=%async_computation.2 | async-start | bytes 524288 | tf_op jit(solution)/shard_map/all_to_all | solution.py:195

commit v7 on v6

--- a/solution.py
+++ b/solution.py
@@ -151,16 +151,14 @@
 
     own = cotangent[0]
     first_in, second_in = own, own
-    blocks = [(own, 0)]
+    product = None
     for step in range(1, nten // 2):
         first_in = turn(first_in, 1)
         second_in = turn(second_in, -1)
-        if step == 2:
-            waiting = tuple(block for block, _ in blocks)
-            waiting, second_in = lax.optimization_barrier((waiting, second_in))
-            blocks = [(block, way) for block, (_, way) in zip(waiting, blocks)]
-        blocks += [(first_in, -step), (second_in, step)]
-    product = sum(times(block, way) for block, way in blocks)
+        if step == 1:
+            own, first_in = lax.optimization_barrier((own, first_in))
+            product = times(own, 0)
+        product = product + times(first_in, -step) + times(second_in, step)
     last_in = turn(first_in, 1)
     product = product + times(last_in, nten // 2)
 

time: 142 us -> 130 us (0.915)
  starting transfers between devices: 74.5 us -> 68.4 us
  waiting for transfers between devices: 38.8 us -> 33.2 us
    all_to_all x1, starting transfers between devices: 20.4 us -> 13.5 us  [shards(): lax.all_to_all(copies, ('dp', 'seq'), 0, 0, tiled=True)]
    ppermute x7, waiting for transfers between devices: 21.1 us -> 15.4 us  [turn(): return lax.ppermute(block, ('seq', 'tensor'), pairs)]
  transfers between devices with their start and end apart: 10 -> 10, of which waited for: 6 -> 7; matrix products, arithmetic and copies ran while one was open for 6% -> 6% of each run, Pallas kernels for 2% -> 2%
where the time goes in v7:
time: 130 us
  starting transfers between devices  68.4 us (53%)
  waiting for transfers between devices  33.2 us (26%)
  blocking collectives  11.8 us (9%)
  matrix products  6.91 us (5%)
  Pallas kernels  4.41 us (3%)
  local copies, waits for them, and re-layouts  2.31 us (2%)
  other arithmetic  1.78 us (1%)
    all_to_all x2, starting transfers between devices, exchange(): lax.all_to_all(parts, 'seq', split_axis=0, concat_axis=0, tiled=True)  33.7 us
    ppermute x7, starting transfers between devices, turn(): return lax.ppermute(block, ('seq', 'tensor'), pairs)  21.2 us
    ppermute x7, waiting for transfers between devices, turn(): return lax.ppermute(block, ('seq', 'tensor'), pairs)  15.4 us
    all_to_all x1, starting transfers between devices, shards(): lax.all_to_all(copies, ('dp', 'seq'), 0, 0, tiled=True)  13.5 us
    all_to_all x1, waiting for transfers between devices, shards(): lax.all_to_all(copies, ('dp', 'seq'), 0, 0, tiled=True)  13.2 us
    psum x1, blocking collectives, shards(): dots = lax.psum(partial_dots, 'tensor')  11.8 us
    dot_general x8, matrix products, times(): lax.dot_general(block, weight, (((1,), (1,)), ((), ())), preferred_elemen...  5.89 us
    all_to_all x2, waiting for transfers between devices, exchange(): lax.all_to_all(parts, 'seq', split_axis=0, concat_axis=0, tiled=True)  4.53 us
  transfers between devices with their start and end apart: 10, of which 7 were waited for; matrix products, arithmetic and copies ran while one was open for 6% of the time, Pallas kernels for 2%

profile of v7, /device:TPU:1, one launch (start us, length us, event | category | flops | bytes accessed | tf_op | source)
XLA Modules:
  0.0 129.6 jit_solution(2471861690338679944)
XLA Ops:
  0.6 5.3 %collective-permute-start = (bf16[512,512]{1,0:T(8,128)(2,1)}, bf16[512,512]{1,0:T(8,128)(2,1)S(1)}, u32[]{:S(2)}, u32[]{:S(2)}) collective-permute-start(bf16[512,512]{1,0:T(8,128)(2,1)} %bitcast.35), channel_id=1, source_target_pairs={{0,1},{1,2},{2,3},{3,4},{4,5},{5,6},{6,7},{7,0},{8,15},{9,8},{10,9... | collective-permute-start | bytes 1572872 | tf_op jit(solution)/shard_map/ppermute | solution.py:119
  6.0 1.9 %collective-permute-start.1 = (bf16[512,512]{1,0:T(8,128)(2,1)}, bf16[512,512]{1,0:T(8,128)(2,1)S(1)}, u32[]{:S(2)}, u32[]{:S(2)}) collective-permute-start(bf16[512,512]{1,0:T(8,128)(2,1)} %bitcast.36), channel_id=1, source_target_pairs={{0,7},{1,0},{2,1},{3,2},{4,3},{5,4},{6,5},{7,6},{8,9},{9,10},{10,1... | collective-permute-start | bytes 1572872 | tf_op jit(solution)/shard_map/ppermute | solution.py:119
  7.9 0.9 copy-done.2
  8.9 0.7 copy-done.3
  9.5 0.7 copy-done.4
  10.2 1.9 %shard_map.103 = (bf16[512,512]{1,0:T(8,128)(2,1)}, s32[1,512]{1,0:T(1,128)S(1)}, s32[1,512]{1,0:T(1,128)S(1)}) custom-call(s32[1]{0:T(128)} %bitcast.here_ref, s32[1,16]{1,0:T(1,128)S(1)} %copy-done.4, s32[1,512]{1,0:T(1,128)S(1)} %copy-done.3, bf16[256,512]{1,0:T(8,128)(2,1)S(1)} %bitcast.34), custom_call_target="tpu_custom_call" | custom-call | flops 134217728 | bytes 1048576 | tf_op jit(solution)/shard_map/pallas_call | solution.py:130
  12.1 17.3 %all-to-all-start = ((bf16[16,32,512]{2,1,0:T(8,128)(2,1)}), bf16[16,32,512]{2,1,0:T(8,128)(2,1)S(1)}, u32[]{:S(2)}, u32[]{:S(2)}) async-start(bf16[16,32,512]{2,1,0:T(8,128)(2,1)} %bitcast.3), calls=%async_computation | async-start | bytes 1048576 | tf_op jit(solution)/shard_map/all_to_all | solution.py:147
  29.4 2.2 %collective-permute-start.2 = (bf16[512,512]{1,0:T(8,128)(2,1)S(1)}, bf16[512,512]{1,0:T(8,128)(2,1)S(1)}, u32[]{:S(2)}, u32[]{:S(2)}) collective-permute-start(bf16[512,512]{1,0:T(8,128)(2,1)S(1)} %collective-permute-done), channel_id=1, source_target_pairs={{0,1},{1,2},{2,3},{3,4},{4,5},{5,6},{6,7},{7,0},{8,15},{9,8},{10,9... | collective-permute-start | bytes 1572872 | tf_op jit(solution)/shard_map/ppermute | solution.py:119
  31.6 1.5 %fusion.10 = f32[512,512]{1,0:T(8,128)S(1)} fusion(bf16[512,512]{1,0:T(8,128)(2,1)S(1)} %collective-permute-done, bf16[512,4096]{1,0:T(8,128)(2,1)} %param.12, s32[]{:T(128)S(6)} %select_n.67), kind=kOutput, calls=%fused_computation.19 | convolution fusion | flops 268435456 | bytes 2097156 | tf_op jit(solution)/shard_map/dot_general | solution.py:124
  33.2 3.4 %collective-permute-start.3 = (bf16[512,512]{1,0:T(8,128)(2,1)S(1)}, bf16[512,512]{1,0:T(8,128)(2,1)S(1)}, u32[]{:S(2)}, u32[]{:S(2)}) collective-permute-start(bf16[512,512]{1,0:T(8,128)(2,1)S(1)} %collective-permute-done.1), channel_id=1, source_target_pairs={{0,7},{1,0},{2,1},{3,2},{4,3},{5,4},{6,5},{7,6},{8,9},{9,10},{10,1... | collective-permute-start | bytes 1572872 | tf_op jit(solution)/shard_map/ppermute | solution.py:119
  36.5 1.5 %convolution_bitcast_fusion.2 = f32[512,512]{1,0:T(8,128)S(1)} fusion(bf16[512,512]{1,0:T(8,128)(2,1)S(1)} %collective-permute-done.1, bf16[512,4096]{1,0:T(8,128)(2,1)} %param.12, s32[]{:T(128)S(6)} %select_n.69), kind=kOutput, calls=%fused_computation.7 | convolution fusion | flops 268435456 | bytes 2097156 | tf_op jit(solution)/shard_map/dot_general | solution.py:124
  38.6 2.6 %collective-permute-done.2 = bf16[512,512]{1,0:T(8,128)(2,1)S(1)} collective-permute-done((bf16[512,512]{1,0:T(8,128)(2,1)S(1)}, bf16[512,512]{1,0:T(8,128)(2,1)S(1)}, u32[]{:S(2)}, u32[]{:S(2)}) %collective-permute-start.2) | collective-permute-done | bytes 524320 | tf_op jit(solution)/shard_map/ppermute | solution.py:119
  41.2 1.9 %collective-permute-start.4 = (bf16[512,512]{1,0:T(8,128)(2,1)S(1)}, bf16[512,512]{1,0:T(8,128)(2,1)S(1)}, u32[]{:S(2)}, u32[]{:S(2)}) collective-permute-start(bf16[512,512]{1,0:T(8,128)(2,1)S(1)} %collective-permute-done.2), channel_id=1, source_target_pairs={{0,1},{1,2},{2,3},{3,4},{4,5},{5,6},{6,7},{7,0},{8,15},{9,8},{10,9... | collective-permute-start | bytes 1572872 | tf_op jit(solution)/shard_map/ppermute | solution.py:119
  43.1 4.2 %collective-permute-done.3 = bf16[512,512]{1,0:T(8,128)(2,1)S(1)} collective-permute-done((bf16[512,512]{1,0:T(8,128)(2,1)S(1)}, bf16[512,512]{1,0:T(8,128)(2,1)S(1)}, u32[]{:S(2)}, u32[]{:S(2)}) %collective-permute-start.3) | collective-permute-done | bytes 524320 | tf_op jit(solution)/shard_map/ppermute | solution.py:119
  47.3 1.9 %collective-permute-start.5 = (bf16[512,512]{1,0:T(8,128)(2,1)S(1)}, bf16[512,512]{1,0:T(8,128)(2,1)S(1)}, u32[]{:S(2)}, u32[]{:S(2)}) collective-permute-start(bf16[512,512]{1,0:T(8,128)(2,1)S(1)} %collective-permute-done.3), channel_id=1, source_target_pairs={{0,7},{1,0},{2,1},{3,2},{4,3},{5,4},{6,5},{7,6},{8,9},{9,10},{10,1... | collective-permute-start | bytes 1572872 | tf_op jit(solution)/shard_map/ppermute | solution.py:119
  49.2 0.5 convolution_add_fusion.2
  49.7 0.5 fusion.1
  50.2 0.8 collective-permute-done.4
  51.1 4.5 %collective-permute-start.6 = (bf16[512,512]{1,0:T(8,128)(2,1)S(1)}, bf16[512,512]{1,0:T(8,128)(2,1)S(1)}, u32[]{:S(2)}, u32[]{:S(2)}) collective-permute-start(bf16[512,512]{1,0:T(8,128)(2,1)S(1)} %collective-permute-done.4), channel_id=1, source_target_pairs={{0,1},{1,2},{2,3},{3,4},{4,5},{5,6},{6,7},{7,0},{8,15},{9,8},{10,9... | collective-permute-start | bytes 1572872 | tf_op jit(solution)/shard_map/ppermute | solution.py:119
  55.6 0.5 convolution_add_fusion.1
  56.1 6.4 %collective-permute-done.5 = bf16[512,512]{1,0:T(8,128)(2,1)S(1)} collective-permute-done((bf16[512,512]{1,0:T(8,128)(2,1)S(1)}, bf16[512,512]{1,0:T(8,128)(2,1)S(1)}, u32[]{:S(2)}, u32[]{:S(2)}) %collective-permute-start.5) | collective-permute-done | bytes 524320 | tf_op jit(solution)/shard_map/ppermute | solution.py:119
  63.0 1.3 collective-permute-done.6
  64.8 1.6 %shard_map.104 = (bf16[512,512]{1,0:T(8,128)(2,1)}, f32[1,512]{1,0:T(1,128)S(1)}) custom-call(bf16[512,512]{1,0:T(8,128)(2,1)S(1)} %bitcast.32, s32[1,512]{1,0:T(1,128)S(1)} %get-tuple-element.16.ids_ref, bf16[1,512]{1,0:T(2,128)(2,1)S(1)} %copy-done.1, f32[512,512]{1,0:T(8,128)S(1)} %convolution_add_fusion.back_ref), custom_call_target="tpu_custom_call" | custom-call | flops 536870912 | bytes 2097152 | tf_op jit(solution)/shard_map/pallas_call | solution.py:165
  66.4 16.4 %all-to-all-start.1 = ((bf16[16,32,512]{2,1,0:T(8,128)(2,1)}), bf16[16,32,512]{2,1,0:T(8,128)(2,1)S(1)}, u32[]{:S(2)}, u32[]{:S(2)}) async-start(bf16[16,32,512]{2,1,0:T(8,128)(2,1)} %bitcast.9), calls=%async_computation.1 | async-start | bytes 1048576 | tf_op jit(solution)/shard_map/all_to_all | solution.py:147
  82.8 11.8 %psum.7.dots_ref = f32[1,512]{1,0:T(1,128)S(1)} all-reduce(f32[1,512]{1,0:T(1,128)S(1)} %get-tuple-element.20), channel_id=1, replica_groups=mesh['dp'=8,'seq'=16,'tensor'=8] {'tensor'}, use_global_device_ids=true, to_apply=%region_0.1 | all-reduce | flops 512 | bytes 4096 | tf_op jit(solution)/shard_map/psum | solution.py:176
  94.7 0.9 shard_map.105
  95.6 4.5 %all-to-all-done.1 = bf16[16,32,512]{2,1,0:T(8,128)(2,1)S(1)} async-done(((bf16[16,32,512]{2,1,0:T(8,128)(2,1)}), bf16[16,32,512]{2,1,0:T(8,128)(2,1)S(1)}, u32[]{:S(2)}, u32[]{:S(2)}) %all-to-all-start.1) | async-done | bytes 524320 | tf_op jit(solution)/shard_map/all_to_all | solution.py:147
  100.1 13.5 %all-to-all-start.2 = ((f32[128,1,512]{2,1,0:T(1,128)}), f32[128,1,512]{2,1,0:T(1,128)S(1)}, u32[]{:S(2)}, u32[]{:S(2)}) async-start(f32[128,1,512]{2,1,0:T(1,128)} %get-tuple-element.24), calls=%async_computation.2 | async-start | bytes 524288 | tf_op jit(solution)/shard_map/all_to_all | solution.py:193
  113.6 1.0 add_convert_fusion
  114.6 1.0 fusion.3
  115.6 13.2 %all-to-all-done.2 = f32[128,1,512]{2,1,0:T(1,128)S(1)} async-done(((f32[128,1,512]{2,1,0:T(1,128)}), f32[128,1,512]{2,1,0:T(1,128)S(1)}, u32[]{:S(2)}, u32[]{:S(2)}) %all-to-all-start.2) | async-done | bytes 262176 | tf_op jit(solution)/shard_map/all_to_all | solution.py:193
  128.8 0.8 reduce_sum.9
  (20 shorter events, 1.5 us)
Async XLA Ops:
  0.6 28.8 %collective-permute-start = (bf16[512,512]{1,0:T(8,128)(2,1)}, bf16[512,512]{1,0:T(8,128)(2,1)S(1)}, u32[]{:S(2)}, u32[]{:S(2)}) collective-permute-start(bf16[512,512]{1,0:T(8,128)(2,1)} %bitcast.35), channel_id=1, source_target_pairs={{0,1},{1,2},{2,3},{3,4},{4,5},{5,6},{6,7},{7,0},{8,15},{9,8},{10,9... | collective-permute-start | bytes 1572872 | tf_op jit(solution)/shard_map/ppermute | solution.py:119
  6.0 27.2 %collective-permute-start.1 = (bf16[512,512]{1,0:T(8,128)(2,1)}, bf16[512,512]{1,0:T(8,128)(2,1)S(1)}, u32[]{:S(2)}, u32[]{:S(2)}) collective-permute-start(bf16[512,512]{1,0:T(8,128)(2,1)} %bitcast.36), channel_id=1, source_target_pairs={{0,7},{1,0},{2,1},{3,2},{4,3},{5,4},{6,5},{7,6},{8,9},{9,10},{10,1... | collective-permute-start | bytes 1572872 | tf_op jit(solution)/shard_map/ppermute | solution.py:119
  7.9 1.0 copy-start.2
  8.9 0.7 copy-start.3
  9.5 0.7 copy-start.4
  10.2 27.9 %copy-start.6 = (bf16[1,512,512]{2,1,0:T(8,128)(2,1)S(1)}, bf16[1,512,512]{2,1,0:T(8,128)(2,1)}, u32[]{:S(2)}) copy-start(bf16[1,512,512]{2,1,0:T(8,128)(2,1)} %param.10) | copy-start | bytes 1572868
  12.1 52.7 %all-to-all-start = ((bf16[16,32,512]{2,1,0:T(8,128)(2,1)}), bf16[16,32,512]{2,1,0:T(8,128)(2,1)S(1)}, u32[]{:S(2)}, u32[]{:S(2)}) async-start(bf16[16,32,512]{2,1,0:T(8,128)(2,1)} %bitcast.3), calls=%async_computation | async-start | bytes 1048576 | tf_op jit(solution)/shard_map/all_to_all | solution.py:147
  29.4 8.6 %copy-start.5 = (bf16[512,4096]{1,0:T(8,128)(2,1)S(1)}, bf16[512,4096]{1,0:T(8,128)(2,1)}, u32[]{:S(2)}) copy-start(bf16[512,4096]{1,0:T(8,128)(2,1)} %param.12) | copy-start | bytes 12582916
  29.4 11.7 %collective-permute-start.2 = (bf16[512,512]{1,0:T(8,128)(2,1)S(1)}, bf16[512,512]{1,0:T(8,128)(2,1)S(1)}, u32[]{:S(2)}, u32[]{:S(2)}) collective-permute-start(bf16[512,512]{1,0:T(8,128)(2,1)S(1)} %collective-permute-done), channel_id=1, source_target_pairs={{0,1},{1,2},{2,3},{3,4},{4,5},{5,6},{6,7},{7,0},{8,15},{9,8},{10,9... | collective-permute-start | bytes 1572872 | tf_op jit(solution)/shard_map/ppermute | solution.py:119
  33.2 14.2 %collective-permute-start.3 = (bf16[512,512]{1,0:T(8,128)(2,1)S(1)}, bf16[512,512]{1,0:T(8,128)(2,1)S(1)}, u32[]{:S(2)}, u32[]{:S(2)}) collective-permute-start(bf16[512,512]{1,0:T(8,128)(2,1)S(1)} %collective-permute-done.1), channel_id=1, source_target_pairs={{0,7},{1,0},{2,1},{3,2},{4,3},{5,4},{6,5},{7,6},{8,9},{9,10},{10,1... | collective-permute-start | bytes 1572872 | tf_op jit(solution)/shard_map/ppermute | solution.py:119
  41.2 9.9 %collective-permute-start.4 = (bf16[512,512]{1,0:T(8,128)(2,1)S(1)}, bf16[512,512]{1,0:T(8,128)(2,1)S(1)}, u32[]{:S(2)}, u32[]{:S(2)}) collective-permute-start(bf16[512,512]{1,0:T(8,128)(2,1)S(1)} %collective-permute-done.2), channel_id=1, source_target_pairs={{0,1},{1,2},{2,3},{3,4},{4,5},{5,6},{6,7},{7,0},{8,15},{9,8},{10,9... | collective-permute-start | bytes 1572872 | tf_op jit(solution)/shard_map/ppermute | solution.py:119
  47.3 15.2 %collective-permute-start.5 = (bf16[512,512]{1,0:T(8,128)(2,1)S(1)}, bf16[512,512]{1,0:T(8,128)(2,1)S(1)}, u32[]{:S(2)}, u32[]{:S(2)}) collective-permute-start(bf16[512,512]{1,0:T(8,128)(2,1)S(1)} %collective-permute-done.3), channel_id=1, source_target_pairs={{0,7},{1,0},{2,1},{3,2},{4,3},{5,4},{6,5},{7,6},{8,9},{9,10},{10,1... | collective-permute-start | bytes 1572872 | tf_op jit(solution)/shard_map/ppermute | solution.py:119
  50.2 14.6 %copy-start.1 = (bf16[1,512]{1,0:T(2,128)(2,1)S(1)}, bf16[1,512]{1,0:T(2,128)(2,1)}, u32[]{:S(2)}) copy-start(bf16[1,512]{1,0:T(2,128)(2,1)} %logits_ref.3) | copy-start | bytes 3076
  51.1 13.2 %collective-permute-start.6 = (bf16[512,512]{1,0:T(8,128)(2,1)S(1)}, bf16[512,512]{1,0:T(8,128)(2,1)S(1)}, u32[]{:S(2)}, u32[]{:S(2)}) collective-permute-start(bf16[512,512]{1,0:T(8,128)(2,1)S(1)} %collective-permute-done.4), channel_id=1, source_target_pairs={{0,1},{1,2},{2,3},{3,4},{4,5},{5,6},{6,7},{7,0},{8,15},{9,8},{10,9... | collective-permute-start | bytes 1572872 | tf_op jit(solution)/shard_map/ppermute | solution.py:119
  56.1 38.5 %copy-start = (bf16[1,512,512]{2,1,0:T(8,128)(2,1)S(1)}, bf16[1,512,512]{2,1,0:T(8,128)(2,1)}, u32[]{:S(2)}) copy-start(bf16[1,512,512]{2,1,0:T(8,128)(2,1)} %param.8) | copy-start | bytes 1572868
  63.0 50.6 %copy-start.7 = (f32[512]{0:T(512)S(1)}, f32[512]{0:T(512)}, u32[]{:S(2)}) copy-start(f32[512]{0:T(512)} %param.13) | copy-start | bytes 6148
  66.4 33.7 %all-to-all-start.1 = ((bf16[16,32,512]{2,1,0:T(8,128)(2,1)}), bf16[16,32,512]{2,1,0:T(8,128)(2,1)S(1)}, u32[]{:S(2)}, u32[]{:S(2)}) async-start(bf16[16,32,512]{2,1,0:T(8,128)(2,1)} %bitcast.9), calls=%async_computation.1 | async-start | bytes 1048576 | tf_op jit(solution)/shard_map/all_to_all | solution.py:147
  100.1 28.7 %all-to-all-start.2 = ((f32[128,1,512]{2,1,0:T(1,128)}), f32[128,1,512]{2,1,0:T(1,128)S(1)}, u32[]{:S(2)}, u32[]{:S(2)}) async-start(f32[128,1,512]{2,1,0:T(1,128)} %get-tuple-element.24), calls=%async_computation.2 | async-start | bytes 524288 | tf_op jit(solution)/shard_map/all_to_all | solution.py:193

commit v8 on v7

--- a/solution.py
+++ b/solution.py
@@ -14,14 +14,9 @@
 PARAMS = pltpu.CompilerParams(vmem_limit_bytes=32 * 1024 * 1024)
 
 
-def pack_kernel(
-    here_ref, counts_ref, keep_ref, att_any, slots_ref, ids_ref, places_ref, att_ref, att_sem
-):
-    fetch = pltpu.make_async_copy(att_any, att_ref, att_sem)
-    fetch.start()
+def table_kernel(here_ref, counts_ref, keep_ref, ids_ref, places_ref):
     nseq = counts_ref.shape[1]
     tok = keep_ref.shape[1]
-    kept_rows = att_ref.shape[0]
     cap = tok // nseq
     seq_bits, cap_bits = nseq.bit_length() - 1, cap.bit_length() - 1
     here = here_ref[0]
@@ -52,13 +47,6 @@
     slot = (ranks & (nseq - 1)) * cap + (local >> seq_bits)
     ids_ref[...] = jnp.where(keep == 1, slot, -1)
 
-    table = lax.broadcasted_iota(jnp.int32, (kept_rows, tok), 0) == places
-    table = jnp.where(table, 1.0, 0.0).astype(jnp.bfloat16)
-    fetch.wait()
-    slots_ref[...] = lax.dot_general(
-        table, att_ref[...], (((0,), (0,)), ((), ())), preferred_element_type=jnp.float32
-    ).astype(jnp.bfloat16)
-
 
 def rate_of(logits_ref):
     return jax.nn.sigmoid(logits_ref[...].astype(jnp.float32))
@@ -118,36 +106,32 @@
         ]
         return lax.ppermute(block, ("seq", "tensor"), pairs)
 
-    def times(block, step):
+    def weight_of(step):
         start = (column + step * flip) % nten * width
-        weight = lax.dynamic_slice(out_weight, (0, start), (heads_width, width))
+        return lax.dynamic_slice(out_weight, (0, start), (heads_width, width))
+
+    def times(block, step, weight=None):
+        weight = weight_of(step) if weight is None else weight
         return lax.dot_general(
             block, weight, (((1,), (1,)), ((), ())), preferred_element_type=jnp.float32
         )
 
     slots_shape = jax.ShapeDtypeStruct((tok, heads_width), jnp.bfloat16)
     row_shape = jax.ShapeDtypeStruct((1, tok), jnp.int32)
-    att_slots, slot_ids, places = pl.pallas_call(
-        pack_kernel,
-        out_shape=(slots_shape, row_shape, row_shape),
-        in_specs=[SMEM, SMEM, VMEM, pl.BlockSpec(memory_space=pl.ANY)],
-        out_specs=(VMEM, VMEM, VMEM),
-        scratch_shapes=[
-            pltpu.VMEM((kept_rows, heads_width), jnp.bfloat16),
-            pltpu.SemaphoreType.DMA,
-        ],
+    slot_ids, places = pl.pallas_call(
+        table_kernel,
+        out_shape=(row_shape, row_shape),
+        in_specs=[SMEM, SMEM, VMEM],
+        out_specs=(VMEM, VMEM),
         compiler_params=PARAMS,
-        cost_estimate=pl.CostEstimate(
-            flops=2 * tok * kept_rows * heads_width, bytes_accessed=2**20, transcendentals=0
-        ),
-    )(here.reshape(1), shard_counts, keep_route, attended[0])
+        cost_estimate=pl.CostEstimate(flops=32 * tok * tok, bytes_accessed=2**13, transcendentals=0),
+    )(here.reshape(1), shard_counts, keep_route)
+    place_table = (jnp.arange(kept_rows, dtype=jnp.int32)[:, None] == places).astype(jnp.bfloat16)
 
     def exchange(slots):
         parts = slots.reshape(nseq, cap, slots.shape[1])
         moved = lax.all_to_all(parts, "seq", split_axis=0, concat_axis=0, tiled=True)
         return moved.reshape(tok, slots.shape[1])
-
-    att_in = exchange(att_slots)
 
     own = cotangent[0]
     first_in, second_in = own, own
@@ -158,9 +142,16 @@
         if step == 1:
             own, first_in = lax.optimization_barrier((own, first_in))
             product = times(own, 0)
+        if step == 2:
+            att_rows, first_in = lax.optimization_barrier((attended[0], first_in))
+            att_slots = lax.dot_general(
+                place_table, att_rows, (((0,), (0,)), ((), ())), preferred_element_type=jnp.float32
+            )
+            att_in = exchange(att_slots.astype(jnp.bfloat16))
         product = product + times(first_in, -step) + times(second_in, step)
     last_in = turn(first_in, 1)
-    product = product + times(last_in, nten // 2)
+    last_weight = lax.optimization_barrier(weight_of(nten // 2))
+    product = product + times(last_in, nten // 2, last_weight)
 
     grad_slots, partial_dots = pl.pallas_call(
         finish_kernel,
@@ -195,9 +186,6 @@
         cotangent.astype(jnp.float32)
         + scale * logit_grad[:, :, None] * router_weight[None, None, :]
     ).astype(jnp.bfloat16)
-    place_table = (
-        jnp.arange(kept_rows, dtype=jnp.int32)[:, None] == places
-    ).astype(jnp.bfloat16)
     att_grad = jnp.dot(place_table, grad_in, preferred_element_type=jnp.float32)
     att_grad = att_grad.astype(jnp.bfloat16)[None]
     return (att_grad, in_grad, router_grad)

time: 130 us -> 135 us (1.038)
  waiting for transfers between devices: 33.2 us -> 24.7 us
  matrix products: 6.91 us -> 14.1 us
  starting transfers between devices: 68.4 us -> 73.4 us
    all_to_all x2, starting transfers between devices: 33.7 us -> 24.2 us  [exchange(): lax.all_to_all(parts, 'seq', split_axis=0, concat_axis=0, tiled=True)]
    all_to_all x1, starting transfers between devices: 13.5 us -> 22.8 us  [shards(): lax.all_to_all(copies, ('dp', 'seq'), 0, 0, tiled=True)]
    ppermute x7, waiting for transfers between devices: 15.4 us -> 8.17 us  [turn(): return lax.ppermute(block, ('seq', 'tensor'), pairs)]
    dot_general x8, matrix products: 5.89 us -> 11.9 us  [times(): lax.dot_general(block, weight, (((1,), (1,)), ((), ())), preferred_elemen...]
    ppermute x7, starting transfers between devices: 21.2 us -> 26.4 us  [turn(): return lax.ppermute(block, ('seq', 'tensor'), pairs)]
  transfers between devices with their start and end apart: 10 -> 10, of which waited for: 7 -> 6; matrix products, arithmetic and copies ran while one was open for 6% -> 12% of each run, Pallas kernels for 2% -> 1%
where the time goes in v8:
time: 135 us; the launch traced here: 134 us
  starting transfers between devices  73.4 us (54%)
  waiting for transfers between devices  24.7 us (18%)
  matrix products  14.1 us (10%)
  blocking collectives  13.1 us (10%)
  Pallas kernels  3.22 us (2%)
  local copies, waits for them, and re-layouts  2.45 us (2%)
  other arithmetic  1.77 us (1%)
    ppermute x7, starting transfers between devices, turn(): return lax.ppermute(block, ('seq', 'tensor'), pairs)  26.4 us
    all_to_all x2, starting transfers between devices, exchange(): lax.all_to_all(parts, 'seq', split_axis=0, concat_axis=0, tiled=True)  24.2 us
    all_to_all x1, starting transfers between devices, shards(): lax.all_to_all(copies, ('dp', 'seq'), 0, 0, tiled=True)  22.8 us
    all_to_all x1, waiting for transfers between devices, shards(): lax.all_to_all(copies, ('dp', 'seq'), 0, 0, tiled=True)  13.2 us
    psum x1, blocking collectives, shards(): dots = lax.psum(partial_dots, 'tensor')  13.1 us
    dot_general x8, matrix products, times(): lax.dot_general(block, weight, (((1,), (1,)), ((), ())), preferred_elemen...  11.9 us
    ppermute x7, waiting for transfers between devices, turn(): return lax.ppermute(block, ('seq', 'tensor'), pairs)  8.17 us
    all_to_all x2, waiting for transfers between devices, exchange(): lax.all_to_all(parts, 'seq', split_axis=0, concat_axis=0, tiled=True)  3.28 us
  transfers between devices with their start and end apart: 10, of which 6 were waited for; matrix products, arithmetic and copies ran while one was open for 12% of the time, Pallas kernels for 1%

profile of v8, /device:TPU:1, one launch (start us, length us, event | category | flops | bytes accessed | tf_op | source)
XLA Modules:
  0.0 133.8 jit_solution(3990938902859936799)
XLA Ops:
  0.7 5.5 %collective-permute-start = (bf16[512,512]{1,0:T(8,128)(2,1)}, bf16[512,512]{1,0:T(8,128)(2,1)}, u32[]{:S(2)}, u32[]{:S(2)}) collective-permute-start(bf16[512,512]{1,0:T(8,128)(2,1)} %bitcast.38), channel_id=1, source_target_pairs={{0,1},{1,2},{2,3},{3,4},{4,5},{5,6},{6,7},{7,0},{8,15},{9,8},{10,9... | collective-permute-start | bytes 1572872 | tf_op jit(solution)/shard_map/ppermute | solution.py:107
  6.1 1.9 %collective-permute-start.2 = (bf16[512,512]{1,0:T(8,128)(2,1)}, bf16[512,512]{1,0:T(8,128)(2,1)}, u32[]{:S(2)}, u32[]{:S(2)}) collective-permute-start(bf16[512,512]{1,0:T(8,128)(2,1)} %bitcast.39), channel_id=1, source_target_pairs={{0,7},{1,0},{2,1},{3,2},{4,3},{5,4},{6,5},{7,6},{8,9},{9,10},{10,1... | collective-permute-start | bytes 1572872 | tf_op jit(solution)/shard_map/ppermute | solution.py:107
  8.2 1.1 constant_dynamic-slice_fusion
  9.4 0.7 copy-done.3
  10.7 0.7 shard_map.103
  11.4 2.0 %collective-permute-done = bf16[512,512]{1,0:T(8,128)(2,1)} collective-permute-done((bf16[512,512]{1,0:T(8,128)(2,1)}, bf16[512,512]{1,0:T(8,128)(2,1)}, u32[]{:S(2)}, u32[]{:S(2)}) %collective-permute-start) | collective-permute-done | bytes 524320 | tf_op jit(solution)/shard_map/ppermute | solution.py:107
  13.5 5.0 %collective-permute-start.1 = (bf16[512,512]{1,0:T(8,128)(2,1)}, bf16[512,512]{1,0:T(8,128)(2,1)}, u32[]{:S(2)}, u32[]{:S(2)}) collective-permute-start(bf16[512,512]{1,0:T(8,128)(2,1)} %collective-permute-done), channel_id=1, source_target_pairs={{0,1},{1,2},{2,3},{3,4},{4,5},{5,6},{6,7},{7,0},{8,15},{9,8},{10,9... | collective-permute-start | bytes 1572872 | tf_op jit(solution)/shard_map/ppermute | solution.py:107
  18.5 1.7 %fusion.9 = f32[512,512]{1,0:T(8,128)S(1)} fusion(bf16[512,512]{1,0:T(8,128)(2,1)} %collective-permute-done, bf16[512,4096]{1,0:T(8,128)(2,1)} %param.12, s32[]{:T(128)S(6)} %select_n.67), kind=kOutput, calls=%fused_computation.19 | convolution fusion | flops 268435456 | bytes 2097156 | tf_op jit(solution)/shard_map/dot_general | solution.py:115
  20.2 1.9 %collective-permute-start.3 = (bf16[512,512]{1,0:T(8,128)(2,1)}, bf16[512,512]{1,0:T(8,128)(2,1)}, u32[]{:S(2)}, u32[]{:S(2)}) collective-permute-start(bf16[512,512]{1,0:T(8,128)(2,1)} %collective-permute-done.2), channel_id=1, source_target_pairs={{0,7},{1,0},{2,1},{3,2},{4,3},{5,4},{6,5},{7,6},{8,9},{9,10},{10,1... | collective-permute-start | bytes 1572872 | tf_op jit(solution)/shard_map/ppermute | solution.py:107
  22.1 1.7 %convolution_bitcast_fusion.2 = f32[512,512]{1,0:T(8,128)S(1)} fusion(bf16[512,512]{1,0:T(8,128)(2,1)} %collective-permute-done.2, bf16[512,4096]{1,0:T(8,128)(2,1)} %param.12, s32[]{:T(128)S(6)} %select_n.69), kind=kOutput, calls=%fused_computation.7 | convolution fusion | flops 268435456 | bytes 2097156 | tf_op jit(solution)/shard_map/dot_general | solution.py:115
  23.8 1.5 %fusion.2 = f32[512,512]{1,0:T(8,128)S(1)} fusion(f32[512,512]{1,0:T(8,128)S(1)} %convolution_bitcast_fusion.2, f32[512,512]{1,0:T(8,128)S(1)} %fusion.9, bf16[512,512]{1,0:T(8,128)(2,1)S(1)} %bitcast.40, bf16[512,4096]{1,0:T(8,128)(2,1)} %param.12, s32[]{:T(128)S(6)} %select_n.64), kind=kOutput, calls=%fused_computation.9 | convolution fusion | flops 268959744 | bytes 4194308 | tf_op jit(solution)/shard_map/dot_general | solution.py:115
  25.4 1.5 %collective-permute-done.1 = bf16[512,512]{1,0:T(8,128)(2,1)} collective-permute-done((bf16[512,512]{1,0:T(8,128)(2,1)}, bf16[512,512]{1,0:T(8,128)(2,1)}, u32[]{:S(2)}, u32[]{:S(2)}) %collective-permute-start.1) | collective-permute-done | bytes 524320 | tf_op jit(solution)/shard_map/ppermute | solution.py:107
  26.8 5.3 %collective-permute-start.4 = (bf16[512,512]{1,0:T(8,128)(2,1)}, bf16[512,512]{1,0:T(8,128)(2,1)}, u32[]{:S(2)}, u32[]{:S(2)}) collective-permute-start(bf16[512,512]{1,0:T(8,128)(2,1)} %collective-permute-done.1), channel_id=1, source_target_pairs={{0,1},{1,2},{2,3},{3,4},{4,5},{5,6},{6,7},{7,0},{8,15},{9,8},{10,9... | collective-permute-start | bytes 1572872 | tf_op jit(solution)/shard_map/ppermute | solution.py:107
  32.1 1.1 convolution_convert_fusion
  33.3 14.0 %all-to-all-start = ((bf16[16,32,512]{2,1,0:T(8,128)(2,1)}), bf16[16,32,512]{2,1,0:T(8,128)(2,1)S(1)}, u32[]{:S(2)}, u32[]{:S(2)}) async-start(bf16[16,32,512]{2,1,0:T(8,128)(2,1)} %bitcast.4), calls=%async_computation | async-start | bytes 1048576 | tf_op jit(solution)/shard_map/all_to_all | solution.py:133
  47.3 3.1 %collective-permute-start.5 = (bf16[512,512]{1,0:T(8,128)(2,1)}, bf16[512,512]{1,0:T(8,128)(2,1)S(1)}, u32[]{:S(2)}, u32[]{:S(2)}) collective-permute-start(bf16[512,512]{1,0:T(8,128)(2,1)} %collective-permute-done.3), channel_id=1, source_target_pairs={{0,7},{1,0},{2,1},{3,2},{4,3},{5,4},{6,5},{7,6},{8,9},{9,10},{10,1... | collective-permute-start | bytes 1572872 | tf_op jit(solution)/shard_map/ppermute | solution.py:107
  50.4 1.7 %convolution_add_fusion.2 = f32[512,512]{1,0:T(8,128)S(1)} fusion(f32[512,512]{1,0:T(8,128)S(1)} %fusion.2, bf16[512,512]{1,0:T(8,128)(2,1)} %collective-permute-done.1, bf16[512,4096]{1,0:T(8,128)(2,1)} %param.12, s32[]{:T(128)S(6)} %select_n.71), kind=kOutput, calls=%fused_computation.6 | convolution fusion | flops 268697600 | bytes 3145732 | tf_op jit(solution)/shard_map/dot_general | solution.py:115
  52.1 1.7 %fusion.1 = f32[512,512]{1,0:T(8,128)S(1)} fusion(f32[512,512]{1,0:T(8,128)S(1)} %convolution_add_fusion.2, bf16[512,512]{1,0:T(8,128)(2,1)} %collective-permute-done.3, bf16[512,4096]{1,0:T(8,128)(2,1)} %param.12, s32[]{:T(128)S(6)} %select_n.73), kind=kOutput, calls=%fused_computation.5 | convolution fusion | flops 268697600 | bytes 3145732 | tf_op jit(solution)/shard_map/dot_general | solution.py:115
  53.8 3.7 %collective-permute-start.6 = (bf16[512,512]{1,0:T(8,128)(2,1)}, bf16[512,512]{1,0:T(8,128)(2,1)S(1)}, u32[]{:S(2)}, u32[]{:S(2)}) collective-permute-start(bf16[512,512]{1,0:T(8,128)(2,1)} %collective-permute-done.4), channel_id=1, source_target_pairs={{0,1},{1,2},{2,3},{3,4},{4,5},{5,6},{6,7},{7,0},{8,15},{9,8},{10,9... | collective-permute-start | bytes 1572872 | tf_op jit(solution)/shard_map/ppermute | solution.py:107
  57.5 1.7 %convolution_add_fusion.1 = f32[512,512]{1,0:T(8,128)S(1)} fusion(f32[512,512]{1,0:T(8,128)S(1)} %fusion.1, bf16[512,512]{1,0:T(8,128)(2,1)} %collective-permute-done.4, bf16[512,4096]{1,0:T(8,128)(2,1)} %param.12, s32[]{:T(128)S(6)} %select_n.75), kind=kOutput, calls=%fused_computation.3 | convolution fusion | flops 268697600 | bytes 3145732 | tf_op jit(solution)/shard_map/dot_general | solution.py:115
  59.2 1.6 %fusion = f32[512,512]{1,0:T(8,128)S(1)} fusion(f32[512,512]{1,0:T(8,128)S(1)} %convolution_add_fusion.1, bf16[512,512]{1,0:T(8,128)(2,1)S(1)} %collective-permute-done.5, bf16[512,4096]{1,0:T(8,128)(2,1)} %param.12, s32[]{:T(128)S(6)} %select_n.77), kind=kOutput, calls=%fused_computation.2 | convolution fusion | flops 268697600 | bytes 3145732 | tf_op jit(solution)/shard_map/dot_general | solution.py:115
  60.8 4.6 %collective-permute-done.6 = bf16[512,512]{1,0:T(8,128)(2,1)S(1)} collective-permute-done((bf16[512,512]{1,0:T(8,128)(2,1)}, bf16[512,512]{1,0:T(8,128)(2,1)S(1)}, u32[]{:S(2)}, u32[]{:S(2)}) %collective-permute-start.6) | collective-permute-done | bytes 524320 | tf_op jit(solution)/shard_map/ppermute | solution.py:107
  65.9 1.6 %shard_map.104 = (bf16[512,512]{1,0:T(8,128)(2,1)}, f32[1,512]{1,0:T(1,128)S(1)}) custom-call(bf16[512,512]{1,0:T(8,128)(2,1)S(1)} %bitcast.35, s32[1,512]{1,0:T(1,128)S(1)} %get-tuple-element.18.ids_ref, bf16[1,512]{1,0:T(2,128)(2,1)S(1)} %copy-done.2, f32[512,512]{1,0:T(8,128)S(1)} %convolution_add_fusion.back_ref), custom_call_target="tpu_custom_call" | custom-call | flops 536870912 | bytes 2097152 | tf_op jit(solution)/shard_map/pallas_call | solution.py:156
  67.5 10.2 %all-to-all-start.1 = ((bf16[16,32,512]{2,1,0:T(8,128)(2,1)}), bf16[16,32,512]{2,1,0:T(8,128)(2,1)S(1)}, u32[]{:S(2)}, u32[]{:S(2)}) async-start(bf16[16,32,512]{2,1,0:T(8,128)(2,1)} %bitcast.9), calls=%async_computation.1 | async-start | bytes 1048576 | tf_op jit(solution)/shard_map/all_to_all | solution.py:133
  77.7 13.1 %psum.7.dots_ref = f32[1,512]{1,0:T(1,128)S(1)} all-reduce(f32[1,512]{1,0:T(1,128)S(1)} %get-tuple-element.22), channel_id=1, replica_groups=mesh['dp'=8,'seq'=16,'tensor'=8] {'tensor'}, use_global_device_ids=true, to_apply=%region_0.1 | all-reduce | flops 512 | bytes 4096 | tf_op jit(solution)/shard_map/psum | solution.py:167
  90.8 0.9 shard_map.105
  91.7 3.3 %all-to-all-done.1 = bf16[16,32,512]{2,1,0:T(8,128)(2,1)S(1)} async-done(((bf16[16,32,512]{2,1,0:T(8,128)(2,1)}), bf16[16,32,512]{2,1,0:T(8,128)(2,1)S(1)}, u32[]{:S(2)}, u32[]{:S(2)}) %all-to-all-start.1) | async-done | bytes 524320 | tf_op jit(solution)/shard_map/all_to_all | solution.py:133
  95.0 22.8 %all-to-all-start.2 = ((f32[128,1,512]{2,1,0:T(1,128)}), f32[128,1,512]{2,1,0:T(1,128)S(1)}, u32[]{:S(2)}, u32[]{:S(2)}) async-start(f32[128,1,512]{2,1,0:T(1,128)} %get-tuple-element.26), calls=%async_computation.2 | async-start | bytes 524288 | tf_op jit(solution)/shard_map/all_to_all | solution.py:184
  117.8 1.0 add_convert_fusion
  118.8 1.0 fusion.3
  119.8 13.2 %all-to-all-done.2 = f32[128,1,512]{2,1,0:T(1,128)S(1)} async-done(((f32[128,1,512]{2,1,0:T(1,128)}), f32[128,1,512]{2,1,0:T(1,128)S(1)}, u32[]{:S(2)}, u32[]{:S(2)}) %all-to-all-start.2) | async-done | bytes 262176 | tf_op jit(solution)/shard_map/all_to_all | solution.py:184
  133.0 0.8 reduce_sum.9
  (20 shorter events, 1.2 us)
Async XLA Ops:
  0.6 26.2 %copy-start = (bf16[1,256,512]{2,1,0:T(8,128)(2,1)S(1)}, bf16[1,256,512]{2,1,0:T(8,128)(2,1)}, u32[]{:S(2)}) copy-start(bf16[1,256,512]{2,1,0:T(8,128)(2,1)} %param.11) | copy-start | bytes 786436
  0.6 23.2 %copy-start.5 = (bf16[1,512,512]{2,1,0:T(8,128)(2,1)S(1)}, bf16[1,512,512]{2,1,0:T(8,128)(2,1)}, u32[]{:S(2)}) copy-start(bf16[1,512,512]{2,1,0:T(8,128)(2,1)} %param.10) | copy-start | bytes 1572868
  0.7 12.8 %collective-permute-start = (bf16[512,512]{1,0:T(8,128)(2,1)}, bf16[512,512]{1,0:T(8,128)(2,1)}, u32[]{:S(2)}, u32[]{:S(2)}) collective-permute-start(bf16[512,512]{1,0:T(8,128)(2,1)} %bitcast.38), channel_id=1, source_target_pairs={{0,1},{1,2},{2,3},{3,4},{4,5},{5,6},{6,7},{7,0},{8,15},{9,8},{10,9... | collective-permute-start | bytes 1572872 | tf_op jit(solution)/shard_map/ppermute | solution.py:107
  6.1 14.1 %collective-permute-start.2 = (bf16[512,512]{1,0:T(8,128)(2,1)}, bf16[512,512]{1,0:T(8,128)(2,1)}, u32[]{:S(2)}, u32[]{:S(2)}) collective-permute-start(bf16[512,512]{1,0:T(8,128)(2,1)} %bitcast.39), channel_id=1, source_target_pairs={{0,7},{1,0},{2,1},{3,2},{4,3},{5,4},{6,5},{7,6},{8,9},{9,10},{10,1... | collective-permute-start | bytes 1572872 | tf_op jit(solution)/shard_map/ppermute | solution.py:107
  9.3 0.7 copy-start.3
  10.0 0.7 copy-start.4
  13.5 13.4 %collective-permute-start.1 = (bf16[512,512]{1,0:T(8,128)(2,1)}, bf16[512,512]{1,0:T(8,128)(2,1)}, u32[]{:S(2)}, u32[]{:S(2)}) collective-permute-start(bf16[512,512]{1,0:T(8,128)(2,1)} %collective-permute-done), channel_id=1, source_target_pairs={{0,1},{1,2},{2,3},{3,4},{4,5},{5,6},{6,7},{7,0},{8,15},{9,8},{10,9... | collective-permute-start | bytes 1572872 | tf_op jit(solution)/shard_map/ppermute | solution.py:107
  20.2 27.1 %collective-permute-start.3 = (bf16[512,512]{1,0:T(8,128)(2,1)}, bf16[512,512]{1,0:T(8,128)(2,1)}, u32[]{:S(2)}, u32[]{:S(2)}) collective-permute-start(bf16[512,512]{1,0:T(8,128)(2,1)} %collective-permute-done.2), channel_id=1, source_target_pairs={{0,7},{1,0},{2,1},{3,2},{4,3},{5,4},{6,5},{7,6},{8,9},{9,10},{10,1... | collective-permute-start | bytes 1572872 | tf_op jit(solution)/shard_map/ppermute | solution.py:107
  26.8 27.0 %collective-permute-start.4 = (bf16[512,512]{1,0:T(8,128)(2,1)}, bf16[512,512]{1,0:T(8,128)(2,1)}, u32[]{:S(2)}, u32[]{:S(2)}) collective-permute-start(bf16[512,512]{1,0:T(8,128)(2,1)} %collective-permute-done.1), channel_id=1, source_target_pairs={{0,1},{1,2},{2,3},{3,4},{4,5},{5,6},{6,7},{7,0},{8,15},{9,8},{10,9... | collective-permute-start | bytes 1572872 | tf_op jit(solution)/shard_map/ppermute | solution.py:107
  33.3 32.6 %all-to-all-start = ((bf16[16,32,512]{2,1,0:T(8,128)(2,1)}), bf16[16,32,512]{2,1,0:T(8,128)(2,1)S(1)}, u32[]{:S(2)}, u32[]{:S(2)}) async-start(bf16[16,32,512]{2,1,0:T(8,128)(2,1)} %bitcast.4), calls=%async_computation | async-start | bytes 1048576 | tf_op jit(solution)/shard_map/all_to_all | solution.py:133
  47.3 11.9 %collective-permute-start.5 = (bf16[512,512]{1,0:T(8,128)(2,1)}, bf16[512,512]{1,0:T(8,128)(2,1)S(1)}, u32[]{:S(2)}, u32[]{:S(2)}) collective-permute-start(bf16[512,512]{1,0:T(8,128)(2,1)} %collective-permute-done.3), channel_id=1, source_target_pairs={{0,7},{1,0},{2,1},{3,2},{4,3},{5,4},{6,5},{7,6},{8,9},{9,10},{10,1... | collective-permute-start | bytes 1572872 | tf_op jit(solution)/shard_map/ppermute | solution.py:107
  53.8 12.1 %copy-start.2 = (bf16[1,512]{1,0:T(2,128)(2,1)S(1)}, bf16[1,512]{1,0:T(2,128)(2,1)}, u32[]{:S(2)}) copy-start(bf16[1,512]{1,0:T(2,128)(2,1)} %logits_ref.3) | copy-start | bytes 3076
  53.8 11.6 %collective-permute-start.6 = (bf16[512,512]{1,0:T(8,128)(2,1)}, bf16[512,512]{1,0:T(8,128)(2,1)S(1)}, u32[]{:S(2)}, u32[]{:S(2)}) collective-permute-start(bf16[512,512]{1,0:T(8,128)(2,1)} %collective-permute-done.4), channel_id=1, source_target_pairs={{0,1},{1,2},{2,3},{3,4},{4,5},{5,6},{6,7},{7,0},{8,15},{9,8},{10,9... | collective-permute-start | bytes 1572872 | tf_op jit(solution)/shard_map/ppermute | solution.py:107
  59.2 31.6 %copy-start.1 = (bf16[1,512,512]{2,1,0:T(8,128)(2,1)S(1)}, bf16[1,512,512]{2,1,0:T(8,128)(2,1)}, u32[]{:S(2)}) copy-start(bf16[1,512,512]{2,1,0:T(8,128)(2,1)} %param.8) | copy-start | bytes 1572868
  60.8 57.0 %copy-start.6 = (f32[512]{0:T(512)S(1)}, f32[512]{0:T(512)}, u32[]{:S(2)}) copy-start(f32[512]{0:T(512)} %param.13) | copy-start | bytes 6148
  67.5 27.5 %all-to-all-start.1 = ((bf16[16,32,512]{2,1,0:T(8,128)(2,1)}), bf16[16,32,512]{2,1,0:T(8,128)(2,1)S(1)}, u32[]{:S(2)}, u32[]{:S(2)}) async-start(bf16[16,32,512]{2,1,0:T(8,128)(2,1)} %bitcast.9), calls=%async_computation.1 | async-start | bytes 1048576 | tf_op jit(solution)/shard_map/all_to_all | solution.py:133
  95.0 38.0 %all-to-all-start.2 = ((f32[128,1,512]{2,1,0:T(1,128)}), f32[128,1,512]{2,1,0:T(1,128)S(1)}, u32[]{:S(2)}, u32[]{:S(2)}) async-start(f32[128,1,512]{2,1,0:T(1,128)} %get-tuple-element.26), calls=%async_computation.2 | async-start | bytes 524288 | tf_op jit(solution)/shard_map/all_to_all | solution.py:184

commit v9 on v7

--- a/solution.py
+++ b/solution.py
@@ -64,14 +64,17 @@
     return jax.nn.sigmoid(logits_ref[...].astype(jnp.float32))
 
 
-def finish_kernel(att_ref, ids_ref, logits_ref, back_ref, slots_ref, dots_ref):
+def finish_kernel(
+    att_ref, ids_ref, logits_ref, sum_ref, last_ref, weight_ref, slots_ref, dots_ref
+):
     tok = ids_ref.shape[1]
     table = lax.broadcasted_iota(jnp.int32, (tok, tok), 0) == ids_ref[...]
     table = jnp.where(table, 1.0, 0.0).astype(jnp.bfloat16)
-    att_tok = lax.dot_general(
-        table, att_ref[...], (((0,), (0,)), ((), ())), preferred_element_type=jnp.float32
-    )
-    back = back_ref[...]
+    att_tok = att_ref[...].astype(jnp.float32)
+    back = sum_ref[...] + lax.dot_general(
+        last_ref[...], weight_ref[...], (((1,), (1,)), ((), ())),
+        preferred_element_type=jnp.float32,
+    )
     column = jnp.sum(att_tok * back, axis=1, keepdims=True)
     dots_ref[...] = jnp.broadcast_to(column, (tok, 128)).T[0:1]
     rate = jnp.broadcast_to(rate_of(logits_ref), (128, tok)).T[:, 0:1]
@@ -118,11 +121,13 @@
         ]
         return lax.ppermute(block, ("seq", "tensor"), pairs)
 
+    def weight_of(step):
+        start = (column + step * flip) % nten * width
+        return lax.dynamic_slice(out_weight, (0, start), (heads_width, width))
+
     def times(block, step):
-        start = (column + step * flip) % nten * width
-        weight = lax.dynamic_slice(out_weight, (0, start), (heads_width, width))
         return lax.dot_general(
-            block, weight, (((1,), (1,)), ((), ())), preferred_element_type=jnp.float32
+            block, weight_of(step), (((1,), (1,)), ((), ())), preferred_element_type=jnp.float32
         )
 
     slots_shape = jax.ShapeDtypeStruct((tok, heads_width), jnp.bfloat16)
@@ -160,18 +165,24 @@
             product = times(own, 0)
         product = product + times(first_in, -step) + times(second_in, step)
     last_in = turn(first_in, 1)
-    product = product + times(last_in, nten // 2)
+    slot_table = (jnp.arange(tok, dtype=jnp.int32)[:, None] == slot_ids).astype(jnp.bfloat16)
+    att_tok = lax.dot_general(
+        slot_table, att_in, (((0,), (0,)), ((), ())), preferred_element_type=jnp.float32
+    ).astype(jnp.bfloat16)
+    product, att_tok, last_weight = lax.optimization_barrier(
+        (product, att_tok, weight_of(nten // 2))
+    )
 
     grad_slots, partial_dots = pl.pallas_call(
         finish_kernel,
         out_shape=(slots_shape, jax.ShapeDtypeStruct((1, tok), jnp.float32)),
-        in_specs=[VMEM] * 4,
+        in_specs=[VMEM] * 6,
         out_specs=(VMEM, VMEM),
         compiler_params=PARAMS,
         cost_estimate=pl.CostEstimate(
             flops=4 * tok * tok * heads_width, bytes_accessed=2**21, transcendentals=0
         ),
-    )(att_in, slot_ids, logits, product)
+    )(att_tok, slot_ids, logits, product, last_in, last_weight)
     grad_in = exchange(grad_slots)
     dots = lax.psum(partial_dots, "tensor")
     group = lax.axis_size("dp") * nseq

time: 130 us -> 135 us (1.038)
  matrix products: 6.91 us -> 13.5 us
  starting transfers between devices: 68.4 us -> 62.8 us
  waiting for transfers between devices: 33.2 us -> 34.8 us
    dot_general x8, matrix products: 5.89 us -> 12.5 us  [the longest x7 11 us: times(): lax.dot_general(block, weight_of(step), (((1,), (1,)), ((), ())), preferr...]
    all_to_all x2, waiting for transfers between devices: 4.53 us -> 11 us  [exchange(): lax.all_to_all(parts, 'seq', split_axis=0, concat_axis=0, tiled=True)]
    ppermute x7, waiting for transfers between devices: 15.4 us -> 10.5 us  [turn(): return lax.ppermute(block, ('seq', 'tensor'), pairs)]
    all_to_all x2, starting transfers between devices: 33.7 us -> 30.3 us  [exchange(): lax.all_to_all(parts, 'seq', split_axis=0, concat_axis=0, tiled=True)]
    ppermute x7, starting transfers between devices: 21.2 us -> 19.7 us  [turn(): return lax.ppermute(block, ('seq', 'tensor'), pairs)]
  transfers between devices with their start and end apart: 10 -> 10, of which waited for: 7 -> 5; matrix products, arithmetic and copies ran while one was open for 6% -> 12% of each run, Pallas kernels for 2% -> 2%
where the time goes in v9:
time: 135 us; the launch traced here: 134 us
  starting transfers between devices  62.8 us (47%)
  waiting for transfers between devices  34.8 us (26%)
  matrix products  13.5 us (10%)
  blocking collectives  11.8 us (9%)
  Pallas kernels  4.51 us (3%)
  local copies, waits for them, and re-layouts  3.38 us (3%)
  other arithmetic  1.78 us (1%)
    all_to_all x2, starting transfers between devices, exchange(): lax.all_to_all(parts, 'seq', split_axis=0, concat_axis=0, tiled=True)  30.3 us
    ppermute x7, starting transfers between devices, turn(): return lax.ppermute(block, ('seq', 'tensor'), pairs)  19.7 us
    all_to_all x1, waiting for transfers between devices, shards(): lax.all_to_all(copies, ('dp', 'seq'), 0, 0, tiled=True)  13.2 us
    all_to_all x1, starting transfers between devices, shards(): lax.all_to_all(copies, ('dp', 'seq'), 0, 0, tiled=True)  12.8 us
    psum x1, blocking collectives, shards(): dots = lax.psum(partial_dots, 'tensor')  11.8 us
    all_to_all x2, waiting for transfers between devices, exchange(): lax.all_to_all(parts, 'seq', split_axis=0, concat_axis=0, tiled=True)  11 us
    dot_general x7, matrix products, times(): lax.dot_general(block, weight_of(step), (((1,), (1,)), ((), ())), preferr...  11 us
    ppermute x7, waiting for transfers between devices, turn(): return lax.ppermute(block, ('seq', 'tensor'), pairs)  10.5 us
  transfers between devices with their start and end apart: 10, of which 5 were waited for; matrix products, arithmetic and copies ran while one was open for 12% of the time, Pallas kernels for 2%

profile of v9, /device:TPU:1, one launch (start us, length us, event | category | flops | bytes accessed | tf_op | source)
XLA Modules:
  0.0 133.5 jit_solution(14100310694780696317)
XLA Ops:
  0.6 5.3 %collective-permute-start = (bf16[512,512]{1,0:T(8,128)(2,1)}, bf16[512,512]{1,0:T(8,128)(2,1)S(1)}, u32[]{:S(2)}, u32[]{:S(2)}) collective-permute-start(bf16[512,512]{1,0:T(8,128)(2,1)} %bitcast.36), channel_id=1, source_target_pairs={{0,1},{1,2},{2,3},{3,4},{4,5},{5,6},{6,7},{7,0},{8,15},{9,8},{10,9... | collective-permute-start | bytes 1572872 | tf_op jit(solution)/shard_map/ppermute | solution.py:122
  6.0 1.9 %collective-permute-start.1 = (bf16[512,512]{1,0:T(8,128)(2,1)}, bf16[512,512]{1,0:T(8,128)(2,1)S(1)}, u32[]{:S(2)}, u32[]{:S(2)}) collective-permute-start(bf16[512,512]{1,0:T(8,128)(2,1)} %bitcast.37), channel_id=1, source_target_pairs={{0,7},{1,0},{2,1},{3,2},{4,3},{5,4},{6,5},{7,6},{8,9},{9,10},{10,1... | collective-permute-start | bytes 1572872 | tf_op jit(solution)/shard_map/ppermute | solution.py:122
  7.9 0.9 copy-done.2
  10.2 1.9 %shard_map.103 = (bf16[512,512]{1,0:T(8,128)(2,1)}, s32[1,512]{1,0:T(1,128)S(1)}, s32[1,512]{1,0:T(1,128)S(1)}) custom-call(s32[1]{0:T(128)} %bitcast.here_ref, s32[1,16]{1,0:T(1,128)S(1)} %copy-done.4, s32[1,512]{1,0:T(1,128)S(1)} %copy-done.3, bf16[256,512]{1,0:T(8,128)(2,1)S(1)} %bitcast.35), custom_call_target="tpu_custom_call" | custom-call | flops 134217728 | bytes 1048576 | tf_op jit(solution)/shard_map/pallas_call | solution.py:135
  12.1 17.9 %all-to-all-start = ((bf16[16,32,512]{2,1,0:T(8,128)(2,1)}), bf16[16,32,512]{2,1,0:T(8,128)(2,1)}, u32[]{:S(2)}, u32[]{:S(2)}) async-start(bf16[16,32,512]{2,1,0:T(8,128)(2,1)} %bitcast.8), calls=%async_computation | async-start | bytes 1048576 | tf_op jit(solution)/shard_map/all_to_all | solution.py:152
  30.0 1.1 constant_dynamic-slice_fusion.weight_ref
  31.1 1.9 %collective-permute-start.2 = (bf16[512,512]{1,0:T(8,128)(2,1)S(1)}, bf16[512,512]{1,0:T(8,128)(2,1)}, u32[]{:S(2)}, u32[]{:S(2)}) collective-permute-start(bf16[512,512]{1,0:T(8,128)(2,1)S(1)} %collective-permute-done), channel_id=1, source_target_pairs={{0,1},{1,2},{2,3},{3,4},{4,5},{5,6},{6,7},{7,0},{8,15},{9,8},{10,9... | collective-permute-start | bytes 1572872 | tf_op jit(solution)/shard_map/ppermute | solution.py:122
  33.1 3.4 %collective-permute-start.3 = (bf16[512,512]{1,0:T(8,128)(2,1)S(1)}, bf16[512,512]{1,0:T(8,128)(2,1)}, u32[]{:S(2)}, u32[]{:S(2)}) collective-permute-start(bf16[512,512]{1,0:T(8,128)(2,1)S(1)} %collective-permute-done.1), channel_id=1, source_target_pairs={{0,7},{1,0},{2,1},{3,2},{4,3},{5,4},{6,5},{7,6},{8,9},{9,10},{10,1... | collective-permute-start | bytes 1572872 | tf_op jit(solution)/shard_map/ppermute | solution.py:122
  36.4 1.5 %fusion.10 = f32[512,512]{1,0:T(8,128)S(1)} fusion(bf16[512,512]{1,0:T(8,128)(2,1)S(1)} %collective-permute-done, bf16[512,4096]{1,0:T(8,128)(2,1)} %param.12, s32[]{:T(128)S(6)} %select_n.67), kind=kOutput, calls=%fused_computation.20 | convolution fusion | flops 268435456 | bytes 2097156 | tf_op jit(solution)/shard_map/dot_general | solution.py:129
  37.9 1.5 %convolution_bitcast_fusion.2 = f32[512,512]{1,0:T(8,128)S(1)} fusion(bf16[512,512]{1,0:T(8,128)(2,1)S(1)} %collective-permute-done.1, bf16[512,4096]{1,0:T(8,128)(2,1)} %param.12, s32[]{:T(128)S(6)} %select_n.69), kind=kOutput, calls=%fused_computation.6 | convolution fusion | flops 268435456 | bytes 2097156 | tf_op jit(solution)/shard_map/dot_general | solution.py:129
  39.5 1.5 %fusion.2 = f32[512,512]{1,0:T(8,128)S(1)} fusion(f32[512,512]{1,0:T(8,128)S(1)} %convolution_bitcast_fusion.2, f32[512,512]{1,0:T(8,128)S(1)} %fusion.10, bf16[512,512]{1,0:T(8,128)(2,1)S(1)} %bitcast.38, bf16[512,4096]{1,0:T(8,128)(2,1)} %param.12, s32[]{:T(128)S(6)} %select_n.64), kind=kOutput, calls=%fused_computation.8 | convolution fusion | flops 268959744 | bytes 4194308 | tf_op jit(solution)/shard_map/dot_general | solution.py:129
  41.0 6.5 %all-to-all-done = bf16[16,32,512]{2,1,0:T(8,128)(2,1)} async-done(((bf16[16,32,512]{2,1,0:T(8,128)(2,1)}), bf16[16,32,512]{2,1,0:T(8,128)(2,1)}, u32[]{:S(2)}, u32[]{:S(2)}) %all-to-all-start) | async-done | bytes 524320 | tf_op jit(solution)/shard_map/all_to_all | solution.py:152
  47.5 1.5 %convolution_convert_fusion.att_ref = bf16[512,512]{1,0:T(8,128)(2,1)S(1)} fusion(bf16[512,512]{1,0:T(8,128)(2,1)} %bitcast.9, s32[512]{0:T(512)S(1)} %bitcast.34), kind=kOutput, calls=%fused_computation.9 | convolution fusion | flops 268959744 | bytes 1050624 | tf_op jit(solution)/shard_map/dot_general | solution.py:169
  49.0 1.9 %collective-permute-start.4 = (bf16[512,512]{1,0:T(8,128)(2,1)}, bf16[512,512]{1,0:T(8,128)(2,1)S(1)}, u32[]{:S(2)}, u32[]{:S(2)}) collective-permute-start(bf16[512,512]{1,0:T(8,128)(2,1)} %collective-permute-done.2), channel_id=1, source_target_pairs={{0,1},{1,2},{2,3},{3,4},{4,5},{5,6},{6,7},{7,0},{8,15},{9,8},{10,9... | collective-permute-start | bytes 1572872 | tf_op jit(solution)/shard_map/ppermute | solution.py:122
  51.0 3.4 %collective-permute-start.5 = (bf16[512,512]{1,0:T(8,128)(2,1)}, bf16[512,512]{1,0:T(8,128)(2,1)S(1)}, u32[]{:S(2)}, u32[]{:S(2)}) collective-permute-start(bf16[512,512]{1,0:T(8,128)(2,1)} %collective-permute-done.3), channel_id=1, source_target_pairs={{0,7},{1,0},{2,1},{3,2},{4,3},{5,4},{6,5},{7,6},{8,9},{9,10},{10,1... | collective-permute-start | bytes 1572872 | tf_op jit(solution)/shard_map/ppermute | solution.py:122
  54.3 1.7 %convolution_add_fusion.1 = f32[512,512]{1,0:T(8,128)S(1)} fusion(f32[512,512]{1,0:T(8,128)S(1)} %fusion.2, bf16[512,512]{1,0:T(8,128)(2,1)} %collective-permute-done.2, bf16[512,4096]{1,0:T(8,128)(2,1)} %param.12, s32[]{:T(128)S(6)} %select_n.71), kind=kOutput, calls=%fused_computation.5 | convolution fusion | flops 268697600 | bytes 3145732 | tf_op jit(solution)/shard_map/dot_general | solution.py:129
  56.0 1.7 %fusion.1 = f32[512,512]{1,0:T(8,128)S(1)} fusion(f32[512,512]{1,0:T(8,128)S(1)} %convolution_add_fusion.1, bf16[512,512]{1,0:T(8,128)(2,1)} %collective-permute-done.3, bf16[512,4096]{1,0:T(8,128)(2,1)} %param.12, s32[]{:T(128)S(6)} %select_n.73), kind=kOutput, calls=%fused_computation.4 | convolution fusion | flops 268697600 | bytes 3145732 | tf_op jit(solution)/shard_map/dot_general | solution.py:129
  57.7 5.4 %collective-permute-done.4 = bf16[512,512]{1,0:T(8,128)(2,1)S(1)} collective-permute-done((bf16[512,512]{1,0:T(8,128)(2,1)}, bf16[512,512]{1,0:T(8,128)(2,1)S(1)}, u32[]{:S(2)}, u32[]{:S(2)}) %collective-permute-start.4) | collective-permute-done | bytes 524320 | tf_op jit(solution)/shard_map/ppermute | solution.py:122
  63.1 1.9 %collective-permute-start.6 = (bf16[512,512]{1,0:T(8,128)(2,1)S(1)}, bf16[512,512]{1,0:T(8,128)(2,1)S(1)}, u32[]{:S(2)}, u32[]{:S(2)}) collective-permute-start(bf16[512,512]{1,0:T(8,128)(2,1)S(1)} %collective-permute-done.4), channel_id=1, source_target_pairs={{0,1},{1,2},{2,3},{3,4},{4,5},{5,6},{6,7},{7,0},{8,15},{9,8},{10,9... | collective-permute-start | bytes 1572872 | tf_op jit(solution)/shard_map/ppermute | solution.py:122
  65.0 1.5 %convolution_add_fusion = f32[512,512]{1,0:T(8,128)S(1)} fusion(f32[512,512]{1,0:T(8,128)S(1)} %fusion.1, bf16[512,512]{1,0:T(8,128)(2,1)S(1)} %collective-permute-done.4, bf16[512,4096]{1,0:T(8,128)(2,1)} %param.12, s32[]{:T(128)S(6)} %select_n.75), kind=kOutput, calls=%fused_computation.2 | convolution fusion | flops 268697600 | bytes 3145732 | tf_op jit(solution)/shard_map/dot_general | solution.py:129
  66.6 1.6 %fusion.sum_ref = f32[512,512]{1,0:T(8,128)S(1)} fusion(f32[512,512]{1,0:T(8,128)S(1)} %convolution_add_fusion, bf16[512,512]{1,0:T(8,128)(2,1)S(1)} %collective-permute-done.5, bf16[512,4096]{1,0:T(8,128)(2,1)} %param.12, s32[]{:T(128)S(6)} %select_n.77), kind=kOutput, calls=%fused_computation.1 | convolution fusion | flops 268697600 | bytes 3145732 | tf_op jit(solution)/shard_map/dot_general | solution.py:129
  68.1 5.2 %collective-permute-done.6.last_ref = bf16[512,512]{1,0:T(8,128)(2,1)S(1)} collective-permute-done((bf16[512,512]{1,0:T(8,128)(2,1)S(1)}, bf16[512,512]{1,0:T(8,128)(2,1)S(1)}, u32[]{:S(2)}, u32[]{:S(2)}) %collective-permute-start.6) | collective-permute-done | bytes 524320 | tf_op jit(solution)/shard_map/ppermute | solution.py:122
  73.3 1.7 %shard_map.104 = (bf16[512,512]{1,0:T(8,128)(2,1)}, f32[1,512]{1,0:T(1,128)S(1)}) custom-call(bf16[512,512]{1,0:T(8,128)(2,1)S(1)} %convolution_convert_fusion.att_ref, s32[1,512]{1,0:T(1,128)S(1)} %get-tuple-element.20.ids_ref, bf16[1,512]{1,0:T(2,128)(2,1)S(1)} %copy-done.1, f32[512,512]{1,0:T(8,128)S(1)} %fusion.sum_ref, ...), custom_call_target="tpu_custom_call" | custom-call | flops 536870912 | bytes 2097152 | tf_op jit(solution)/shard_map/pallas_call | solution.py:176
  75.0 12.3 %all-to-all-start.1 = ((bf16[16,32,512]{2,1,0:T(8,128)(2,1)}), bf16[16,32,512]{2,1,0:T(8,128)(2,1)S(1)}, u32[]{:S(2)}, u32[]{:S(2)}) async-start(bf16[16,32,512]{2,1,0:T(8,128)(2,1)} %bitcast.10), calls=%async_computation.1 | async-start | bytes 1048576 | tf_op jit(solution)/shard_map/all_to_all | solution.py:152
  87.3 11.8 %psum.7.dots_ref = f32[1,512]{1,0:T(1,128)S(1)} all-reduce(f32[1,512]{1,0:T(1,128)S(1)} %get-tuple-element.26), channel_id=1, replica_groups=mesh['dp'=8,'seq'=16,'tensor'=8] {'tensor'}, use_global_device_ids=true, to_apply=%region_0.1 | all-reduce | flops 512 | bytes 4096 | tf_op jit(solution)/shard_map/psum | solution.py:187
  99.2 0.9 shard_map.105
  100.1 4.5 %all-to-all-done.1 = bf16[16,32,512]{2,1,0:T(8,128)(2,1)S(1)} async-done(((bf16[16,32,512]{2,1,0:T(8,128)(2,1)}), bf16[16,32,512]{2,1,0:T(8,128)(2,1)S(1)}, u32[]{:S(2)}, u32[]{:S(2)}) %all-to-all-start.1) | async-done | bytes 524320 | tf_op jit(solution)/shard_map/all_to_all | solution.py:152
  104.6 12.8 %all-to-all-start.2 = ((f32[128,1,512]{2,1,0:T(1,128)}), f32[128,1,512]{2,1,0:T(1,128)S(1)}, u32[]{:S(2)}, u32[]{:S(2)}) async-start(f32[128,1,512]{2,1,0:T(1,128)} %get-tuple-element.30), calls=%async_computation.2 | async-start | bytes 524288 | tf_op jit(solution)/shard_map/all_to_all | solution.py:204
  117.5 1.0 add_convert_fusion
  118.5 1.0 fusion.3
  119.5 13.2 %all-to-all-done.2 = f32[128,1,512]{2,1,0:T(1,128)S(1)} async-done(((f32[128,1,512]{2,1,0:T(1,128)}), f32[128,1,512]{2,1,0:T(1,128)S(1)}, u32[]{:S(2)}, u32[]{:S(2)}) %all-to-all-start.2) | async-done | bytes 262176 | tf_op jit(solution)/shard_map/all_to_all | solution.py:204
  132.7 0.8 reduce_sum.9
  (19 shorter events, 1.4 us)
Async XLA Ops:
  0.6 30.5 %collective-permute-start = (bf16[512,512]{1,0:T(8,128)(2,1)}, bf16[512,512]{1,0:T(8,128)(2,1)S(1)}, u32[]{:S(2)}, u32[]{:S(2)}) collective-permute-start(bf16[512,512]{1,0:T(8,128)(2,1)} %bitcast.36), channel_id=1, source_target_pairs={{0,1},{1,2},{2,3},{3,4},{4,5},{5,6},{6,7},{7,0},{8,15},{9,8},{10,9... | collective-permute-start | bytes 1572872 | tf_op jit(solution)/shard_map/ppermute | solution.py:122
  6.0 27.1 %collective-permute-start.1 = (bf16[512,512]{1,0:T(8,128)(2,1)}, bf16[512,512]{1,0:T(8,128)(2,1)S(1)}, u32[]{:S(2)}, u32[]{:S(2)}) collective-permute-start(bf16[512,512]{1,0:T(8,128)(2,1)} %bitcast.37), channel_id=1, source_target_pairs={{0,7},{1,0},{2,1},{3,2},{4,3},{5,4},{6,5},{7,6},{8,9},{9,10},{10,1... | collective-permute-start | bytes 1572872 | tf_op jit(solution)/shard_map/ppermute | solution.py:122
  7.9 1.0 copy-start.2
  8.9 0.7 copy-start.3
  9.5 0.7 copy-start.4
  10.2 29.3 %copy-start.5 = (bf16[1,512,512]{2,1,0:T(8,128)(2,1)S(1)}, bf16[1,512,512]{2,1,0:T(8,128)(2,1)}, u32[]{:S(2)}) copy-start(bf16[1,512,512]{2,1,0:T(8,128)(2,1)} %param.10) | copy-start | bytes 1572868
  12.1 35.4 %all-to-all-start = ((bf16[16,32,512]{2,1,0:T(8,128)(2,1)}), bf16[16,32,512]{2,1,0:T(8,128)(2,1)}, u32[]{:S(2)}, u32[]{:S(2)}) async-start(bf16[16,32,512]{2,1,0:T(8,128)(2,1)} %bitcast.8), calls=%async_computation | async-start | bytes 1048576 | tf_op jit(solution)/shard_map/all_to_all | solution.py:152
  31.1 17.9 %collective-permute-start.2 = (bf16[512,512]{1,0:T(8,128)(2,1)S(1)}, bf16[512,512]{1,0:T(8,128)(2,1)}, u32[]{:S(2)}, u32[]{:S(2)}) collective-permute-start(bf16[512,512]{1,0:T(8,128)(2,1)S(1)} %collective-permute-done), channel_id=1, source_target_pairs={{0,1},{1,2},{2,3},{3,4},{4,5},{5,6},{6,7},{7,0},{8,15},{9,8},{10,9... | collective-permute-start | bytes 1572872 | tf_op jit(solution)/shard_map/ppermute | solution.py:122
  33.1 17.9 %collective-permute-start.3 = (bf16[512,512]{1,0:T(8,128)(2,1)S(1)}, bf16[512,512]{1,0:T(8,128)(2,1)}, u32[]{:S(2)}, u32[]{:S(2)}) collective-permute-start(bf16[512,512]{1,0:T(8,128)(2,1)S(1)} %collective-permute-done.1), channel_id=1, source_target_pairs={{0,7},{1,0},{2,1},{3,2},{4,3},{5,4},{6,5},{7,6},{8,9},{9,10},{10,1... | collective-permute-start | bytes 1572872 | tf_op jit(solution)/shard_map/ppermute | solution.py:122
  49.0 14.1 %collective-permute-start.4 = (bf16[512,512]{1,0:T(8,128)(2,1)}, bf16[512,512]{1,0:T(8,128)(2,1)S(1)}, u32[]{:S(2)}, u32[]{:S(2)}) collective-permute-start(bf16[512,512]{1,0:T(8,128)(2,1)} %collective-permute-done.2), channel_id=1, source_target_pairs={{0,1},{1,2},{2,3},{3,4},{4,5},{5,6},{6,7},{7,0},{8,15},{9,8},{10,9... | collective-permute-start | bytes 1572872 | tf_op jit(solution)/shard_map/ppermute | solution.py:122
  51.0 15.6 %collective-permute-start.5 = (bf16[512,512]{1,0:T(8,128)(2,1)}, bf16[512,512]{1,0:T(8,128)(2,1)S(1)}, u32[]{:S(2)}, u32[]{:S(2)}) collective-permute-start(bf16[512,512]{1,0:T(8,128)(2,1)} %collective-permute-done.3), channel_id=1, source_target_pairs={{0,7},{1,0},{2,1},{3,2},{4,3},{5,4},{6,5},{7,6},{8,9},{9,10},{10,1... | collective-permute-start | bytes 1572872 | tf_op jit(solution)/shard_map/ppermute | solution.py:122
  56.0 17.3 %copy-start.1 = (bf16[1,512]{1,0:T(2,128)(2,1)S(1)}, bf16[1,512]{1,0:T(2,128)(2,1)}, u32[]{:S(2)}) copy-start(bf16[1,512]{1,0:T(2,128)(2,1)} %logits_ref.3) | copy-start | bytes 3076
  63.1 10.2 %collective-permute-start.6 = (bf16[512,512]{1,0:T(8,128)(2,1)S(1)}, bf16[512,512]{1,0:T(8,128)(2,1)S(1)}, u32[]{:S(2)}, u32[]{:S(2)}) collective-permute-start(bf16[512,512]{1,0:T(8,128)(2,1)S(1)} %collective-permute-done.4), channel_id=1, source_target_pairs={{0,1},{1,2},{2,3},{3,4},{4,5},{5,6},{6,7},{7,0},{8,15},{9,8},{10,9... | collective-permute-start | bytes 1572872 | tf_op jit(solution)/shard_map/ppermute | solution.py:122
  66.5 32.6 %copy-start = (bf16[1,512,512]{2,1,0:T(8,128)(2,1)S(1)}, bf16[1,512,512]{2,1,0:T(8,128)(2,1)}, u32[]{:S(2)}) copy-start(bf16[1,512,512]{2,1,0:T(8,128)(2,1)} %param.8) | copy-start | bytes 1572868
  66.5 50.9 %copy-start.6 = (f32[512]{0:T(512)S(1)}, f32[512]{0:T(512)}, u32[]{:S(2)}) copy-start(f32[512]{0:T(512)} %param.13) | copy-start | bytes 6148
  75.0 29.7 %all-to-all-start.1 = ((bf16[16,32,512]{2,1,0:T(8,128)(2,1)}), bf16[16,32,512]{2,1,0:T(8,128)(2,1)S(1)}, u32[]{:S(2)}, u32[]{:S(2)}) async-start(bf16[16,32,512]{2,1,0:T(8,128)(2,1)} %bitcast.10), calls=%async_computation.1 | async-start | bytes 1048576 | tf_op jit(solution)/shard_map/all_to_all | solution.py:152
  104.6 28.1 %all-to-all-start.2 = ((f32[128,1,512]{2,1,0:T(1,128)}), f32[128,1,512]{2,1,0:T(1,128)S(1)}, u32[]{:S(2)}, u32[]{:S(2)}) async-start(f32[128,1,512]{2,1,0:T(1,128)} %get-tuple-element.30), calls=%async_computation.2 | async-start | bytes 524288 | tf_op jit(solution)/shard_map/all_to_all | solution.py:204

commit v10 on v9

--- a/solution.py
+++ b/solution.py
@@ -121,9 +121,9 @@
         ]
         return lax.ppermute(block, ("seq", "tensor"), pairs)
 
-    def weight_of(step):
+    def weight_of(step, weight=out_weight):
         start = (column + step * flip) % nten * width
-        return lax.dynamic_slice(out_weight, (0, start), (heads_width, width))
+        return lax.dynamic_slice(weight, (0, start), (heads_width, width))
 
     def times(block, step):
         return lax.dot_general(
@@ -164,13 +164,14 @@
             own, first_in = lax.optimization_barrier((own, first_in))
             product = times(own, 0)
         product = product + times(first_in, -step) + times(second_in, step)
+    att_in, late_weight, first_in = lax.optimization_barrier((att_in, out_weight, first_in))
     last_in = turn(first_in, 1)
     slot_table = (jnp.arange(tok, dtype=jnp.int32)[:, None] == slot_ids).astype(jnp.bfloat16)
     att_tok = lax.dot_general(
         slot_table, att_in, (((0,), (0,)), ((), ())), preferred_element_type=jnp.float32
     ).astype(jnp.bfloat16)
     product, att_tok, last_weight = lax.optimization_barrier(
-        (product, att_tok, weight_of(nten // 2))
+        (product, att_tok, weight_of(nten // 2, late_weight))
     )
 
     grad_slots, partial_dots = pl.pallas_call(

time: 135 us -> 130 us (0.963)
  waiting for transfers between devices: 34.8 us -> 26.1 us
  starting transfers between devices: 62.8 us -> 68.4 us
    all_to_all x2, waiting for transfers between devices: 11 us -> 4.54 us  [exchange(): lax.all_to_all(parts, 'seq', split_axis=0, concat_axis=0, tiled=True)]
    all_to_all x2, starting transfers between devices: 30.3 us -> 34.1 us  [exchange(): lax.all_to_all(parts, 'seq', split_axis=0, concat_axis=0, tiled=True)]
    ppermute x7, waiting for transfers between devices: 10.5 us -> 8.37 us  [turn(): return lax.ppermute(block, ('seq', 'tensor'), pairs)]
  transfers between devices with their start and end apart: 10 -> 10, of which waited for: 5 -> 6; matrix products, arithmetic and copies ran while one was open for 12% -> 11% of each run, Pallas kernels for 2% -> 2%
where the time goes in v10:
time: 130 us; the launch traced here: 129 us
  starting transfers between devices  68.4 us (53%)
  waiting for transfers between devices  26.1 us (20%)
  matrix products  12.4 us (10%)
  blocking collectives  11.8 us (9%)
  Pallas kernels  4.51 us (3%)
  local copies, waits for them, and re-layouts  3.38 us (3%)
  other arithmetic  1.78 us (1%)
    all_to_all x2, starting transfers between devices, exchange(): lax.all_to_all(parts, 'seq', split_axis=0, concat_axis=0, tiled=True)  34.1 us
    ppermute x7, starting transfers between devices, turn(): return lax.ppermute(block, ('seq', 'tensor'), pairs)  20.9 us
    all_to_all x1, starting transfers between devices, shards(): lax.all_to_all(copies, ('dp', 'seq'), 0, 0, tiled=True)  13.4 us
    all_to_all x1, waiting for transfers between devices, shards(): lax.all_to_all(copies, ('dp', 'seq'), 0, 0, tiled=True)  13.2 us
    psum x1, blocking collectives, shards(): dots = lax.psum(partial_dots, 'tensor')  11.8 us
    dot_general x7, matrix products, times(): lax.dot_general(block, weight_of(step), (((1,), (1,)), ((), ())), preferr...  10.9 us
    ppermute x7, waiting for transfers between devices, turn(): return lax.ppermute(block, ('seq', 'tensor'), pairs)  8.37 us
    all_to_all x2, waiting for transfers between devices, exchange(): lax.all_to_all(parts, 'seq', split_axis=0, concat_axis=0, tiled=True)  4.54 us
  transfers between devices with their start and end apart: 10, of which 6 were waited for; matrix products, arithmetic and copies ran while one was open for 11% of the time, Pallas kernels for 2%

profile of v10, /device:TPU:1, one launch (start us, length us, event | category | flops | bytes accessed | tf_op | source)
XLA Modules:
  0.0 129.4 jit_solution(17730220311535001942)
XLA Ops:
  0.6 5.3 %collective-permute-start = (bf16[512,512]{1,0:T(8,128)(2,1)}, bf16[512,512]{1,0:T(8,128)(2,1)S(1)}, u32[]{:S(2)}, u32[]{:S(2)}) collective-permute-start(bf16[512,512]{1,0:T(8,128)(2,1)} %bitcast.36), channel_id=1, source_target_pairs={{0,1},{1,2},{2,3},{3,4},{4,5},{5,6},{6,7},{7,0},{8,15},{9,8},{10,9... | collective-permute-start | bytes 1572872 | tf_op jit(solution)/shard_map/ppermute | solution.py:122
  6.0 1.9 %collective-permute-start.1 = (bf16[512,512]{1,0:T(8,128)(2,1)}, bf16[512,512]{1,0:T(8,128)(2,1)S(1)}, u32[]{:S(2)}, u32[]{:S(2)}) collective-permute-start(bf16[512,512]{1,0:T(8,128)(2,1)} %bitcast.37), channel_id=1, source_target_pairs={{0,7},{1,0},{2,1},{3,2},{4,3},{5,4},{6,5},{7,6},{8,9},{9,10},{10,1... | collective-permute-start | bytes 1572872 | tf_op jit(solution)/shard_map/ppermute | solution.py:122
  7.9 0.9 copy-done.2
  8.9 0.7 copy-done.3
  10.2 1.9 %shard_map.103 = (bf16[512,512]{1,0:T(8,128)(2,1)}, s32[1,512]{1,0:T(1,128)S(1)}, s32[1,512]{1,0:T(1,128)S(1)}) custom-call(s32[1]{0:T(128)} %bitcast.here_ref, s32[1,16]{1,0:T(1,128)S(1)} %copy-done.4, s32[1,512]{1,0:T(1,128)S(1)} %copy-done.3, bf16[256,512]{1,0:T(8,128)(2,1)S(1)} %bitcast.35), custom_call_target="tpu_custom_call" | custom-call | flops 134217728 | bytes 1048576 | tf_op jit(solution)/shard_map/pallas_call | solution.py:135
  12.1 17.3 %all-to-all-start = ((bf16[16,32,512]{2,1,0:T(8,128)(2,1)}), bf16[16,32,512]{2,1,0:T(8,128)(2,1)S(1)}, u32[]{:S(2)}, u32[]{:S(2)}) async-start(bf16[16,32,512]{2,1,0:T(8,128)(2,1)} %bitcast.8), calls=%async_computation | async-start | bytes 1048576 | tf_op jit(solution)/shard_map/all_to_all | solution.py:152
  29.4 1.9 %collective-permute-start.2 = (bf16[512,512]{1,0:T(8,128)(2,1)S(1)}, bf16[512,512]{1,0:T(8,128)(2,1)S(1)}, u32[]{:S(2)}, u32[]{:S(2)}) collective-permute-start(bf16[512,512]{1,0:T(8,128)(2,1)S(1)} %collective-permute-done), channel_id=1, source_target_pairs={{0,1},{1,2},{2,3},{3,4},{4,5},{5,6},{6,7},{7,0},{8,15},{9,8},{10,9... | collective-permute-start | bytes 1572872 | tf_op jit(solution)/shard_map/ppermute | solution.py:122
  31.4 1.5 %fusion.10 = f32[512,512]{1,0:T(8,128)S(1)} fusion(bf16[512,512]{1,0:T(8,128)(2,1)S(1)} %collective-permute-done, bf16[512,4096]{1,0:T(8,128)(2,1)} %param.12, s32[]{:T(128)S(6)} %select_n.67), kind=kOutput, calls=%fused_computation.20 | convolution fusion | flops 268435456 | bytes 2097156 | tf_op jit(solution)/shard_map/dot_general | solution.py:129
  32.9 3.4 %collective-permute-start.3 = (bf16[512,512]{1,0:T(8,128)(2,1)S(1)}, bf16[512,512]{1,0:T(8,128)(2,1)S(1)}, u32[]{:S(2)}, u32[]{:S(2)}) collective-permute-start(bf16[512,512]{1,0:T(8,128)(2,1)S(1)} %collective-permute-done.1), channel_id=1, source_target_pairs={{0,7},{1,0},{2,1},{3,2},{4,3},{5,4},{6,5},{7,6},{8,9},{9,10},{10,1... | collective-permute-start | bytes 1572872 | tf_op jit(solution)/shard_map/ppermute | solution.py:122
  36.3 1.5 %convolution_bitcast_fusion.2 = f32[512,512]{1,0:T(8,128)S(1)} fusion(bf16[512,512]{1,0:T(8,128)(2,1)S(1)} %collective-permute-done.1, bf16[512,4096]{1,0:T(8,128)(2,1)} %param.12, s32[]{:T(128)S(6)} %select_n.69), kind=kOutput, calls=%fused_computation.6 | convolution fusion | flops 268435456 | bytes 2097156 | tf_op jit(solution)/shard_map/dot_general | solution.py:129
  37.8 1.5 %fusion.2 = f32[512,512]{1,0:T(8,128)S(1)} fusion(f32[512,512]{1,0:T(8,128)S(1)} %convolution_bitcast_fusion.2, f32[512,512]{1,0:T(8,128)S(1)} %fusion.10, bf16[512,512]{1,0:T(8,128)(2,1)S(1)} %bitcast.38, bf16[512,4096]{1,0:T(8,128)(2,1)} %param.12, s32[]{:T(128)S(6)} %select_n.64), kind=kOutput, calls=%fused_computation.8 | convolution fusion | flops 268959744 | bytes 4194308 | tf_op jit(solution)/shard_map/dot_general | solution.py:129
  39.3 1.6 %collective-permute-done.2 = bf16[512,512]{1,0:T(8,128)(2,1)S(1)} collective-permute-done((bf16[512,512]{1,0:T(8,128)(2,1)S(1)}, bf16[512,512]{1,0:T(8,128)(2,1)S(1)}, u32[]{:S(2)}, u32[]{:S(2)}) %collective-permute-start.2) | collective-permute-done | bytes 524320 | tf_op jit(solution)/shard_map/ppermute | solution.py:122
  40.9 1.9 %collective-permute-start.4 = (bf16[512,512]{1,0:T(8,128)(2,1)S(1)}, bf16[512,512]{1,0:T(8,128)(2,1)}, u32[]{:S(2)}, u32[]{:S(2)}) collective-permute-start(bf16[512,512]{1,0:T(8,128)(2,1)S(1)} %collective-permute-done.2), channel_id=1, source_target_pairs={{0,1},{1,2},{2,3},{3,4},{4,5},{5,6},{6,7},{7,0},{8,15},{9,8},{10,9... | collective-permute-start | bytes 1572872 | tf_op jit(solution)/shard_map/ppermute | solution.py:122
  42.8 4.2 %collective-permute-done.3 = bf16[512,512]{1,0:T(8,128)(2,1)S(1)} collective-permute-done((bf16[512,512]{1,0:T(8,128)(2,1)S(1)}, bf16[512,512]{1,0:T(8,128)(2,1)S(1)}, u32[]{:S(2)}, u32[]{:S(2)}) %collective-permute-start.3) | collective-permute-done | bytes 524320 | tf_op jit(solution)/shard_map/ppermute | solution.py:122
  47.0 1.9 %collective-permute-start.5 = (bf16[512,512]{1,0:T(8,128)(2,1)S(1)}, bf16[512,512]{1,0:T(8,128)(2,1)}, u32[]{:S(2)}, u32[]{:S(2)}) collective-permute-start(bf16[512,512]{1,0:T(8,128)(2,1)S(1)} %collective-permute-done.3), channel_id=1, source_target_pairs={{0,7},{1,0},{2,1},{3,2},{4,3},{5,4},{6,5},{7,6},{8,9},{9,10},{10,1... | collective-permute-start | bytes 1572872 | tf_op jit(solution)/shard_map/ppermute | solution.py:122
  49.0 1.5 %convolution_add_fusion.1 = f32[512,512]{1,0:T(8,128)S(1)} fusion(f32[512,512]{1,0:T(8,128)S(1)} %fusion.2, bf16[512,512]{1,0:T(8,128)(2,1)S(1)} %collective-permute-done.2, bf16[512,4096]{1,0:T(8,128)(2,1)} %param.12, s32[]{:T(128)S(6)} %select_n.71), kind=kOutput, calls=%fused_computation.5 | convolution fusion | flops 268697600 | bytes 3145732 | tf_op jit(solution)/shard_map/dot_general | solution.py:129
  50.5 1.5 %fusion.1 = f32[512,512]{1,0:T(8,128)S(1)} fusion(f32[512,512]{1,0:T(8,128)S(1)} %convolution_add_fusion.1, bf16[512,512]{1,0:T(8,128)(2,1)S(1)} %collective-permute-done.3, bf16[512,4096]{1,0:T(8,128)(2,1)} %param.12, s32[]{:T(128)S(6)} %select_n.73), kind=kOutput, calls=%fused_computation.4 | convolution fusion | flops 268697600 | bytes 3145732 | tf_op jit(solution)/shard_map/dot_general | solution.py:129
  52.0 4.6 %collective-permute-start.6 = (bf16[512,512]{1,0:T(8,128)(2,1)}, bf16[512,512]{1,0:T(8,128)(2,1)S(1)}, u32[]{:S(2)}, u32[]{:S(2)}) collective-permute-start(bf16[512,512]{1,0:T(8,128)(2,1)} %collective-permute-done.4), channel_id=1, source_target_pairs={{0,1},{1,2},{2,3},{3,4},{4,5},{5,6},{6,7},{7,0},{8,15},{9,8},{10,9... | collective-permute-start | bytes 1572872 | tf_op jit(solution)/shard_map/ppermute | solution.py:122
  56.6 1.1 constant_dynamic-slice_fusion.weight_ref
  57.7 1.7 %convolution_add_fusion = f32[512,512]{1,0:T(8,128)S(1)} fusion(f32[512,512]{1,0:T(8,128)S(1)} %fusion.1, bf16[512,512]{1,0:T(8,128)(2,1)} %collective-permute-done.4, bf16[512,4096]{1,0:T(8,128)(2,1)} %param.12, s32[]{:T(128)S(6)} %select_n.75), kind=kOutput, calls=%fused_computation.2 | convolution fusion | flops 268697600 | bytes 3145732 | tf_op jit(solution)/shard_map/dot_general | solution.py:129
  59.9 2.5 %collective-permute-done.5 = bf16[512,512]{1,0:T(8,128)(2,1)} collective-permute-done((bf16[512,512]{1,0:T(8,128)(2,1)S(1)}, bf16[512,512]{1,0:T(8,128)(2,1)}, u32[]{:S(2)}, u32[]{:S(2)}) %collective-permute-start.5) | collective-permute-done | bytes 524320 | tf_op jit(solution)/shard_map/ppermute | solution.py:122
  62.4 1.7 %fusion.sum_ref = f32[512,512]{1,0:T(8,128)S(1)} fusion(f32[512,512]{1,0:T(8,128)S(1)} %convolution_add_fusion, bf16[512,512]{1,0:T(8,128)(2,1)} %collective-permute-done.5, bf16[512,4096]{1,0:T(8,128)(2,1)} %param.12, s32[]{:T(128)S(6)} %select_n.77), kind=kOutput, calls=%fused_computation.1 | convolution fusion | flops 268697600 | bytes 3145732 | tf_op jit(solution)/shard_map/dot_general | solution.py:129
  64.1 1.7 %shard_map.104 = (bf16[512,512]{1,0:T(8,128)(2,1)}, f32[1,512]{1,0:T(1,128)S(1)}) custom-call(bf16[512,512]{1,0:T(8,128)(2,1)S(1)} %convolution_convert_fusion.att_ref, s32[1,512]{1,0:T(1,128)S(1)} %get-tuple-element.23.ids_ref, bf16[1,512]{1,0:T(2,128)(2,1)S(1)} %copy-done.1, f32[512,512]{1,0:T(8,128)S(1)} %fusion.sum_ref, ...), custom_call_target="tpu_custom_call" | custom-call | flops 536870912 | bytes 2097152 | tf_op jit(solution)/shard_map/pallas_call | solution.py:177
  65.8 16.7 %all-to-all-start.1 = ((bf16[16,32,512]{2,1,0:T(8,128)(2,1)}), bf16[16,32,512]{2,1,0:T(8,128)(2,1)S(1)}, u32[]{:S(2)}, u32[]{:S(2)}) async-start(bf16[16,32,512]{2,1,0:T(8,128)(2,1)} %bitcast.10), calls=%async_computation.1 | async-start | bytes 1048576 | tf_op jit(solution)/shard_map/all_to_all | solution.py:152
  82.6 11.8 %psum.7.dots_ref = f32[1,512]{1,0:T(1,128)S(1)} all-reduce(f32[1,512]{1,0:T(1,128)S(1)} %get-tuple-element.32), channel_id=1, replica_groups=mesh['dp'=8,'seq'=16,'tensor'=8] {'tensor'}, use_global_device_ids=true, to_apply=%region_0.1 | all-reduce | flops 512 | bytes 4096 | tf_op jit(solution)/shard_map/psum | solution.py:188
  94.4 0.9 shard_map.105
  95.4 4.5 %all-to-all-done.1 = bf16[16,32,512]{2,1,0:T(8,128)(2,1)S(1)} async-done(((bf16[16,32,512]{2,1,0:T(8,128)(2,1)}), bf16[16,32,512]{2,1,0:T(8,128)(2,1)S(1)}, u32[]{:S(2)}, u32[]{:S(2)}) %all-to-all-start.1) | async-done | bytes 524320 | tf_op jit(solution)/shard_map/all_to_all | solution.py:152
  99.9 13.4 %all-to-all-start.2 = ((f32[128,1,512]{2,1,0:T(1,128)}), f32[128,1,512]{2,1,0:T(1,128)S(1)}, u32[]{:S(2)}, u32[]{:S(2)}) async-start(f32[128,1,512]{2,1,0:T(1,128)} %get-tuple-element.36), calls=%async_computation.2 | async-start | bytes 524288 | tf_op jit(solution)/shard_map/all_to_all | solution.py:205
  113.4 1.0 add_convert_fusion
  114.4 1.0 fusion.3
  115.4 13.2 %all-to-all-done.2 = f32[128,1,512]{2,1,0:T(1,128)S(1)} async-done(((f32[128,1,512]{2,1,0:T(1,128)}), f32[128,1,512]{2,1,0:T(1,128)S(1)}, u32[]{:S(2)}, u32[]{:S(2)}) %all-to-all-start.2) | async-done | bytes 262176 | tf_op jit(solution)/shard_map/all_to_all | solution.py:205
  128.6 0.8 reduce_sum.9
  (19 shorter events, 1.3 us)
Async XLA Ops:
  0.6 28.8 %collective-permute-start = (bf16[512,512]{1,0:T(8,128)(2,1)}, bf16[512,512]{1,0:T(8,128)(2,1)S(1)}, u32[]{:S(2)}, u32[]{:S(2)}) collective-permute-start(bf16[512,512]{1,0:T(8,128)(2,1)} %bitcast.36), channel_id=1, source_target_pairs={{0,1},{1,2},{2,3},{3,4},{4,5},{5,6},{6,7},{7,0},{8,15},{9,8},{10,9... | collective-permute-start | bytes 1572872 | tf_op jit(solution)/shard_map/ppermute | solution.py:122
  6.0 26.9 %collective-permute-start.1 = (bf16[512,512]{1,0:T(8,128)(2,1)}, bf16[512,512]{1,0:T(8,128)(2,1)S(1)}, u32[]{:S(2)}, u32[]{:S(2)}) collective-permute-start(bf16[512,512]{1,0:T(8,128)(2,1)} %bitcast.37), channel_id=1, source_target_pairs={{0,7},{1,0},{2,1},{3,2},{4,3},{5,4},{6,5},{7,6},{8,9},{9,10},{10,1... | collective-permute-start | bytes 1572872 | tf_op jit(solution)/shard_map/ppermute | solution.py:122
  7.9 1.0 copy-start.2
  8.9 0.7 copy-start.3
  9.5 0.7 copy-start.4
  10.2 27.6 %copy-start.5 = (bf16[1,512,512]{2,1,0:T(8,128)(2,1)S(1)}, bf16[1,512,512]{2,1,0:T(8,128)(2,1)}, u32[]{:S(2)}) copy-start(bf16[1,512,512]{2,1,0:T(8,128)(2,1)} %param.10) | copy-start | bytes 1572868
  12.1 39.9 %all-to-all-start = ((bf16[16,32,512]{2,1,0:T(8,128)(2,1)}), bf16[16,32,512]{2,1,0:T(8,128)(2,1)S(1)}, u32[]{:S(2)}, u32[]{:S(2)}) async-start(bf16[16,32,512]{2,1,0:T(8,128)(2,1)} %bitcast.8), calls=%async_computation | async-start | bytes 1048576 | tf_op jit(solution)/shard_map/all_to_all | solution.py:152
  29.4 11.5 %collective-permute-start.2 = (bf16[512,512]{1,0:T(8,128)(2,1)S(1)}, bf16[512,512]{1,0:T(8,128)(2,1)S(1)}, u32[]{:S(2)}, u32[]{:S(2)}) collective-permute-start(bf16[512,512]{1,0:T(8,128)(2,1)S(1)} %collective-permute-done), channel_id=1, source_target_pairs={{0,1},{1,2},{2,3},{3,4},{4,5},{5,6},{6,7},{7,0},{8,15},{9,8},{10,9... | collective-permute-start | bytes 1572872 | tf_op jit(solution)/shard_map/ppermute | solution.py:122
  32.9 14.2 %collective-permute-start.3 = (bf16[512,512]{1,0:T(8,128)(2,1)S(1)}, bf16[512,512]{1,0:T(8,128)(2,1)S(1)}, u32[]{:S(2)}, u32[]{:S(2)}) collective-permute-start(bf16[512,512]{1,0:T(8,128)(2,1)S(1)} %collective-permute-done.1), channel_id=1, source_target_pairs={{0,7},{1,0},{2,1},{3,2},{4,3},{5,4},{6,5},{7,6},{8,9},{9,10},{10,1... | collective-permute-start | bytes 1572872 | tf_op jit(solution)/shard_map/ppermute | solution.py:122
  40.9 11.1 %collective-permute-start.4 = (bf16[512,512]{1,0:T(8,128)(2,1)S(1)}, bf16[512,512]{1,0:T(8,128)(2,1)}, u32[]{:S(2)}, u32[]{:S(2)}) collective-permute-start(bf16[512,512]{1,0:T(8,128)(2,1)S(1)} %collective-permute-done.2), channel_id=1, source_target_pairs={{0,1},{1,2},{2,3},{3,4},{4,5},{5,6},{6,7},{7,0},{8,15},{9,8},{10,9... | collective-permute-start | bytes 1572872 | tf_op jit(solution)/shard_map/ppermute | solution.py:122
  47.0 15.3 %collective-permute-start.5 = (bf16[512,512]{1,0:T(8,128)(2,1)S(1)}, bf16[512,512]{1,0:T(8,128)(2,1)}, u32[]{:S(2)}, u32[]{:S(2)}) collective-permute-start(bf16[512,512]{1,0:T(8,128)(2,1)S(1)} %collective-permute-done.3), channel_id=1, source_target_pairs={{0,7},{1,0},{2,1},{3,2},{4,3},{5,4},{6,5},{7,6},{8,9},{9,10},{10,1... | collective-permute-start | bytes 1572872 | tf_op jit(solution)/shard_map/ppermute | solution.py:122
  52.0 12.1 %copy-start.1 = (bf16[1,512]{1,0:T(2,128)(2,1)S(1)}, bf16[1,512]{1,0:T(2,128)(2,1)}, u32[]{:S(2)}) copy-start(bf16[1,512]{1,0:T(2,128)(2,1)} %logits_ref.3) | copy-start | bytes 3076
  52.0 12.1 %collective-permute-start.6 = (bf16[512,512]{1,0:T(8,128)(2,1)}, bf16[512,512]{1,0:T(8,128)(2,1)S(1)}, u32[]{:S(2)}, u32[]{:S(2)}) collective-permute-start(bf16[512,512]{1,0:T(8,128)(2,1)} %collective-permute-done.4), channel_id=1, source_target_pairs={{0,1},{1,2},{2,3},{3,4},{4,5},{5,6},{6,7},{7,0},{8,15},{9,8},{10,9... | collective-permute-start | bytes 1572872 | tf_op jit(solution)/shard_map/ppermute | solution.py:122
  59.4 35.0 %copy-start = (bf16[1,512,512]{2,1,0:T(8,128)(2,1)S(1)}, bf16[1,512,512]{2,1,0:T(8,128)(2,1)}, u32[]{:S(2)}) copy-start(bf16[1,512,512]{2,1,0:T(8,128)(2,1)} %param.8) | copy-start | bytes 1572868
  59.9 53.5 %copy-start.6 = (f32[512]{0:T(512)S(1)}, f32[512]{0:T(512)}, u32[]{:S(2)}) copy-start(f32[512]{0:T(512)} %param.13) | copy-start | bytes 6148
  65.8 34.1 %all-to-all-start.1 = ((bf16[16,32,512]{2,1,0:T(8,128)(2,1)}), bf16[16,32,512]{2,1,0:T(8,128)(2,1)S(1)}, u32[]{:S(2)}, u32[]{:S(2)}) async-start(bf16[16,32,512]{2,1,0:T(8,128)(2,1)} %bitcast.10), calls=%async_computation.1 | async-start | bytes 1048576 | tf_op jit(solution)/shard_map/all_to_all | solution.py:152
  99.9 28.7 %all-to-all-start.2 = ((f32[128,1,512]{2,1,0:T(1,128)}), f32[128,1,512]{2,1,0:T(1,128)S(1)}, u32[]{:S(2)}, u32[]{:S(2)}) async-start(f32[128,1,512]{2,1,0:T(1,128)} %get-tuple-element.36), calls=%async_computation.2 | async-start | bytes 524288 | tf_op jit(solution)/shard_map/all_to_all | solution.py:205
